TPU v7x, 32 devices: a whole 2x2x4 slice. The times are simulated.
32 devices in a mesh: owner: 4 (over y, x), worker: 8 (over z, core).
Axes of the slice: x: 2, y: 2, z: 4, core: 2. Of those that a mesh axis runs over, the one named last changes fastest.
Arguments:
- states: float32 [65536, 512], P(('owner', 'worker')), may hold values from -3 to 3
- row_of_user: int32 [65536], replicated, may hold values from 0 to 65535, as said below
- event_users: int32 [16384], P(('owner', 'worker')), may hold values from 0 to 65535, as said below
- event_features: int32 [16384], P(('owner', 'worker')), may hold values from 0 to 4095
- feature_table: bfloat16 [4096, 512], replicated, may hold values from -6 to 6
- gate_in: bfloat16 [512, 1536], replicated, may hold values from -0.25 to 0.25
- gate_state: bfloat16 [512, 1536], replicated, may hold values from -0.25 to 0.25
- tower_in: bfloat16 [4096, 1024], P(('owner', 'worker')), may hold values from -0.1875 to 0.1875
- tower_out: bfloat16 [512, 4096], P(('owner', 'worker')), may hold values from -0.09375 to 0.09375
Outputs:
- new_states: float32 [65536, 512], P(('owner', 'worker'))
- scores: float32 [16384], P(('owner', 'worker'))
Inputs may be any that keep to these rules, and one draw needn't show every extreme that they name: `row_of_user`: A permutation: each user has its own state row. `event_users`: among the 512 events of one device, at most 32 have their row (row_of_user of the user) in one device's block of 2048 rows, and for every device some block receives exactly 32 of its events.
All inputs are finite; a program needn't handle non-finite values.
Results may differ from a plain program's by a relative error of at most 0.0034.
Values may be sent and summed in bfloat16 or wider, within the bound.
No kernel may reach another device: no remote copies, remote signals or barrier semaphores. Data moves between devices by JAX's collectives and lax.ppermute only.
A program may use at most 128 MiB of HBM per device.

v0:
```python
import jax
import jax.numpy as jnp
from jax import lax
from jax.sharding import PartitionSpec as P


def gru_cell(inputs, prior, gate_in, gate_state):
    gx = jnp.dot(inputs, gate_in, preferred_element_type=jnp.float32)
    gh = jnp.dot(prior, gate_state, preferred_element_type=jnp.float32)
    width = prior.shape[-1]
    reset = jax.nn.sigmoid(gx[:, :width] + gh[:, :width])
    update = jax.nn.sigmoid(gx[:, width : 2 * width] + gh[:, width : 2 * width])
    cand = jnp.tanh(gx[:, 2 * width :] + reset * gh[:, 2 * width :])
    return (1.0 - update) * cand + update * prior.astype(jnp.float32)


def per_device(
    states,
    row_of_user,
    event_users,
    event_features,
    feature_table,
    gate_in,
    gate_state,
    tower_in,
    tower_out,
):
    shards = lax.axis_size(("owner", "worker"))
    events = event_users.shape[0]
    row_count = states.shape[0]
    width = states.shape[1]
    cap = 2 * (events // shards)
    rows = row_of_user[event_users]
    target = rows // row_count
    local = rows - target * row_count
    inputs = feature_table[event_features]
    hits = (target[:, None] == jnp.arange(shards, dtype=jnp.int32)[None, :]).astype(jnp.int32)
    rank = jnp.sum((jnp.cumsum(hits, axis=0) - hits) * hits, axis=1)
    slot = target * cap + rank
    requests = jnp.full((shards * cap,), -1, jnp.int32).at[slot].set(local).reshape(shards, cap)
    asked = lax.all_to_all(requests, ("owner", "worker"), split_axis=0, concat_axis=0, tiled=True)
    fetched = states[jnp.maximum(asked, 0)].astype(jnp.bfloat16)
    arrived, asked = (
        lax.all_to_all(fetched, ("owner", "worker"), split_axis=0, concat_axis=0, tiled=True),
        asked,
    )
    prior = arrived.reshape(shards * cap, width)[slot]
    fresh = gru_cell(inputs, prior, gate_in, gate_state)
    fresh_low = fresh.astype(jnp.bfloat16)
    delta = fresh - prior.astype(jnp.float32)
    outgoing = (
        jnp.zeros((shards * cap, width), jnp.float32)
        .at[slot]
        .set(delta)
        .reshape(shards, cap, width)
    )
    changes = lax.all_to_all(outgoing, ("owner", "worker"), split_axis=0, concat_axis=0, tiled=True)
    valid = asked.reshape(-1) >= 0
    owners_ids = jnp.where(valid, asked.reshape(-1), row_count)
    total = jax.ops.segment_sum(changes.reshape(-1, width), owners_ids, num_segments=row_count + 1)[
        :row_count
    ]
    count = jax.ops.segment_sum(valid.astype(jnp.int32), owners_ids, num_segments=row_count + 1)[
        :row_count
    ]
    new_states = states + total / jnp.maximum(count, 1).astype(jnp.float32)[:, None]
    joined = jnp.concatenate([fresh_low, inputs], axis=1)
    hidden = jax.nn.gelu(
        lax.dot_general(
            joined,
            lax.all_gather(tower_in, ("owner", "worker"), axis=0, tiled=True),
            (((1,), (1,)), ((), ())),
            preferred_element_type=jnp.float32,
        )
    ).astype(jnp.bfloat16)
    tower = lax.dot_general(
        hidden,
        lax.all_gather(tower_out, ("owner", "worker"), axis=0, tiled=True),
        (((1,), (1,)), ((), ())),
        preferred_element_type=jnp.float32,
    )
    scores = jnp.sum(tower * inputs.astype(jnp.float32), axis=1) / jnp.sqrt(jnp.float32(width))
    return (new_states, scores)


def solution(mesh):
    placed = (
        P(("owner", "worker"), None),
        P(),
        P(("owner", "worker")),
        P(("owner", "worker")),
        P(),
        P(),
        P(),
        P(("owner", "worker"), None),
        P(("owner", "worker"), None),
    )
    return jax.shard_map(
        per_device,
        mesh=mesh,
        in_specs=placed,
        out_specs=(P(("owner", "worker"), None), P(("owner", "worker"))),
        check_vma=False,
    )
```

profile of v0, /device:TPU:0, one launch (start us, length us, event | category | flops | bytes accessed | tf_op | source)
XLA Modules:
  0.0 208.8 jit_solution(3960965799113573063)
XLA Ops:
  7.2 0.7 all-gather.5.cloned.1.call-update
  8.0 0.7 all-gather.3.cloned.1.call-update
  8.7 0.7 compare_select_fusion.3
  9.4 3.6 %gather_fusion = s32[512]{0:T(512)S(1)} fusion(s32[65536]{0:T(1024)} %param.10, s32[1024]{0:T(1024)S(1)} %pad_clamp_fusion.2), kind=kCustom, calls=%fused_computation | custom fusion | bytes 6144 | tf_op jit(solution)/shard_map/gather | solution.py:33
  13.0 1.2 reduce-window.6
  14.2 0.2 slice_reduce_fusion
  14.5 0.1 fusion.45
  14.6 2.4 %scatter_custom_fusion = s32[1024]{0:T(1024)S(1)} fusion(s32[512]{0:T(512)S(1)} %bitcast.53, s32[512]{0:T(512)S(1)} %get-tuple-element.7, s32[]{:T(128)} %constant.17.clone.1), kind=kCustom, calls=%fused_computation.90 | custom fusion | bytes 4100 | tf_op jit(solution)/shard_map/scatter | solution.py:40
  17.1 0.1 all_to_all.12
  17.1 14.3 %all_to_all.19 = s32[32,1,32]{2,1,0:T(1,128)S(1)} all-to-all(s32[32,1,32]{2,1,0:T(1,128)S(1)} %all_to_all.12), channel_id=1, replica_groups=mesh['owner'=4,'worker'=8] {'owner','worker'}, dimensions={0} | all-to-all | bytes 8192 | tf_op jit(solution)/shard_map/all_to_all | solution.py:41
  31.4 0.5 broadcast.213
  32.0 0.8 fusion.47
  32.7 0.1 reshape.170
  32.8 7.3 %gather_fusion.2 = bf16[1024,512]{1,0:T(8,128)(2,1)} fusion(f32[2048,512]{1,0:T(8,128)} %param.9, s32[1024]{0:T(1024)S(1)} %broadcast_clamp_fusion), kind=kCustom, calls=%fused_computation.2 | custom fusion | bytes 2101248 | tf_op jit(solution)/shard_map/gather | solution.py:42
  40.1 2.6 %all-to-all-start.1 = ((bf16[32,32,512]{2,1,0:T(8,128)(2,1)}), bf16[32,32,512]{2,1,0:T(8,128)(2,1)S(1)}, u32[]{:S(2)}, u32[]{:S(2)}) async-start(bf16[32,32,512]{2,1,0:T(8,128)(2,1)} %bitcast.51), calls=%async_computation.1 | async-start | bytes 2097152 | tf_op jit(solution)/shard_map/all_to_all | solution.py:44
  42.8 4.7 %gather_fusion.1 = bf16[512,512]{1,0:T(8,128)(2,1)S(1)} fusion(bf16[4096,512]{1,0:T(8,128)(2,1)} %param.13, s32[1024]{0:T(1024)S(1)} %pad_clamp_fusion.1), kind=kCustom, calls=%fused_computation.1 | custom fusion | bytes 1050624 | tf_op jit(solution)/shard_map/gather | solution.py:36
  47.6 2.6 %fusion.66 = f32[512,1536]{1,0:T(8,128)} fusion(bf16[512,512]{1,0:T(8,128)(2,1)S(1)} %gather_fusion.1, bf16[512,1536]{1,0:T(8,128)(2,1)S(1)} %copy-done), kind=kOutput, calls=%fused_computation.101 | convolution fusion | flops 805306368 | bytes 5242880 | tf_op jit(solution)/shard_map/dot_general | solution.py:8
  50.2 34.4 %all-to-all-done.1 = bf16[32,32,512]{2,1,0:T(8,128)(2,1)S(1)} async-done(((bf16[32,32,512]{2,1,0:T(8,128)(2,1)}), bf16[32,32,512]{2,1,0:T(8,128)(2,1)S(1)}, u32[]{:S(2)}, u32[]{:S(2)}) %all-to-all-start.1) | async-done | bytes 1048608 | tf_op jit(solution)/shard_map/all_to_all | solution.py:44
  84.6 2.0 gather_fusion.3
  86.6 2.5 %fusion.67 = f32[512,1536]{1,0:T(8,128)S(1)} fusion(bf16[512,512]{1,0:T(8,128)(2,1)S(1)} %gather_fusion.3, bf16[512,1536]{1,0:T(8,128)(2,1)} %param.15), kind=kOutput, calls=%fused_computation.102 | convolution fusion | flops 805306368 | bytes 5242880 | tf_op jit(solution)/shard_map/dot_general | solution.py:9
  89.2 1.9 fusion.64
  91.1 4.4 %scatter_custom_fusion.1 = f32[1024,512]{1,0:T(8,128)} fusion(s32[512]{0:T(512)S(1)} %bitcast.55, f32[512,512]{1,0:T(8,128)} %get-tuple-element.6, bf16[512,512]{1,0:T(8,128)(2,1)S(1)} %gather_fusion.3, f32[]{:T(128)} %constant.16.clone.1), kind=kCustom, calls=%fused_computation.27 | custom fusion | flops 524288 | bytes 3670020 | tf_op jit(solution)/shard_map/scatter | solution.py:54
  95.5 3.5 %all-to-all-start.2 = ((f32[32,32,512]{2,1,0:T(8,128)}), f32[32,32,512]{2,1,0:T(8,128)}, u32[]{:S(2)}, u32[]{:S(2)}) async-start(f32[32,32,512]{2,1,0:T(8,128)} %bitcast.50), calls=%async_computation.2 | async-start | bytes 4194304 | tf_op jit(solution)/shard_map/all_to_all | solution.py:57
  99.0 0.2 copy.13
  99.2 0.1 reshape.147
  99.3 0.1 reshape.212
  99.4 6.5 %scatter_custom_fusion.3 = s32[2049]{0:T(1024)S(1)} fusion(s32[1024]{0:T(1024)S(1)} %bitcast.57, s32[1024]{0:T(1024)S(1)} %reshape.212, s32[]{:T(128)} %constant.18.clone.1), kind=kCustom, calls=%fused_computation.64 | custom fusion | flops 1024 | bytes 8200 | tf_op jit(solution)/shard_map/scatter-add | solution.py:63
  105.9 68.3 %all-to-all-done.2 = f32[32,32,512]{2,1,0:T(8,128)} async-done(((f32[32,32,512]{2,1,0:T(8,128)}), f32[32,32,512]{2,1,0:T(8,128)}, u32[]{:S(2)}, u32[]{:S(2)}) %all-to-all-start.2) | async-done | bytes 2097184 | tf_op jit(solution)/shard_map/all_to_all | solution.py:57
  174.2 9.6 %scatter_custom_fusion.2 = f32[2049,512]{1,0:T(8,128)} fusion(s32[1024]{0:T(1024)S(1)} %bitcast.58, f32[1024,512]{1,0:T(8,128)} %bitcast.9, f32[]{:T(128)} %constant.16.clone.1), kind=kCustom, calls=%fused_computation.20 | custom fusion | flops 524288 | bytes 4196864 | tf_op jit(solution)/shard_map/scatter-add | solution.py:60
  183.7 6.2 %fusion.8 = f32[2048,512]{1,0:T(8,128)} fusion(f32[2048,512]{1,0:T(8,128)} %param.9, f32[2049,512]{1,0:T(8,128)} %scatter_custom_fusion.2, f32[2048]{0:T(1024)S(1)} %fusion.48), kind=kLoop, calls=%fused_computation.18 | loop fusion | flops 2097152 | bytes 12591104 | tf_op jit(solution)/shard_map/add | solution.py:66
  190.0 11.4 %fusion.16 = f32[512]{0:T(512)S(1)} fusion(bf16[512,4096]{1,0:T(8,128)(2,1)} %all-gather.5.cloned.1.call-done, bf16[4096,1024]{1,0:T(8,128)(2,1)} %all-gather.3.cloned.1.call-done, bf16[512,512]{1,0:T(8,128)(2,1)S(1)} %copy-done.3, bf16[512,512]{1,0:T(8,128)(2,1)S(1)} %get-tuple-element.5, bf16[512,512]{0,1:T(8,128)(2,1)S(1)} %copy.13), kind=kOutput, calls=%fused_computation.25 | convolution fusion | flops 6464208384 | bytes 14157824 | tf_op jit(solution)/shard_map/dot_general | solution.py:76
  201.4 0.6 broadcast_multiply_fusion
  (27 shorter events, 0.2 us)
Async XLA Ops:
  7.2 40.4 %copy-start = (bf16[512,1536]{1,0:T(8,128)(2,1)S(1)}, bf16[512,1536]{1,0:T(8,128)(2,1)}, u32[]{:S(2)}) copy-start(bf16[512,1536]{1,0:T(8,128)(2,1)} %param.14) | copy-start | bytes 4718596
  7.2 182.8 %all-gather.5.cloned.1.call-start = ((), (), s32[]{:S(2)}) async-start(), calls=%async_computation.4 | async-start | bytes 4325376 | tf_op jit(solution)/shard_map/all_gather | solution.py:78
  7.9 182.1 %all-gather.3.cloned.1.call-start = ((), (), s32[]{:S(2)}) async-start(), calls=%async_computation.3 | async-start | bytes 8650752 | tf_op jit(solution)/shard_map/all_gather | solution.py:71
  32.8 10.0 %copy-start.4 = (s32[512]{0:T(512)S(1)}, s32[512]{0:T(512)}, u32[]{:S(2)}) copy-start(s32[512]{0:T(512)} %param.12) | copy-start | bytes 6148
  40.1 44.5 %all-to-all-start.1 = ((bf16[32,32,512]{2,1,0:T(8,128)(2,1)}), bf16[32,32,512]{2,1,0:T(8,128)(2,1)S(1)}, u32[]{:S(2)}, u32[]{:S(2)}) async-start(bf16[32,32,512]{2,1,0:T(8,128)(2,1)} %bitcast.51), calls=%async_computation.1 | async-start | bytes 2097152 | tf_op jit(solution)/shard_map/all_to_all | solution.py:44
  47.6 37.1 %copy-start.2 = (bf16[512,512]{1,0:T(8,128)(2,1)}, bf16[512,512]{1,0:T(8,128)(2,1)S(1)}, u32[]{:S(2)}) copy-start(bf16[512,512]{1,0:T(8,128)(2,1)S(1)} %gather_fusion.1) | copy-start | bytes 1572868
  86.6 2.6 %copy-start.1 = (f32[512,1536]{1,0:T(8,128)S(1)}, f32[512,1536]{1,0:T(8,128)}, u32[]{:S(2)}) copy-start(f32[512,1536]{1,0:T(8,128)} %fusion.66) | copy-start | bytes 9437188
  91.1 7.9 %copy-start.3 = (bf16[512,512]{1,0:T(8,128)(2,1)S(1)}, bf16[512,512]{1,0:T(8,128)(2,1)}, u32[]{:S(2)}) copy-start(bf16[512,512]{1,0:T(8,128)(2,1)} %copy-done.2) | copy-start | bytes 1572868
  95.5 78.7 %all-to-all-start.2 = ((f32[32,32,512]{2,1,0:T(8,128)}), f32[32,32,512]{2,1,0:T(8,128)}, u32[]{:S(2)}, u32[]{:S(2)}) async-start(f32[32,32,512]{2,1,0:T(8,128)} %bitcast.50), calls=%async_computation.2 | async-start | bytes 4194304 | tf_op jit(solution)/shard_map/all_to_all | solution.py:57
Sparse Core Ops, SparseCore 0:
  11.0 74.3 all-gather.4
  88.4 98.5 all-gather.2
where the time goes:
time: 210 us; the launch traced here: 209 us
  waiting for transfers between devices  104 us (50%)
  other arithmetic  32.1 us (15%)
  local copies, waits for them, and re-layouts  21.4 us (10%)
  matrix products  16.6 us (8%)
  blocking collectives  14.3 us (7%)
  between operations  14.2 us (7%)
  starting transfers between devices  6.2 us (3%)
    all_to_all x1, waiting for transfers between devices, per_device(): lax.all_to_all(outgoing, ('owner', 'worker'), split_axis=0, concat_axis=0...  68.3 us
    all_to_all x1, waiting for transfers between devices, per_device(): lax.all_to_all(fetched, ('owner', 'worker'), split_axis=0, concat_axis=0,...  34.4 us
    all_to_all x1, blocking collectives, per_device(): lax.all_to_all(requests, ('owner', 'worker'), split_axis=0, concat_axis=0...  14.3 us
    dot_general x1, matrix products, per_device(): lax.dot_general(hidden, lax.all_gather(tower_out, ('owner', 'worker'), ax...  11.4 us
    scatter-add x1, other arithmetic, per_device(): jax.ops.segment_sum(changes.reshape(-1, width), owners_ids, num_segments=...  9.57 us
    gather x1, local copies, waits for them, and re-layouts, per_device(): fetched = states[jnp.maximum(asked, 0)].astype(jnp.bfloat16)  7.3 us
    scatter-add x1, other arithmetic, per_device(): jax.ops.segment_sum(valid.astype(jnp.int32), owners_ids, num_segments=row...  6.47 us
    add x1, other arithmetic, per_device(): states + total / jnp.maximum(count, 1).astype(jnp.float32)[:, None]  6.25 us
  transfers between devices with their start and end apart: 4, of which 2 were waited for; matrix products, arithmetic and copies ran while one was open for 28% of the time, Pallas kernels for 0%

commit v1 on v0

v1 whole, which is shorter than its diff:
```python
import functools

import jax
import jax.numpy as jnp
from jax import lax
from jax.experimental import pallas as pl
from jax.experimental.pallas import tpu as pltpu
from jax.sharding import PartitionSpec as P

AXES = ("owner", "worker")
LANES = 128
CHUNK = 256
F32 = jnp.float32
BF16 = jnp.bfloat16
I32 = jnp.int32
VMEM = pl.BlockSpec(memory_space=pltpu.VMEM)
ANY = pl.BlockSpec(memory_space=pl.ANY)
HBM = pl.BlockSpec(memory_space=pltpu.HBM)


def iota(shape, axis):
    return lax.broadcasted_iota(I32, shape, axis)


def onehot(mask):
    return jnp.where(mask, 1.0, 0.0).astype(BF16)


def dot(a, b, ca=1, cb=0):
    return lax.dot_general(a, b, (((ca,), (cb,)), ((), ())), preferred_element_type=F32)


def split3(x):
    a = x.astype(BF16)
    r = x - a.astype(F32)
    b = r.astype(BF16)
    return a, b, (r - b.astype(F32)).astype(BF16)


def route_kernel(table_hbm, users_ref, feats_ref, *refs, shards, cap, row_count, chips):
    table_ref, sem = refs[-2:]
    copy = pltpu.make_async_copy(table_hbm, table_ref, sem)
    copy.start()
    if chips:
        wout_ref, req_ref, slot_ref, mine_ref, theirs_ref = refs[:5]
        owners, depth = chips
        units = wout_ref.shape[1] // (2 * owners * depth)
        rows = wout_ref.shape[0]
        even = lax.axis_index("worker") % 2 == 0
        for place in range(depth):
            for owner in range(owners):
                at = 2 * units * (owner * depth + place)
                a, b = wout_ref[:, at : at + units], wout_ref[:, at + units : at + 2 * units]
                to = units * ((place % (depth // 2)) * owners + owner)
                line = slice((place // (depth // 2)) * rows, (place // (depth // 2) + 1) * rows)
                mine_ref[line, to : to + units] = jnp.where(even, a, b)
                theirs_ref[line, to : to + units] = jnp.where(even, b, a)
    else:
        req_ref, slot_ref = refs[:2]
    users = users_ref[...]
    events = users.shape[1]
    high, low = users >> 7, users & 127
    pick = onehot(iota((table_ref.shape[0], events), 0) == high)
    copy.wait()
    table = table_ref[...]
    parts = [((table >> (8 * k)) & 255).astype(F32).astype(BF16) for k in range(3)]
    got = dot(jnp.concatenate(parts, axis=1), pick, 0, 0)
    here = iota((LANES, events), 0) == low
    row = jnp.zeros((1, events), F32)
    for k in range(3):
        part = jnp.where(here, got[k * LANES : (k + 1) * LANES], 0.0)
        row = row + float(256**k) * jnp.sum(part, axis=0, keepdims=True)
    row = row.astype(I32)
    device = iota((shards, events), 0)
    first = device * row_count
    mine = (row >= first) & (row < first + row_count)
    hit = jnp.where(mine, 1.0, 0.0)
    target = jnp.sum(jnp.where(mine, device, 0), axis=0, keepdims=True)
    local = row - target * row_count + 1
    before = onehot(iota((events, events), 0) < iota((events, events), 1))
    rank = dot(hit.astype(BF16), before)
    rank = jnp.sum(hit * rank, axis=0, keepdims=True).astype(I32)
    place = onehot(iota((cap, events), 0) == rank)
    feats = feats_ref[...]
    bytes_of = [(v & 255).astype(F32) for v in (local >> 8, local, feats >> 8, feats)]
    filled = dot(jnp.concatenate([hit * v for v in bytes_of], axis=0).astype(BF16), place, 1, 1)
    q = [filled[k * shards : (k + 1) * shards].astype(I32) for k in range(4)]
    req_ref[:, :cap] = q[0] * 256 + q[1]
    req_ref[:, cap:] = q[2] * 256 + q[3]
    slot_ref[:1, :] = target
    slot_ref[1:, :] = rank


def route(row_of_user, event_users, event_features, tower_out, shards, cap, row_count, chips):
    events = event_users.shape[0]
    table = row_of_user.reshape(-1, LANES)
    rows, hidden = tower_out.shape
    cut = [jax.ShapeDtypeStruct((2 * rows, hidden // 4), BF16)] * 2 if chips else []
    return pl.pallas_call(
        functools.partial(route_kernel, shards=shards, cap=cap, row_count=row_count, chips=chips),
        out_shape=[
            jax.ShapeDtypeStruct((shards, 2 * cap), I32),
            jax.ShapeDtypeStruct((2, events), I32),
            *cut,
        ],
        in_specs=[HBM, VMEM, VMEM] + [VMEM] * bool(chips),
        out_specs=[VMEM] * (2 + len(cut)),
        scratch_shapes=[pltpu.VMEM(table.shape, I32), pltpu.SemaphoreType.DMA],
        compiler_params=pltpu.CompilerParams(vmem_limit_bytes=24 * 2**20),
        cost_estimate=pl.CostEstimate(flops=10**9, bytes_accessed=10**6, transcendentals=0),
        name="route",
    )(table, event_users.reshape(1, events), event_features.reshape(1, events), *([tower_out] if chips else []))


def slot_column(asked, n, cap):
    shards = asked.shape[0]
    source = onehot(iota((n, shards), 0) // cap == iota((n, shards), 1))
    place = (iota((n, cap), 0) & (cap - 1)) == iota((n, cap), 1)
    wide = [dot(source, b.astype(F32).astype(BF16)) for b in (asked >> 8, asked & 255)]
    return jnp.sum(jnp.where(place, wide[0] * 256.0 + wide[1], 0.0), axis=1, keepdims=True).astype(I32)


def slot_row(asked, n, cap):
    shards = asked.shape[0]
    place = onehot((iota((cap, n), 1) & (cap - 1)) == iota((cap, n), 0))
    source = iota((shards, n), 1) // cap == iota((shards, n), 0)
    v = asked[:, :cap]
    wide = [dot(b.astype(F32).astype(BF16), place) for b in (v >> 8, v & 255)]
    return jnp.sum(jnp.where(source, wide[0] * 256.0 + wide[1], 0.0), axis=0, keepdims=True).astype(I32) - 1


def sigmoid(x):
    return 0.5 * jnp.tanh(0.5 * x) + 0.5


def fetch_kernel(asked_ref, table_hbm, *refs, cap, column):
    out_ref, table_ref, *low, sem = refs[-3 - (table_hbm.dtype != BF16) :]
    copy = pltpu.make_async_copy(table_hbm, table_ref, sem)
    copy.start()
    n, rows = out_ref.shape[0], table_hbm.shape[0]
    at_row = slot_column(asked_ref[:, column * cap : (column + 1) * cap], n, cap) - (1 - column)
    copy.wait()
    if low:
        low[0][...] = table_ref[...].astype(BF16)
    known = low[0] if low else table_ref
    for k in range(n // CHUNK):
        at = slice(k * CHUNK, (k + 1) * CHUNK)
        out_ref[at, :] = dot(onehot(iota((CHUNK, rows), 1) == at_row[at]), known[...]).astype(BF16)


def fetch(asked, table, cap, column, after=()):
    n, width = asked.shape[0] * cap, table.shape[1]
    low = [] if table.dtype == BF16 else [pltpu.VMEM(table.shape, BF16)]
    return pl.pallas_call(
        functools.partial(fetch_kernel, cap=cap, column=column),
        out_shape=jax.ShapeDtypeStruct((n, width), BF16),
        in_specs=[VMEM, HBM] + [ANY] * len(after),
        out_specs=VMEM,
        scratch_shapes=[pltpu.VMEM(table.shape, table.dtype), *low, pltpu.SemaphoreType.DMA],
        compiler_params=pltpu.CompilerParams(vmem_limit_bytes=32 * 2**20),
        cost_estimate=pl.CostEstimate(flops=2 * n * width * table.shape[0], bytes_accessed=5 * 10**6, transcendentals=0),
        name="fetch",
    )(asked, table, *after)


def cell_kernel(prior_ref, inputs_ref, gin_hbm, gst_hbm, *refs):
    fresh_ref, gin_ref, gst_ref, sems = refs[-4:]
    copies = [pltpu.make_async_copy(gst_hbm, gst_ref, sems.at[0]), pltpu.make_async_copy(gin_hbm, gin_ref, sems.at[1])]
    for copy in copies:
        copy.start()
    for copy in copies:
        copy.wait()
    n, width = fresh_ref.shape
    for k in range(n // CHUNK):
        at = slice(k * CHUNK, (k + 1) * CHUNK)
        prior = prior_ref[at, :]
        gh = dot(prior, gst_ref[...])
        gx = dot(inputs_ref[at, :], gin_ref[...])
        reset = sigmoid(gx[:, :width] + gh[:, :width])
        update = sigmoid(gx[:, width : 2 * width] + gh[:, width : 2 * width])
        cand = jnp.tanh(gx[:, 2 * width :] + reset * gh[:, 2 * width :])
        fresh = (1.0 - update) * cand + update * prior.astype(F32)
        fresh_ref[at, :] = fresh.astype(BF16)


def cell(prior, inputs, gate_in, gate_state, after=()):
    n, width = prior.shape
    return pl.pallas_call(
        cell_kernel,
        out_shape=jax.ShapeDtypeStruct((n, width), BF16),
        in_specs=[VMEM, VMEM, HBM, HBM] + [ANY] * len(after),
        out_specs=VMEM,
        scratch_shapes=[pltpu.VMEM(gate_in.shape, BF16)] * 2 + [pltpu.SemaphoreType.DMA((2,))],
        compiler_params=pltpu.CompilerParams(vmem_limit_bytes=32 * 2**20),
        cost_estimate=pl.CostEstimate(flops=4 * 10**9, bytes_accessed=6 * 10**6, transcendentals=2 * 10**6),
        name="cell",
    )(prior, inputs, gate_in, gate_state, *after)


def update_kernel(asked_ref, fresh_ref, states_ref, *refs, cap):
    out_ref, old_ref, new_ref, in_sems, out_sems = refs[-5:]
    n, rows = fresh_ref.shape[0], states_ref.shape[0]
    chunks = rows // CHUNK
    parts = [pl.ds(k * CHUNK, CHUNK) for k in range(chunks)]
    reads = [pltpu.make_async_copy(states_ref.at[p], old_ref.at[p], in_sems.at[k]) for k, p in enumerate(parts)]
    writes = [pltpu.make_async_copy(new_ref.at[p], out_ref.at[p], out_sems.at[k]) for k, p in enumerate(parts)]
    for read in reads:
        read.start()
    local = slot_row(asked_ref[...], n, cap)
    fresh = fresh_ref[...]
    ones = jnp.ones((n, LANES), BF16)
    for k in range(chunks):
        at = slice(k * CHUNK, (k + 1) * CHUNK)
        pick = onehot(iota((CHUNK, n), 0) + k * CHUNK == local)
        total = dot(pick, fresh)
        count = dot(pick, ones)[:, :1]
        reads[k].wait()
        old = old_ref[at, :]
        change = total / jnp.maximum(count, 1.0) - old.astype(BF16).astype(F32)
        new_ref[at, :] = old + jnp.where(count > 0.0, change, 0.0)
        writes[k].start()
    for write in writes:
        write.wait()


def update(asked, fresh, states, cap, after=()):
    chunks = states.shape[0] // CHUNK
    return pl.pallas_call(
        functools.partial(update_kernel, cap=cap),
        out_shape=jax.ShapeDtypeStruct(states.shape, F32),
        in_specs=[VMEM, VMEM, HBM] + [ANY] * len(after),
        out_specs=HBM,
        scratch_shapes=[pltpu.VMEM(states.shape, F32)] * 2 + [pltpu.SemaphoreType.DMA((chunks,))] * 2,
        compiler_params=pltpu.CompilerParams(vmem_limit_bytes=32 * 2**20),
        cost_estimate=pl.CostEstimate(flops=4 * 10**9, bytes_accessed=10**7, transcendentals=0),
        name="update",
    )(asked, fresh, states, *after)


def gelu(x):
    inner = 0.7978845608028654 * (x + 0.044715 * (x * x * x))
    return x * (0.5 * (1.0 + jnp.tanh(inner)))


def owner_at(flip):
    return lax.axis_index("owner") ^ flip


def depth_at(back, depth):
    return lax.rem(lax.axis_index("worker") // 2 + depth - back, depth)


def step_kernel(*refs, n_in, n_out, n_after, ins, outs, backs, rows, depth, cap, first, last):
    it = iter(refs)
    take = lambda k: [next(it) for _ in range(k)]
    fresh, inputs = take(2), take(2)
    before = None if first else next(it)
    in_refs, out_refs = take(n_in), take(n_out)
    take(n_after)
    line_ref, win_ref, wout_ref = take(3)
    groups, width, both = win_ref.shape
    half = both // 2
    chunk = fresh[0].shape[0]

    @pl.when(pl.program_id(0) == 0)
    def _():
        for group, index, count, flip, place in ins:
            owner = 0 if flip is None else owner_at(flip)
            at = pl.multiple_of(owner * rows[0] + place, 16)
            win_ref[group, pl.ds(at, count), :] = in_refs[index][...]
        if depth == 1:
            wout_ref[0] = out_refs[0][...]
        else:
            for index, start, flip, back in outs:
                chip = owner_at(flip) * depth + depth_at(back, depth)
                to = pl.ds(pl.multiple_of(chip * rows[1], 16), rows[1])
                for g, group_back in enumerate(backs):
                    place = depth_at(group_back, depth)
                    lanes = pl.ds(pl.multiple_of(lax.rem(place, 2) * width, LANES), width)
                    line = pl.ds(pl.multiple_of(start + rows[1] * (place // 2), 16), rows[1])
                    wout_ref[g, to, :] = out_refs[index][line, lanes]

    near = chunk // cap
    at = pl.ds(pl.multiple_of(pl.program_id(0) * near, near), near)
    for side in range(2):
        x, f = inputs[side][...], fresh[side][...]
        joined = jnp.concatenate([f, x], axis=1)
        tower = jnp.zeros((chunk, half), F32)
        for g in range(groups):
            h = gelu(dot(joined, win_ref[g], 1, 1)).astype(BF16)
            tower = tower + dot(h, wout_ref[g], 1, 1)
        score = jnp.sum(tower * x.astype(F32), axis=1, keepdims=True)
        place = (iota((chunk, cap), 0) & (cap - 1)) == iota((chunk, cap), 1)
        source = onehot(iota((near, chunk), 1) // cap == iota((near, chunk), 0))
        lines = sum(dot(source, p) for p in split3(jnp.where(place, score, 0.0)))
        lanes = slice(side * cap, (side + 1) * cap)
        if not first:
            lines = lines + before[at, lanes]
        if last:
            lines = lines / jnp.sqrt(F32(half))
        line_ref[at, lanes] = lines


def step(fresh, inputs, before, ins, outs, backs, rows, depth, cap, last, after=()):
    n, half = fresh[0].shape
    shards = n // cap
    chunk = min(n, 2 * CHUNK)
    in_parts = [(group, i, count, flip, place) for i, (group, _, count, flip, place) in enumerate(ins)]
    out_parts = [(i, start, flip, back) for i, (_, parts) in enumerate(outs) for start, flip, back in parts]
    width = sum(count for group, _, count, _, _ in ins if group == 0)
    side = pl.BlockSpec((chunk, half), lambda i: (i, 0))
    line = pl.BlockSpec((shards, 2 * cap), lambda i: (0, 0))
    whole = lambda a: pl.BlockSpec(a.shape, lambda i: (0, 0))
    units = len(backs) * width
    in_arrays, out_arrays = [a for _, a, _, _, _ in ins], [a for a, _ in outs]
    return pl.pallas_call(
        functools.partial(
            step_kernel,
            n_in=len(in_arrays),
            n_out=len(out_arrays),
            n_after=len(after),
            ins=in_parts,
            outs=out_parts,
            backs=backs,
            rows=rows,
            depth=depth,
            cap=cap,
            first=before is None,
            last=last,
        ),
        grid=(n // chunk,),
        out_shape=jax.ShapeDtypeStruct((shards, 2 * cap), F32),
        in_specs=[side] * 4
        + ([] if before is None else [line])
        + [whole(a) for a in in_arrays + out_arrays]
        + [ANY] * len(after),
        out_specs=line,
        scratch_shapes=[pltpu.VMEM((len(backs), width, 2 * half), BF16), pltpu.VMEM((len(backs), half, width), BF16)],
        compiler_params=pltpu.CompilerParams(vmem_limit_bytes=44 * 2**20),
        cost_estimate=pl.CostEstimate(flops=12 * n * units * half, bytes_accessed=10**7, transcendentals=2 * n * units),
        name="tower",
    )(*fresh, *inputs, *([] if before is None else [before]), *in_arrays, *out_arrays, *after)


def pick_kernel(back_ref, slot_ref, out_ref, *, cap):
    back = back_ref[...]
    shards = back.shape[0]
    target, rank = slot_ref[:1, :], slot_ref[1:, :]
    events = target.shape[1]
    place = onehot(iota((cap, events), 0) == rank)
    device = iota((shards, events), 0)
    score = jnp.zeros((shards, events), F32)
    for side in range(2):
        parts = split3(back[:, side * cap : (side + 1) * cap])
        here = device == (target if side == 0 else target + 1 - 2 * (target & 1))
        score = score + jnp.where(here, sum(dot(p, place) for p in parts), 0.0)
    out_ref[...] = jnp.sum(score, axis=0, keepdims=True)


def pick(back, slots, cap):
    return pl.pallas_call(
        functools.partial(pick_kernel, cap=cap),
        out_shape=jax.ShapeDtypeStruct((1, slots.shape[1]), F32),
        in_specs=[VMEM] * 2,
        out_specs=VMEM,
        cost_estimate=pl.CostEstimate(flops=10**8, bytes_accessed=10**5, transcendentals=0),
        name="pick",
    )(back, slots)


def exchange(x):
    return lax.all_to_all(x, AXES, split_axis=0, concat_axis=0, tiled=True)


def send(x, devices, to):
    return lax.ppermute(x, AXES, [(d, to(d)) for d in range(devices)])


def by_core(mine, theirs, devices, axis):
    even = lax.axis_index("worker") % 2 == 0
    got = send(theirs, devices, lambda d: d ^ 1)
    return jnp.concatenate([jnp.where(even, mine, got), jnp.where(even, got, mine)], axis=axis)


def tower_gathered(fresh, inputs, tower_in, tower_out, devices, cap):
    same_core = [list(range(0, devices, 2)), list(range(1, devices, 2))]
    rows = tower_out.shape[0]
    cols = tower_out.reshape(rows, devices // 2, 2, -1)
    cols = [cols[:, :, k].reshape(rows, -1) for k in range(2)]
    even = lax.axis_index("worker") % 2 == 0
    half = by_core(jnp.where(even, cols[0], cols[1]), jnp.where(even, cols[1], cols[0]), devices, 0)
    win, wout = [lax.all_gather(w, AXES, axis_index_groups=same_core, tiled=True) for w in (tower_in, half)]
    ins = [(0, win, win.shape[0], None, 0)]
    return step(fresh, inputs, None, ins, [(wout, [])], [0], (0, 0), 1, cap, True)


def per_device(
    states,
    row_of_user,
    event_users,
    event_features,
    feature_table,
    gate_in,
    gate_state,
    tower_in,
    tower_out,
):
    shards = lax.axis_size(AXES)
    events = event_users.shape[0]
    cap = 2 * (events // shards)
    owners, depth = lax.axis_size("owner"), lax.axis_size("worker") // 2
    by_steps = (owners, depth) == (4, 4)
    chips = (owners, depth) if by_steps else None
    requests, slots, *cut = route(
        row_of_user, event_users, event_features, tower_out, shards, cap, states.shape[0], chips
    )
    sent = send_tower(tower_in, *cut, shards) if by_steps else None
    due = sent[2] if by_steps else [()] * 4
    asked = exchange(requests)
    prior = fetch(asked, states, cap, 0, after=due[0])
    inputs = fetch(asked, feature_table, cap, 1, after=(*due[1], prior))
    fresh = cell(prior, inputs, gate_in, gate_state, after=due[2])
    new_states = update(asked, fresh, states, cap, after=due[3])
    both = [[x, send(x, shards, lambda d: d ^ 1)] for x in (fresh, inputs)]
    if by_steps:
        parts = tower_by_steps(*both, sent, tower_in.shape[0], 2 * tower_out.shape[0], cap, new_states)
    else:
        parts = tower_gathered(*both, tower_in, tower_out, shards, cap)
    back = exchange(parts)
    scores = pick(back, slots, cap).reshape(events)
    return (new_states, scores)


def send_tower(tower_in, mine, theirs, devices):
    def ahead(x):
        return send(x, devices, lambda d: (d & ~6) | ((d + 2) & 6))

    def along_x(x):
        return send(x, devices, lambda d: d ^ 8)

    def along_y(x):
        return send(x, devices, lambda d: d ^ 16)

    def plane(x):
        ax, ay = along_x(x), along_y(x)
        half = x.shape[0] // 2
        return x, ax, ay, along_x(ay[:half]), along_y(ax[half:])

    line = [tower_in]
    for _ in range(3):
        line.append(ahead(line[-1]))
    ins = [plane(x) for x in line]
    parts = (2, mine.shape[0] // 2, mine.shape[1])
    rows = [by_core(mine.reshape(parts), theirs.reshape(parts), devices, 1).reshape(-1, mine.shape[1])]
    for _ in range(3):
        rows.append(ahead(rows[-1]))
    outs = plane(jnp.concatenate(rows, axis=0))
    due = [
        (*ins[0][1:3], line[1], rows[1]),
        (*ins[0][3:], *ins[1][1:3], line[2], rows[2]),
        (*ins[1][3:], line[3], rows[3]),
        outs[1:3],
    ]
    return ins, outs, due


def tower_by_steps(fresh, inputs, sent, rows_in, rows_out, cap, done):
    depth = 4
    planes, outs, _ = sent
    half = rows_in // 2

    def ins_of(back, group):
        line, ax, ay, top, bottom = planes[back]
        whole = [(group, a, rows_in, flip, 0) for flip, a in enumerate((line, ax, ay))]
        return whole + [(group, top, half, 3, 0), (group, bottom, half, 3, half)]

    block = 2 * rows_out
    out_parts = [(a, [(back * block, flip, back) for back in range(depth)]) for flip, a in enumerate(outs[:3])]
    out_parts += [(a, [(k * block, 3, 2 * i + k) for k in range(2)]) for i, a in enumerate(outs[3:])]
    score = None
    for backs in ([0, 1], [2], [3]):
        ins = [part for group, back in enumerate(backs) for part in ins_of(back, group)]
        after = (done,) if score is None else ()
        last = backs[-1] == depth - 1
        score = step(fresh, inputs, score, ins, out_parts, backs, (rows_in, rows_out), depth, cap, last, after)
    return score


def solution(mesh):
    placed = (
        P(AXES, None),
        P(),
        P(AXES),
        P(AXES),
        P(),
        P(),
        P(),
        P(AXES, None),
        P(AXES, None),
    )
    return jax.shard_map(
        per_device,
        mesh=mesh,
        in_specs=placed,
        out_specs=(P(AXES, None), P(AXES)),
        check_vma=False,
    )
```

time: 210 us -> 129 us (0.61)
  waiting for transfers between devices: 104 us -> 36.4 us
  Pallas kernels: 0 us -> 41.9 us
  other arithmetic: 32.1 us -> 0.06 us
  starting transfers between devices: 6.2 us -> 34.4 us
  matrix products: 16.6 us -> 0 us
  local copies, waits for them, and re-layouts: 21.4 us -> 6.13 us
  between operations: 14.2 us -> 0.91 us
  blocking collectives: 14.3 us -> 9.34 us
    all_to_all x2 -> x1, waiting for transfers between devices: 103 us -> 3.66 us  [exchange(): return lax.all_to_all(x, AXES, split_axis=0, concat_axis=0, tiled=True)]
    pallas_call x0 -> x9, Pallas kernels: none -> 41.9 us  [the longest x3 19.7 us: step(): pl.pallas_call(functools.partial(step_kernel, n_in=len(in_arrays), n_out=...]
    ppermute x0 -> x29, waiting for transfers between devices: none -> 32.7 us  [send(): return lax.ppermute(x, AXES, [(d, to(d)) for d in range(devices)])]
    ppermute x0 -> x29, starting transfers between devices: none -> 30.9 us  [send(): return lax.ppermute(x, AXES, [(d, to(d)) for d in range(devices)])]
    gather x5 -> x0, local copies, waits for them, and re-layouts: 17.8 us -> none  [the longest x1 7.3 us: per_device(): fetched = states[jnp.maximum(asked, 0)].astype(jnp.bfloat16)]
    dot_general x3 -> x0, matrix products: 16.6 us -> none  [the longest x1 11.4 us: per_device(): lax.dot_general(hidden, lax.all_gather(tower_out, ('owner', 'worker'), ax...]
    scatter-add x2 -> x0, other arithmetic: 16 us -> none  [the longest x1 9.57 us: per_device(): jax.ops.segment_sum(changes.reshape(-1, width), owners_ids, num_segments=...]
    add x1 -> x0, other arithmetic: 6.25 us -> none  [per_device(): states + total / jnp.maximum(count, 1).astype(jnp.float32)[:, None]]
  transfers between devices with their start and end apart: 4 -> 30, of which waited for: 2 -> 6; matrix products, arithmetic and copies ran while one was open for 28% -> 0% of each run, Pallas kernels for 0% -> 26%
where the time goes in v1:
time: 129 us
  Pallas kernels  41.9 us (32%)
  waiting for transfers between devices  36.4 us (28%)
  starting transfers between devices  34.4 us (27%)
  blocking collectives  9.34 us (7%)
  local copies, waits for them, and re-layouts  6.13 us (5%)
    ppermute x29, waiting for transfers between devices, send(): return lax.ppermute(x, AXES, [(d, to(d)) for d in range(devices)])  32.7 us
    ppermute x29, starting transfers between devices, send(): return lax.ppermute(x, AXES, [(d, to(d)) for d in range(devices)])  30.9 us
    pallas_call x3, Pallas kernels, step(): pl.pallas_call(functools.partial(step_kernel, n_in=len(in_arrays), n_out=...  19.7 us
    all_to_all x1, blocking collectives, exchange(): return lax.all_to_all(x, AXES, split_axis=0, concat_axis=0, tiled=True)  9.34 us
    pallas_call x2, Pallas kernels, fetch(): pl.pallas_call(functools.partial(fetch_kernel, cap=cap, column=column), o...  8.22 us
    pallas_call x1, Pallas kernels, update(): pl.pallas_call(functools.partial(update_kernel, cap=cap), out_shape=jax.S...  6.81 us
    unnamed x22, local copies, waits for them, and re-layouts  6.01 us
    pallas_call x1, Pallas kernels, cell(): pl.pallas_call(cell_kernel, out_shape=jax.ShapeDtypeStruct((n, width), BF...  3.96 us
  transfers between devices with their start and end apart: 30, of which 6 were waited for; matrix products, arithmetic and copies ran while one was open for 0% of the time, Pallas kernels for 26%

profile of v1, /device:TPU:0, one launch (start us, length us, event | category | flops | bytes accessed | tf_op | source)
XLA Modules:
  0.0 129.0 jit_solution(7509359790839652423)
XLA Ops:
  3.9 1.6 %route.1 = (s32[32,64]{1,0:T(8,128)}, s32[2,512]{1,0:T(2,128)S(1)}, bf16[32,1024]{1,0:T(8,128)(2,1)S(1)}, bf16[32,1024]{1,0:T(8,128)(2,1)S(1)}) custom-call(s32[512,128]{1,0:T(8,128)S(1)} %bitcast.20, s32[1,512]{1,0:T(1,128)S(1)} %bitcast.22, s32[1,512]{1,0:T(1,128)S(1)} %bitcast.23, bf16[16,4096]{1,0:T(8,128)(2,1)S(1)} %copy-done.7), custom_call_target="tpu_custom_call" | custom-call | flops 1000000000 | bytes 1000000 | tf_op jit(solution)/shard_map/route/pallas_call | solution.py:99
  6.5 2.6 %collective-permute-start.2 = (bf16[128,1024]{1,0:T(8,128)(2,1)}, bf16[128,1024]{1,0:T(8,128)(2,1)S(1)}, u32[]{:S(2)}, u32[]{:S(2)}) collective-permute-start(bf16[128,1024]{1,0:T(8,128)(2,1)} %refs_4_.1), channel_id=1, source_target_pairs={{0,2},{1,3},{2,4},{3,5},{4,6},{5,7},{6,0},{7,1},{8,10},{9,11},{10,... | collective-permute-start | bytes 786440 | tf_op jit(solution)/shard_map/ppermute | solution.py:376
  9.1 1.5 %collective-permute-start = (bf16[128,1024]{1,0:T(8,128)(2,1)}, bf16[128,1024]{1,0:T(8,128)(2,1)S(1)}, u32[]{:S(2)}, u32[]{:S(2)}) collective-permute-start(bf16[128,1024]{1,0:T(8,128)(2,1)} %refs_4_.1), channel_id=1, source_target_pairs={{0,8},{1,9},{2,10},{3,11},{4,12},{5,13},{6,14},{7,15},{8,0},{9,1},... | collective-permute-start | bytes 786440 | tf_op jit(solution)/shard_map/ppermute | solution.py:376
  10.6 1.5 %collective-permute-start.1 = (bf16[128,1024]{1,0:T(8,128)(2,1)}, bf16[128,1024]{1,0:T(8,128)(2,1)S(1)}, u32[]{:S(2)}, u32[]{:S(2)}) collective-permute-start(bf16[128,1024]{1,0:T(8,128)(2,1)} %refs_4_.1), channel_id=1, source_target_pairs={{0,16},{1,17},{2,18},{3,19},{4,20},{5,21},{6,22},{7,23},{8,24},{9,... | collective-permute-start | bytes 786440 | tf_op jit(solution)/shard_map/ppermute | solution.py:376
  12.1 1.6 %collective-permute-start.4 = (bf16[64,1024]{1,0:T(8,128)(2,1)S(1)}, bf16[64,1024]{1,0:T(8,128)(2,1)S(1)}, u32[]{:S(2)}, u32[]{:S(2)}) collective-permute-start(bf16[64,1024]{1,0:T(8,128)(2,1)S(1)} %bitcast.24), channel_id=1, source_target_pairs={{0,2},{1,3},{2,4},{3,5},{4,6},{5,7},{6,0},{7,1},{8,10},{9,11},{10,... | collective-permute-start | bytes 393224 | tf_op jit(solution)/shard_map/ppermute | solution.py:376
  13.8 7.3 %collective-permute-done.4.refs_3_ = bf16[64,1024]{1,0:T(8,128)(2,1)S(1)} collective-permute-done((bf16[64,1024]{1,0:T(8,128)(2,1)S(1)}, bf16[64,1024]{1,0:T(8,128)(2,1)S(1)}, u32[]{:S(2)}, u32[]{:S(2)}) %collective-permute-start.4) | collective-permute-done | bytes 131104 | tf_op jit(solution)/shard_map/ppermute | solution.py:376
  21.1 1.5 %collective-permute-start.8 = (bf16[128,1024]{1,0:T(8,128)(2,1)S(1)}, bf16[128,1024]{1,0:T(8,128)(2,1)S(1)}, u32[]{:S(2)}, u32[]{:S(2)}) collective-permute-start(bf16[128,1024]{1,0:T(8,128)(2,1)S(1)} %collective-permute-done.2.refs_2_.refs_9_), channel_id=1, source_target_pairs={{0,16},{1,17},{2,18},{3,19},{4,20},{5,21},{6,22},{7,23},{8,24},{9,... | collective-permute-start | bytes 786440 | tf_op jit(solution)/shard_map/ppermute | solution.py:376
  22.6 1.5 %collective-permute-start.7 = (bf16[128,1024]{1,0:T(8,128)(2,1)S(1)}, bf16[128,1024]{1,0:T(8,128)(2,1)S(1)}, u32[]{:S(2)}, u32[]{:S(2)}) collective-permute-start(bf16[128,1024]{1,0:T(8,128)(2,1)S(1)} %collective-permute-done.2.refs_2_.refs_9_), channel_id=1, source_target_pairs={{0,8},{1,9},{2,10},{3,11},{4,12},{5,13},{6,14},{7,15},{8,0},{9,1},... | collective-permute-start | bytes 786440 | tf_op jit(solution)/shard_map/ppermute | solution.py:376
  24.1 1.3 collective-permute-start.9
  25.4 3.5 %all-to-all-start = ((s32[32,1,64]{2,1,0:T(1,128)}), s32[32,1,64]{2,1,0:T(1,128)S(1)}, u32[]{:S(2)}, u32[]{:S(2)}) async-start(s32[32,1,64]{2,1,0:T(1,128)} %bitcast.4), calls=%async_computation | async-start | bytes 32768 | tf_op jit(solution)/shard_map/all_to_all | solution.py:372
  28.9 1.8 %collective-permute-start.5 = (bf16[64,1024]{1,0:T(8,128)(2,1)S(1)}, bf16[64,1024]{1,0:T(8,128)(2,1)S(1)}, u32[]{:S(2)}, u32[]{:S(2)}) collective-permute-start(bf16[64,1024]{1,0:T(8,128)(2,1)S(1)} %slice.40), channel_id=1, source_target_pairs={{0,8},{1,9},{2,10},{3,11},{4,12},{5,13},{6,14},{7,15},{8,0},{9,1},... | collective-permute-start | bytes 393224 | tf_op jit(solution)/shard_map/ppermute | solution.py:376
  30.8 1.5 %collective-permute-start.6 = (bf16[64,1024]{1,0:T(8,128)(2,1)S(1)}, bf16[64,1024]{1,0:T(8,128)(2,1)S(1)}, u32[]{:S(2)}, u32[]{:S(2)}) collective-permute-start(bf16[64,1024]{1,0:T(8,128)(2,1)S(1)} %slice.41), channel_id=1, source_target_pairs={{0,16},{1,17},{2,18},{3,19},{4,20},{5,21},{6,22},{7,23},{8,24},{9,... | collective-permute-start | bytes 393224 | tf_op jit(solution)/shard_map/ppermute | solution.py:376
  32.3 3.7 %all-to-all-done = s32[32,1,64]{2,1,0:T(1,128)S(1)} async-done(((s32[32,1,64]{2,1,0:T(1,128)}), s32[32,1,64]{2,1,0:T(1,128)S(1)}, u32[]{:S(2)}, u32[]{:S(2)}) %all-to-all-start) | async-done | bytes 8224 | tf_op jit(solution)/shard_map/all_to_all | solution.py:372
  36.0 2.2 %copy-done.1 = f32[2048,512]{1,0:T(8,128)S(1)} copy-done((f32[2048,512]{1,0:T(8,128)S(1)}, f32[2048,512]{1,0:T(8,128)}, u32[]{:S(2)}) %copy-start.1) | copy-done | bytes 4194328
  38.2 3.0 %fetch.2.refs_6_.prior_ref = bf16[1024,512]{1,0:T(8,128)(2,1)S(1)} custom-call(s32[32,64]{1,0:T(8,128)S(1)} %bitcast.16, f32[2048,512]{1,0:T(8,128)S(1)} %copy-done.1, bf16[128,1024]{1,0:T(8,128)(2,1)S(1)} %collective-permute-done.refs_0_.refs_5_, bf16[128,1024]{1,0:T(8,128)(2,1)S(1)} %collective-permute-done.1.refs_1_.refs_6_, ...), custom_call_target="tpu_custom_call" | custom-call | flops 2147483648 | bytes 5000000 | tf_op jit(solution)/shard_map/fetch/pallas_call | solution.py:154
  43.7 5.2 %fetch.3.inputs_ref.refs_2_ = bf16[1024,512]{1,0:T(8,128)(2,1)S(1)} custom-call(s32[32,64]{1,0:T(8,128)S(1)} %bitcast.17, bf16[4096,512]{1,0:T(8,128)(2,1)S(1)} %copy-done, bf16[64,1024]{1,0:T(8,128)(2,1)S(1)} %collective-permute-done.5.refs_0_.refs_7_, bf16[64,1024]{1,0:T(8,128)(2,1)S(1)} %collective-permute-done.6.refs_1_.refs_8_, ...), custom_call_target="tpu_custom_call" | custom-call | flops 4294967296 | bytes 5000000 | tf_op jit(solution)/shard_map/fetch/pallas_call | solution.py:154
  50.5 3.4 %collective-permute-done.13.refs_2_.refs_5_ = bf16[128,1024]{1,0:T(8,128)(2,1)S(1)} collective-permute-done((bf16[128,1024]{1,0:T(8,128)(2,1)S(1)}, bf16[128,1024]{1,0:T(8,128)(2,1)S(1)}, u32[]{:S(2)}, u32[]{:S(2)}) %collective-permute-start.13) | collective-permute-done | bytes 262176 | tf_op jit(solution)/shard_map/ppermute | solution.py:376
  54.0 4.0 %cell.1.fresh_ref.refs_0_ = bf16[1024,512]{1,0:T(8,128)(2,1)S(1)} custom-call(bf16[1024,512]{1,0:T(8,128)(2,1)S(1)} %fetch.2.refs_6_.prior_ref, bf16[1024,512]{1,0:T(8,128)(2,1)S(1)} %fetch.3.inputs_ref.refs_2_, bf16[512,1536]{1,0:T(8,128)(2,1)S(1)} %copy-done.3, bf16[512,1536]{1,0:T(8,128)(2,1)S(1)} %copy-done.4, ...), custom_call_target="tpu_custom_call" | custom-call | flops 4000000000 | bytes 6000000 | tf_op jit(solution)/shard_map/cell/pallas_call | solution.py:188
  59.2 1.4 %collective-permute-start.21 = (bf16[128,1024]{1,0:T(8,128)(2,1)S(1)}, bf16[128,1024]{1,0:T(8,128)(2,1)S(1)}, u32[]{:S(2)}, u32[]{:S(2)}) collective-permute-start(bf16[128,1024]{1,0:T(8,128)(2,1)S(1)} %collective-permute-done.9.refs_4_.refs_5_), channel_id=1, source_target_pairs={{0,8},{1,9},{2,10},{3,11},{4,12},{5,13},{6,14},{7,15},{8,0},{9,1},... | collective-permute-start | bytes 786440 | tf_op jit(solution)/shard_map/ppermute | solution.py:376
  60.7 17.6 %collective-permute-done.21.refs_6_ = bf16[128,1024]{1,0:T(8,128)(2,1)S(1)} collective-permute-done((bf16[128,1024]{1,0:T(8,128)(2,1)S(1)}, bf16[128,1024]{1,0:T(8,128)(2,1)S(1)}, u32[]{:S(2)}, u32[]{:S(2)}) %collective-permute-start.21) | collective-permute-done | bytes 262176 | tf_op jit(solution)/shard_map/ppermute | solution.py:376
  78.3 1.5 %collective-permute-start.26 = (bf16[128,1024]{1,0:T(8,128)(2,1)S(1)}, bf16[128,1024]{1,0:T(8,128)(2,1)S(1)}, u32[]{:S(2)}, u32[]{:S(2)}) collective-permute-start(bf16[128,1024]{1,0:T(8,128)(2,1)S(1)} %collective-permute-done.13.refs_2_.refs_5_), channel_id=1, source_target_pairs={{0,16},{1,17},{2,18},{3,19},{4,20},{5,21},{6,22},{7,23},{8,24},{9,... | collective-permute-start | bytes 786440 | tf_op jit(solution)/shard_map/ppermute | solution.py:376
  80.4 1.6 %collective-permute-start.19 = (bf16[128,1024]{1,0:T(8,128)(2,1)S(1)}, bf16[128,1024]{1,0:T(8,128)(2,1)S(1)}, u32[]{:S(2)}, u32[]{:S(2)}) collective-permute-start(bf16[128,1024]{1,0:T(8,128)(2,1)S(1)} %slice.44), channel_id=1, source_target_pairs={{0,8},{1,9},{2,10},{3,11},{4,12},{5,13},{6,14},{7,15},{8,0},{9,1},... | collective-permute-start | bytes 786440 | tf_op jit(solution)/shard_map/ppermute | solution.py:376
  82.1 3.8 %collective-permute-done.26.refs_7_ = bf16[128,1024]{1,0:T(8,128)(2,1)S(1)} collective-permute-done((bf16[128,1024]{1,0:T(8,128)(2,1)S(1)}, bf16[128,1024]{1,0:T(8,128)(2,1)S(1)}, u32[]{:S(2)}, u32[]{:S(2)}) %collective-permute-start.26) | collective-permute-done | bytes 262176 | tf_op jit(solution)/shard_map/ppermute | solution.py:376
  85.9 1.5 %collective-permute-start.20 = (bf16[128,1024]{1,0:T(8,128)(2,1)S(1)}, bf16[128,1024]{1,0:T(8,128)(2,1)S(1)}, u32[]{:S(2)}, u32[]{:S(2)}) collective-permute-start(bf16[128,1024]{1,0:T(8,128)(2,1)S(1)} %slice.45), channel_id=1, source_target_pairs={{0,16},{1,17},{2,18},{3,19},{4,20},{5,21},{6,22},{7,23},{8,24},{9,... | collective-permute-start | bytes 786440 | tf_op jit(solution)/shard_map/ppermute | solution.py:376
  87.4 6.8 %update.1.refs_19_ = f32[2048,512]{1,0:T(8,128)} custom-call(s32[32,64]{1,0:T(8,128)S(1)} %bitcast.18, bf16[1024,512]{1,0:T(8,128)(2,1)S(1)} %cell.1.fresh_ref.refs_0_, f32[2048,512]{1,0:T(8,128)S(1)} %copy-done.2, bf16[256,1024]{1,0:T(8,128)(2,1)S(1)} %collective-permute-done.15.refs_0_.refs_15_.refs_11_, ...), custom_call_target="tpu_custom_call" | custom-call | flops 4000000000 | bytes 10000000 | tf_op jit(solution)/shard_map/update/pallas_call | solution.py:228
  95.5 1.4 %collective-permute-start.27 = (bf16[64,1024]{1,0:T(8,128)(2,1)S(1)}, bf16[64,1024]{1,0:T(8,128)(2,1)S(1)}, u32[]{:S(2)}, u32[]{:S(2)}) collective-permute-start(bf16[64,1024]{1,0:T(8,128)(2,1)S(1)} %slice.48), channel_id=1, source_target_pairs={{0,8},{1,9},{2,10},{3,11},{4,12},{5,13},{6,14},{7,15},{8,0},{9,1},... | collective-permute-start | bytes 393224 | tf_op jit(solution)/shard_map/ppermute | solution.py:376
  97.0 1.5 %collective-permute-start.28 = (bf16[64,1024]{1,0:T(8,128)(2,1)S(1)}, bf16[64,1024]{1,0:T(8,128)(2,1)S(1)}, u32[]{:S(2)}, u32[]{:S(2)}) collective-permute-start(bf16[64,1024]{1,0:T(8,128)(2,1)S(1)} %slice.49), channel_id=1, source_target_pairs={{0,16},{1,17},{2,18},{3,19},{4,20},{5,21},{6,22},{7,23},{8,24},{9,... | collective-permute-start | bytes 393224 | tf_op jit(solution)/shard_map/ppermute | solution.py:376
  98.4 8.9 %tower.3.refs_4_ = f32[32,64]{1,0:T(8,128)S(1)} custom-call(bf16[1024,512]{1,0:T(8,128)(2,1)S(1)} %cell.1.fresh_ref.refs_0_, bf16[1024,512]{1,0:T(8,128)(2,1)S(1)} %collective-permute-done.17.refs_1_, bf16[1024,512]{1,0:T(8,128)(2,1)S(1)} %fetch.3.inputs_ref.refs_2_, bf16[1024,512]{1,0:T(8,128)(2,1)S(1)} %collective-permute-done.18.refs_3_, ...), custom_call_target="tpu_custom_call" | custom-call | flops 6442450944 | bytes 10000000 | tf_op jit(solution)/shard_map/tower/pallas_call | solution.py:316
  107.4 5.3 %tower.4.refs_4_ = f32[32,64]{1,0:T(8,128)S(1)} custom-call(bf16[1024,512]{1,0:T(8,128)(2,1)S(1)} %cell.1.fresh_ref.refs_0_, bf16[1024,512]{1,0:T(8,128)(2,1)S(1)} %collective-permute-done.17.refs_1_, bf16[1024,512]{1,0:T(8,128)(2,1)S(1)} %fetch.3.inputs_ref.refs_2_, bf16[1024,512]{1,0:T(8,128)(2,1)S(1)} %collective-permute-done.18.refs_3_, ...), custom_call_target="tpu_custom_call" | custom-call | flops 3221225472 | bytes 10000000 | tf_op jit(solution)/shard_map/tower/pallas_call | solution.py:316
  112.6 5.5 %tower.5 = f32[32,64]{1,0:T(8,128)S(1)} custom-call(bf16[1024,512]{1,0:T(8,128)(2,1)S(1)} %cell.1.fresh_ref.refs_0_, bf16[1024,512]{1,0:T(8,128)(2,1)S(1)} %collective-permute-done.17.refs_1_, bf16[1024,512]{1,0:T(8,128)(2,1)S(1)} %fetch.3.inputs_ref.refs_2_, bf16[1024,512]{1,0:T(8,128)(2,1)S(1)} %collective-permute-done.18.refs_3_, ...), custom_call_target="tpu_custom_call" | custom-call | flops 3221225472 | bytes 10000000 | tf_op jit(solution)/shard_map/tower/pallas_call | solution.py:316
  118.2 9.3 %all_to_all.22 = f32[32,1,64]{2,1,0:T(1,128)} all-to-all(f32[32,1,64]{2,1,0:T(1,128)S(1)} %bitcast.19), channel_id=1, replica_groups=mesh['owner'=4,'worker'=8] {'owner','worker'}, dimensions={0} | all-to-all | bytes 16384 | tf_op jit(solution)/shard_map/all_to_all | solution.py:372
  127.5 1.5 %pick.1 = f32[1,512]{1,0:T(1,128)} custom-call(f32[32,64]{1,0:T(8,128)} %bitcast.26, s32[2,512]{1,0:T(2,128)} %copy-done.10), custom_call_target="tpu_custom_call" | custom-call | flops 100000000 | bytes 100000 | tf_op jit(solution)/shard_map/pick/pallas_call | solution.py:361
  (73 shorter events, 11.6 us)
Async XLA Ops:
  6.1 6.0 %collective-permute-start.3 = (bf16[2,16,1024]{2,1,0:T(8,128)(2,1)S(1)}, bf16[2,16,1024]{2,1,0:T(8,128)(2,1)S(1)}, u32[]{:S(2)}, u32[]{:S(2)}) collective-permute-start(bf16[2,16,1024]{2,1,0:T(8,128)(2,1)S(1)} %bitcast.21), channel_id=1, source_target_pairs={{0,1},{1,0},{2,3},{3,2},{4,5},{5,4},{6,7},{7,6},{8,9},{9,8},{10,11... | collective-permute-start | bytes 196616 | tf_op jit(solution)/shard_map/ppermute | solution.py:376
  6.5 14.6 %collective-permute-start.2 = (bf16[128,1024]{1,0:T(8,128)(2,1)}, bf16[128,1024]{1,0:T(8,128)(2,1)S(1)}, u32[]{:S(2)}, u32[]{:S(2)}) collective-permute-start(bf16[128,1024]{1,0:T(8,128)(2,1)} %refs_4_.1), channel_id=1, source_target_pairs={{0,2},{1,3},{2,4},{3,5},{4,6},{5,7},{6,0},{7,1},{8,10},{9,11},{10,... | collective-permute-start | bytes 786440 | tf_op jit(solution)/shard_map/ppermute | solution.py:376
  9.1 19.8 %collective-permute-start = (bf16[128,1024]{1,0:T(8,128)(2,1)}, bf16[128,1024]{1,0:T(8,128)(2,1)S(1)}, u32[]{:S(2)}, u32[]{:S(2)}) collective-permute-start(bf16[128,1024]{1,0:T(8,128)(2,1)} %refs_4_.1), channel_id=1, source_target_pairs={{0,8},{1,9},{2,10},{3,11},{4,12},{5,13},{6,14},{7,15},{8,0},{9,1},... | collective-permute-start | bytes 786440 | tf_op jit(solution)/shard_map/ppermute | solution.py:376
  10.6 13.6 %collective-permute-start.1 = (bf16[128,1024]{1,0:T(8,128)(2,1)}, bf16[128,1024]{1,0:T(8,128)(2,1)S(1)}, u32[]{:S(2)}, u32[]{:S(2)}) collective-permute-start(bf16[128,1024]{1,0:T(8,128)(2,1)} %refs_4_.1), channel_id=1, source_target_pairs={{0,16},{1,17},{2,18},{3,19},{4,20},{5,21},{6,22},{7,23},{8,24},{9,... | collective-permute-start | bytes 786440 | tf_op jit(solution)/shard_map/ppermute | solution.py:376
  12.1 9.0 %collective-permute-start.4 = (bf16[64,1024]{1,0:T(8,128)(2,1)S(1)}, bf16[64,1024]{1,0:T(8,128)(2,1)S(1)}, u32[]{:S(2)}, u32[]{:S(2)}) collective-permute-start(bf16[64,1024]{1,0:T(8,128)(2,1)S(1)} %bitcast.24), channel_id=1, source_target_pairs={{0,2},{1,3},{2,4},{3,5},{4,6},{5,7},{6,0},{7,1},{8,10},{9,11},{10,... | collective-permute-start | bytes 393224 | tf_op jit(solution)/shard_map/ppermute | solution.py:376
  21.1 9.7 %collective-permute-start.10 = (bf16[64,1024]{1,0:T(8,128)(2,1)S(1)}, bf16[64,1024]{1,0:T(8,128)(2,1)S(1)}, u32[]{:S(2)}, u32[]{:S(2)}) collective-permute-start(bf16[64,1024]{1,0:T(8,128)(2,1)S(1)} %collective-permute-done.4.refs_3_), channel_id=1, source_target_pairs={{0,2},{1,3},{2,4},{3,5},{4,6},{5,7},{6,0},{7,1},{8,10},{9,11},{10,... | collective-permute-start | bytes 393224 | tf_op jit(solution)/shard_map/ppermute | solution.py:376
  21.1 20.1 %collective-permute-start.8 = (bf16[128,1024]{1,0:T(8,128)(2,1)S(1)}, bf16[128,1024]{1,0:T(8,128)(2,1)S(1)}, u32[]{:S(2)}, u32[]{:S(2)}) collective-permute-start(bf16[128,1024]{1,0:T(8,128)(2,1)S(1)} %collective-permute-done.2.refs_2_.refs_9_), channel_id=1, source_target_pairs={{0,16},{1,17},{2,18},{3,19},{4,20},{5,21},{6,22},{7,23},{8,24},{9,... | collective-permute-start | bytes 786440 | tf_op jit(solution)/shard_map/ppermute | solution.py:376
  22.6 19.1 %collective-permute-start.7 = (bf16[128,1024]{1,0:T(8,128)(2,1)S(1)}, bf16[128,1024]{1,0:T(8,128)(2,1)S(1)}, u32[]{:S(2)}, u32[]{:S(2)}) collective-permute-start(bf16[128,1024]{1,0:T(8,128)(2,1)S(1)} %collective-permute-done.2.refs_2_.refs_9_), channel_id=1, source_target_pairs={{0,8},{1,9},{2,10},{3,11},{4,12},{5,13},{6,14},{7,15},{8,0},{9,1},... | collective-permute-start | bytes 786440 | tf_op jit(solution)/shard_map/ppermute | solution.py:376
  24.1 19.0 %collective-permute-start.9 = (bf16[128,1024]{1,0:T(8,128)(2,1)S(1)}, bf16[128,1024]{1,0:T(8,128)(2,1)S(1)}, u32[]{:S(2)}, u32[]{:S(2)}) collective-permute-start(bf16[128,1024]{1,0:T(8,128)(2,1)S(1)} %collective-permute-done.2.refs_2_.refs_9_), channel_id=1, source_target_pairs={{0,2},{1,3},{2,4},{3,5},{4,6},{5,7},{6,0},{7,1},{8,10},{9,11},{10,... | collective-permute-start | bytes 786440 | tf_op jit(solution)/shard_map/ppermute | solution.py:376
  25.4 10.5 %all-to-all-start = ((s32[32,1,64]{2,1,0:T(1,128)}), s32[32,1,64]{2,1,0:T(1,128)S(1)}, u32[]{:S(2)}, u32[]{:S(2)}) async-start(s32[32,1,64]{2,1,0:T(1,128)} %bitcast.4), calls=%async_computation | async-start | bytes 32768 | tf_op jit(solution)/shard_map/all_to_all | solution.py:372
  28.9 13.6 %collective-permute-start.5 = (bf16[64,1024]{1,0:T(8,128)(2,1)S(1)}, bf16[64,1024]{1,0:T(8,128)(2,1)S(1)}, u32[]{:S(2)}, u32[]{:S(2)}) collective-permute-start(bf16[64,1024]{1,0:T(8,128)(2,1)S(1)} %slice.40), channel_id=1, source_target_pairs={{0,8},{1,9},{2,10},{3,11},{4,12},{5,13},{6,14},{7,15},{8,0},{9,1},... | collective-permute-start | bytes 393224 | tf_op jit(solution)/shard_map/ppermute | solution.py:376
  30.8 12.9 %collective-permute-start.6 = (bf16[64,1024]{1,0:T(8,128)(2,1)S(1)}, bf16[64,1024]{1,0:T(8,128)(2,1)S(1)}, u32[]{:S(2)}, u32[]{:S(2)}) collective-permute-start(bf16[64,1024]{1,0:T(8,128)(2,1)S(1)} %slice.41), channel_id=1, source_target_pairs={{0,16},{1,17},{2,18},{3,19},{4,20},{5,21},{6,22},{7,23},{8,24},{9,... | collective-permute-start | bytes 393224 | tf_op jit(solution)/shard_map/ppermute | solution.py:376
  41.2 8.2 %collective-permute-start.14 = (bf16[64,1024]{1,0:T(8,128)(2,1)S(1)}, bf16[64,1024]{1,0:T(8,128)(2,1)S(1)}, u32[]{:S(2)}, u32[]{:S(2)}) collective-permute-start(bf16[64,1024]{1,0:T(8,128)(2,1)S(1)} %collective-permute-done.10.refs_5_), channel_id=1, source_target_pairs={{0,2},{1,3},{2,4},{3,5},{4,6},{5,7},{6,0},{7,1},{8,10},{9,11},{10,... | collective-permute-start | bytes 393224 | tf_op jit(solution)/shard_map/ppermute | solution.py:376
  41.8 8.7 %collective-permute-start.11 = (bf16[64,1024]{1,0:T(8,128)(2,1)S(1)}, bf16[64,1024]{1,0:T(8,128)(2,1)S(1)}, u32[]{:S(2)}, u32[]{:S(2)}) collective-permute-start(bf16[64,1024]{1,0:T(8,128)(2,1)S(1)} %slice.42), channel_id=1, source_target_pairs={{0,8},{1,9},{2,10},{3,11},{4,12},{5,13},{6,14},{7,15},{8,0},{9,1},... | collective-permute-start | bytes 393224 | tf_op jit(solution)/shard_map/ppermute | solution.py:376
  42.5 8.0 %collective-permute-start.12 = (bf16[64,1024]{1,0:T(8,128)(2,1)S(1)}, bf16[64,1024]{1,0:T(8,128)(2,1)S(1)}, u32[]{:S(2)}, u32[]{:S(2)}) collective-permute-start(bf16[64,1024]{1,0:T(8,128)(2,1)S(1)} %slice.43), channel_id=1, source_target_pairs={{0,16},{1,17},{2,18},{3,19},{4,20},{5,21},{6,22},{7,23},{8,24},{9,... | collective-permute-start | bytes 393224 | tf_op jit(solution)/shard_map/ppermute | solution.py:376
  43.2 10.8 %collective-permute-start.13 = (bf16[128,1024]{1,0:T(8,128)(2,1)S(1)}, bf16[128,1024]{1,0:T(8,128)(2,1)S(1)}, u32[]{:S(2)}, u32[]{:S(2)}) collective-permute-start(bf16[128,1024]{1,0:T(8,128)(2,1)S(1)} %collective-permute-done.9.refs_4_.refs_5_), channel_id=1, source_target_pairs={{0,2},{1,3},{2,4},{3,5},{4,6},{5,7},{6,0},{7,1},{8,10},{9,11},{10,... | collective-permute-start | bytes 786440 | tf_op jit(solution)/shard_map/ppermute | solution.py:376
  48.9 38.5 %copy-start.2 = (f32[2048,512]{1,0:T(8,128)S(1)}, f32[2048,512]{1,0:T(8,128)}, u32[]{:S(2)}) copy-start(f32[2048,512]{1,0:T(8,128)} %states_ref.1) | copy-start | bytes 12582916
  48.9 48.0 %collective-permute-start.18 = (bf16[1024,512]{1,0:T(8,128)(2,1)S(1)}, bf16[1024,512]{1,0:T(8,128)(2,1)S(1)}, u32[]{:S(2)}, u32[]{:S(2)}) collective-permute-start(bf16[1024,512]{1,0:T(8,128)(2,1)S(1)} %fetch.3.inputs_ref.refs_2_), channel_id=1, source_target_pairs={{0,1},{1,0},{2,3},{3,2},{4,5},{5,4},{6,7},{7,6},{8,9},{9,8},{10,11... | collective-permute-start | bytes 3145736 | tf_op jit(solution)/shard_map/ppermute | solution.py:376
  49.4 9.8 %collective-permute-start.22 = (bf16[128,1024]{1,0:T(8,128)(2,1)S(1)}, bf16[128,1024]{1,0:T(8,128)(2,1)S(1)}, u32[]{:S(2)}, u32[]{:S(2)}) collective-permute-start(bf16[128,1024]{1,0:T(8,128)(2,1)S(1)} %collective-permute-done.9.refs_4_.refs_5_), channel_id=1, source_target_pairs={{0,16},{1,17},{2,18},{3,19},{4,20},{5,21},{6,22},{7,23},{8,24},{9,... | collective-permute-start | bytes 786440 | tf_op jit(solution)/shard_map/ppermute | solution.py:376
  57.9 40.5 %collective-permute-start.17 = (bf16[1024,512]{1,0:T(8,128)(2,1)S(1)}, bf16[1024,512]{1,0:T(8,128)(2,1)S(1)}, u32[]{:S(2)}, u32[]{:S(2)}) collective-permute-start(bf16[1024,512]{1,0:T(8,128)(2,1)S(1)} %cell.1.fresh_ref.refs_0_), channel_id=1, source_target_pairs={{0,1},{1,0},{2,3},{3,2},{4,5},{5,4},{6,7},{7,6},{8,9},{9,8},{10,11... | collective-permute-start | bytes 3145736 | tf_op jit(solution)/shard_map/ppermute | solution.py:376
  58.0 21.8 %collective-permute-start.16 = (bf16[256,1024]{1,0:T(8,128)(2,1)S(1)}, bf16[256,1024]{1,0:T(8,128)(2,1)S(1)}, u32[]{:S(2)}, u32[]{:S(2)}) collective-permute-start(bf16[256,1024]{1,0:T(8,128)(2,1)S(1)} %pad_maximum_fusion.refs_14_.refs_10_), channel_id=1, source_target_pairs={{0,16},{1,17},{2,18},{3,19},{4,20},{5,21},{6,22},{7,23},{8,24},{9,... | collective-permute-start | bytes 1572872 | tf_op jit(solution)/shard_map/ppermute | solution.py:376
  58.6 21.7 %collective-permute-start.15 = (bf16[256,1024]{1,0:T(8,128)(2,1)S(1)}, bf16[256,1024]{1,0:T(8,128)(2,1)S(1)}, u32[]{:S(2)}, u32[]{:S(2)}) collective-permute-start(bf16[256,1024]{1,0:T(8,128)(2,1)S(1)} %pad_maximum_fusion.refs_14_.refs_10_), channel_id=1, source_target_pairs={{0,8},{1,9},{2,10},{3,11},{4,12},{5,13},{6,14},{7,15},{8,0},{9,1},... | collective-permute-start | bytes 1572872 | tf_op jit(solution)/shard_map/ppermute | solution.py:376
  59.2 19.0 %collective-permute-start.21 = (bf16[128,1024]{1,0:T(8,128)(2,1)S(1)}, bf16[128,1024]{1,0:T(8,128)(2,1)S(1)}, u32[]{:S(2)}, u32[]{:S(2)}) collective-permute-start(bf16[128,1024]{1,0:T(8,128)(2,1)S(1)} %collective-permute-done.9.refs_4_.refs_5_), channel_id=1, source_target_pairs={{0,8},{1,9},{2,10},{3,11},{4,12},{5,13},{6,14},{7,15},{8,0},{9,1},... | collective-permute-start | bytes 786440 | tf_op jit(solution)/shard_map/ppermute | solution.py:376
  78.3 7.6 %collective-permute-start.26 = (bf16[128,1024]{1,0:T(8,128)(2,1)S(1)}, bf16[128,1024]{1,0:T(8,128)(2,1)S(1)}, u32[]{:S(2)}, u32[]{:S(2)}) collective-permute-start(bf16[128,1024]{1,0:T(8,128)(2,1)S(1)} %collective-permute-done.13.refs_2_.refs_5_), channel_id=1, source_target_pairs={{0,16},{1,17},{2,18},{3,19},{4,20},{5,21},{6,22},{7,23},{8,24},{9,... | collective-permute-start | bytes 786440 | tf_op jit(solution)/shard_map/ppermute | solution.py:376
  79.8 14.4 %collective-permute-start.25 = (bf16[128,1024]{1,0:T(8,128)(2,1)S(1)}, bf16[128,1024]{1,0:T(8,128)(2,1)S(1)}, u32[]{:S(2)}, u32[]{:S(2)}) collective-permute-start(bf16[128,1024]{1,0:T(8,128)(2,1)S(1)} %collective-permute-done.13.refs_2_.refs_5_), channel_id=1, source_target_pairs={{0,8},{1,9},{2,10},{3,11},{4,12},{5,13},{6,14},{7,15},{8,0},{9,1},... | collective-permute-start | bytes 786440 | tf_op jit(solution)/shard_map/ppermute | solution.py:376
  80.4 14.4 %collective-permute-start.19 = (bf16[128,1024]{1,0:T(8,128)(2,1)S(1)}, bf16[128,1024]{1,0:T(8,128)(2,1)S(1)}, u32[]{:S(2)}, u32[]{:S(2)}) collective-permute-start(bf16[128,1024]{1,0:T(8,128)(2,1)S(1)} %slice.44), channel_id=1, source_target_pairs={{0,8},{1,9},{2,10},{3,11},{4,12},{5,13},{6,14},{7,15},{8,0},{9,1},... | collective-permute-start | bytes 786440 | tf_op jit(solution)/shard_map/ppermute | solution.py:376
  82.0 16.4 %copy-start.6 = (bf16[128,1024]{1,0:T(8,128)(2,1)S(1)}, bf16[128,1024]{1,0:T(8,128)(2,1)}, u32[]{:S(2)}) copy-start(bf16[128,1024]{1,0:T(8,128)(2,1)} %refs_4_.1) | copy-start | bytes 786436
  85.9 9.6 %collective-permute-start.20 = (bf16[128,1024]{1,0:T(8,128)(2,1)S(1)}, bf16[128,1024]{1,0:T(8,128)(2,1)S(1)}, u32[]{:S(2)}, u32[]{:S(2)}) collective-permute-start(bf16[128,1024]{1,0:T(8,128)(2,1)S(1)} %slice.45), channel_id=1, source_target_pairs={{0,16},{1,17},{2,18},{3,19},{4,20},{5,21},{6,22},{7,23},{8,24},{9,... | collective-permute-start | bytes 786440 | tf_op jit(solution)/shard_map/ppermute | solution.py:376
  94.2 13.2 %collective-permute-start.23 = (bf16[64,1024]{1,0:T(8,128)(2,1)S(1)}, bf16[64,1024]{1,0:T(8,128)(2,1)S(1)}, u32[]{:S(2)}, u32[]{:S(2)}) collective-permute-start(bf16[64,1024]{1,0:T(8,128)(2,1)S(1)} %slice.46), channel_id=1, source_target_pairs={{0,8},{1,9},{2,10},{3,11},{4,12},{5,13},{6,14},{7,15},{8,0},{9,1},... | collective-permute-start | bytes 393224 | tf_op jit(solution)/shard_map/ppermute | solution.py:376
  94.8 12.6 %collective-permute-start.24 = (bf16[64,1024]{1,0:T(8,128)(2,1)S(1)}, bf16[64,1024]{1,0:T(8,128)(2,1)S(1)}, u32[]{:S(2)}, u32[]{:S(2)}) collective-permute-start(bf16[64,1024]{1,0:T(8,128)(2,1)S(1)} %slice.47), channel_id=1, source_target_pairs={{0,16},{1,17},{2,18},{3,19},{4,20},{5,21},{6,22},{7,23},{8,24},{9,... | collective-permute-start | bytes 393224 | tf_op jit(solution)/shard_map/ppermute | solution.py:376
  95.5 17.1 %collective-permute-start.27 = (bf16[64,1024]{1,0:T(8,128)(2,1)S(1)}, bf16[64,1024]{1,0:T(8,128)(2,1)S(1)}, u32[]{:S(2)}, u32[]{:S(2)}) collective-permute-start(bf16[64,1024]{1,0:T(8,128)(2,1)S(1)} %slice.48), channel_id=1, source_target_pairs={{0,8},{1,9},{2,10},{3,11},{4,12},{5,13},{6,14},{7,15},{8,0},{9,1},... | collective-permute-start | bytes 393224 | tf_op jit(solution)/shard_map/ppermute | solution.py:376
  97.0 15.7 %collective-permute-start.28 = (bf16[64,1024]{1,0:T(8,128)(2,1)S(1)}, bf16[64,1024]{1,0:T(8,128)(2,1)S(1)}, u32[]{:S(2)}, u32[]{:S(2)}) collective-permute-start(bf16[64,1024]{1,0:T(8,128)(2,1)S(1)} %slice.49), channel_id=1, source_target_pairs={{0,16},{1,17},{2,18},{3,19},{4,20},{5,21},{6,22},{7,23},{8,24},{9,... | collective-permute-start | bytes 393224 | tf_op jit(solution)/shard_map/ppermute | solution.py:376
  (9 other events, 34.5 us)

commit v2 on v1

--- a/solution.py
+++ b/solution.py
@@ -37,12 +37,18 @@
     return a, b, (r - b.astype(F32)).astype(BF16)
 
 
-def route_kernel(table_hbm, users_ref, feats_ref, *refs, shards, cap, row_count, chips):
-    table_ref, sem = refs[-2:]
-    copy = pltpu.make_async_copy(table_hbm, table_ref, sem)
-    copy.start()
+def route_kernel(*refs, shards, cap, row_count, chips):
+    n = 4 if chips else 3
+    sources, held, sems = refs[:n], refs[-n - 1 : -1], refs[-1]
+    copies = [pltpu.make_async_copy(a, b, sems.at[k]) for k, (a, b) in enumerate(zip(sources, held, strict=True))]
+    for copy in copies:
+        copy.start()
+    table_ref, users_ref, feats_ref = held[:3]
+    req_ref, slot_ref = refs[n : n + 2]
     if chips:
-        wout_ref, req_ref, slot_ref, mine_ref, theirs_ref = refs[:5]
+        mine_ref, theirs_ref = refs[n + 2 : n + 4]
+        wout_ref = held[3]
+        copies[3].wait()
         owners, depth = chips
         units = wout_ref.shape[1] // (2 * owners * depth)
         rows = wout_ref.shape[0]
@@ -55,13 +61,12 @@
                 line = slice((place // (depth // 2)) * rows, (place // (depth // 2) + 1) * rows)
                 mine_ref[line, to : to + units] = jnp.where(even, a, b)
                 theirs_ref[line, to : to + units] = jnp.where(even, b, a)
-    else:
-        req_ref, slot_ref = refs[:2]
+    copies[1].wait()
     users = users_ref[...]
     events = users.shape[1]
     high, low = users >> 7, users & 127
     pick = onehot(iota((table_ref.shape[0], events), 0) == high)
-    copy.wait()
+    copies[0].wait()
     table = table_ref[...]
     parts = [((table >> (8 * k)) & 255).astype(F32).astype(BF16) for k in range(3)]
     got = dot(jnp.concatenate(parts, axis=1), pick, 0, 0)
@@ -81,6 +86,7 @@
     rank = dot(hit.astype(BF16), before)
     rank = jnp.sum(hit * rank, axis=0, keepdims=True).astype(I32)
     place = onehot(iota((cap, events), 0) == rank)
+    copies[2].wait()
     feats = feats_ref[...]
     bytes_of = [(v & 255).astype(F32) for v in (local >> 8, local, feats >> 8, feats)]
     filled = dot(jnp.concatenate([hit * v for v in bytes_of], axis=0).astype(BF16), place, 1, 1)
@@ -93,7 +99,8 @@
 
 def route(row_of_user, event_users, event_features, tower_out, shards, cap, row_count, chips):
     events = event_users.shape[0]
-    table = row_of_user.reshape(-1, LANES)
+    arrays = [row_of_user.reshape(-1, LANES), event_users.reshape(1, events), event_features.reshape(1, events)]
+    arrays += [tower_out] if chips else []
     rows, hidden = tower_out.shape
     cut = [jax.ShapeDtypeStruct((2 * rows, hidden // 4), BF16)] * 2 if chips else []
     return pl.pallas_call(
@@ -103,13 +110,13 @@
             jax.ShapeDtypeStruct((2, events), I32),
             *cut,
         ],
-        in_specs=[HBM, VMEM, VMEM] + [VMEM] * bool(chips),
+        in_specs=[HBM] * len(arrays),
         out_specs=[VMEM] * (2 + len(cut)),
-        scratch_shapes=[pltpu.VMEM(table.shape, I32), pltpu.SemaphoreType.DMA],
-        compiler_params=pltpu.CompilerParams(vmem_limit_bytes=24 * 2**20),
+        scratch_shapes=[pltpu.VMEM(a.shape, a.dtype) for a in arrays] + [pltpu.SemaphoreType.DMA((len(arrays),))],
+        compiler_params=pltpu.CompilerParams(vmem_limit_bytes=60 * 2**20),
         cost_estimate=pl.CostEstimate(flops=10**9, bytes_accessed=10**6, transcendentals=0),
         name="route",
-    )(table, event_users.reshape(1, events), event_features.reshape(1, events), *([tower_out] if chips else []))
+    )(*arrays)
 
 
 def slot_column(asked, n, cap):
@@ -157,49 +164,50 @@
         in_specs=[VMEM, HBM] + [ANY] * len(after),
         out_specs=VMEM,
         scratch_shapes=[pltpu.VMEM(table.shape, table.dtype), *low, pltpu.SemaphoreType.DMA],
-        compiler_params=pltpu.CompilerParams(vmem_limit_bytes=32 * 2**20),
-        cost_estimate=pl.CostEstimate(flops=2 * n * width * table.shape[0], bytes_accessed=5 * 10**6, transcendentals=0),
+        compiler_params=pltpu.CompilerParams(vmem_limit_bytes=24 * 2**20),
+        cost_estimate=pl.CostEstimate(flops=10 * n * width * table.shape[0], bytes_accessed=5 * 10**6, transcendentals=0),
         name="fetch",
     )(asked, table, *after)
 
 
 def cell_kernel(prior_ref, inputs_ref, gin_hbm, gst_hbm, *refs):
-    fresh_ref, gin_ref, gst_ref, sems = refs[-4:]
+    joined_ref, gin_ref, gst_ref, sems = refs[-4:]
     copies = [pltpu.make_async_copy(gst_hbm, gst_ref, sems.at[0]), pltpu.make_async_copy(gin_hbm, gin_ref, sems.at[1])]
     for copy in copies:
         copy.start()
     for copy in copies:
         copy.wait()
-    n, width = fresh_ref.shape
+    n, width = prior_ref.shape
     for k in range(n // CHUNK):
         at = slice(k * CHUNK, (k + 1) * CHUNK)
         prior = prior_ref[at, :]
+        joined_ref[at, width:] = inputs_ref[at, :]
         gh = dot(prior, gst_ref[...])
         gx = dot(inputs_ref[at, :], gin_ref[...])
         reset = sigmoid(gx[:, :width] + gh[:, :width])
         update = sigmoid(gx[:, width : 2 * width] + gh[:, width : 2 * width])
         cand = jnp.tanh(gx[:, 2 * width :] + reset * gh[:, 2 * width :])
         fresh = (1.0 - update) * cand + update * prior.astype(F32)
-        fresh_ref[at, :] = fresh.astype(BF16)
+        joined_ref[at, :width] = fresh.astype(BF16)
 
 
 def cell(prior, inputs, gate_in, gate_state, after=()):
     n, width = prior.shape
     return pl.pallas_call(
         cell_kernel,
-        out_shape=jax.ShapeDtypeStruct((n, width), BF16),
+        out_shape=jax.ShapeDtypeStruct((n, 2 * width), BF16),
         in_specs=[VMEM, VMEM, HBM, HBM] + [ANY] * len(after),
         out_specs=VMEM,
         scratch_shapes=[pltpu.VMEM(gate_in.shape, BF16)] * 2 + [pltpu.SemaphoreType.DMA((2,))],
-        compiler_params=pltpu.CompilerParams(vmem_limit_bytes=32 * 2**20),
+        compiler_params=pltpu.CompilerParams(vmem_limit_bytes=24 * 2**20),
         cost_estimate=pl.CostEstimate(flops=4 * 10**9, bytes_accessed=6 * 10**6, transcendentals=2 * 10**6),
         name="cell",
     )(prior, inputs, gate_in, gate_state, *after)
 
 
-def update_kernel(asked_ref, fresh_ref, states_ref, *refs, cap):
+def update_kernel(asked_ref, joined_ref, states_ref, *refs, cap):
     out_ref, old_ref, new_ref, in_sems, out_sems = refs[-5:]
-    n, rows = fresh_ref.shape[0], states_ref.shape[0]
+    n, rows = joined_ref.shape[0], states_ref.shape[0]
     chunks = rows // CHUNK
     parts = [pl.ds(k * CHUNK, CHUNK) for k in range(chunks)]
     reads = [pltpu.make_async_copy(states_ref.at[p], old_ref.at[p], in_sems.at[k]) for k, p in enumerate(parts)]
@@ -207,13 +215,14 @@
     for read in reads:
         read.start()
     local = slot_row(asked_ref[...], n, cap)
-    fresh = fresh_ref[...]
-    ones = jnp.ones((n, LANES), BF16)
+    fresh = joined_ref[:, : states_ref.shape[1]]
+    within = onehot(iota((CHUNK, n), 0) == (local & (CHUNK - 1)))
+    counts = dot(within, onehot(iota((chunks, n), 0) * CHUNK == local - (local & (CHUNK - 1))), 1, 1)
     for k in range(chunks):
         at = slice(k * CHUNK, (k + 1) * CHUNK)
         pick = onehot(iota((CHUNK, n), 0) + k * CHUNK == local)
         total = dot(pick, fresh)
-        count = dot(pick, ones)[:, :1]
+        count = counts[:, k : k + 1]
         reads[k].wait()
         old = old_ref[at, :]
         change = total / jnp.maximum(count, 1.0) - old.astype(BF16).astype(F32)
@@ -223,7 +232,7 @@
         write.wait()
 
 
-def update(asked, fresh, states, cap, after=()):
+def update(asked, joined, states, cap, after=()):
     chunks = states.shape[0] // CHUNK
     return pl.pallas_call(
         functools.partial(update_kernel, cap=cap),
@@ -231,10 +240,10 @@
         in_specs=[VMEM, VMEM, HBM] + [ANY] * len(after),
         out_specs=HBM,
         scratch_shapes=[pltpu.VMEM(states.shape, F32)] * 2 + [pltpu.SemaphoreType.DMA((chunks,))] * 2,
-        compiler_params=pltpu.CompilerParams(vmem_limit_bytes=32 * 2**20),
+        compiler_params=pltpu.CompilerParams(vmem_limit_bytes=57 * 2**20),
         cost_estimate=pl.CostEstimate(flops=4 * 10**9, bytes_accessed=10**7, transcendentals=0),
         name="update",
-    )(asked, fresh, states, *after)
+    )(asked, joined, states, *after)
 
 
 def gelu(x):
@@ -253,14 +262,14 @@
 def step_kernel(*refs, n_in, n_out, n_after, ins, outs, backs, rows, depth, cap, first, last):
     it = iter(refs)
     take = lambda k: [next(it) for _ in range(k)]
-    fresh, inputs = take(2), take(2)
+    sides = take(2)
     before = None if first else next(it)
     in_refs, out_refs = take(n_in), take(n_out)
     take(n_after)
     line_ref, win_ref, wout_ref = take(3)
     groups, width, both = win_ref.shape
     half = both // 2
-    chunk = fresh[0].shape[0]
+    chunk = sides[0].shape[0]
 
     @pl.when(pl.program_id(0) == 0)
     def _():
@@ -283,13 +292,12 @@
     near = chunk // cap
     at = pl.ds(pl.multiple_of(pl.program_id(0) * near, near), near)
     for side in range(2):
-        x, f = inputs[side][...], fresh[side][...]
-        joined = jnp.concatenate([f, x], axis=1)
+        joined = sides[side][...]
         tower = jnp.zeros((chunk, half), F32)
         for g in range(groups):
             h = gelu(dot(joined, win_ref[g], 1, 1)).astype(BF16)
             tower = tower + dot(h, wout_ref[g], 1, 1)
-        score = jnp.sum(tower * x.astype(F32), axis=1, keepdims=True)
+        score = jnp.sum(tower * joined[:, half:].astype(F32), axis=1, keepdims=True)
         place = (iota((chunk, cap), 0) & (cap - 1)) == iota((chunk, cap), 1)
         source = onehot(iota((near, chunk), 1) // cap == iota((near, chunk), 0))
         lines = sum(dot(source, p) for p in split3(jnp.where(place, score, 0.0)))
@@ -301,14 +309,14 @@
         line_ref[at, lanes] = lines
 
 
-def step(fresh, inputs, before, ins, outs, backs, rows, depth, cap, last, after=()):
-    n, half = fresh[0].shape
+def step(sides, before, ins, outs, backs, rows, depth, cap, last, after=()):
+    n, half = sides[0].shape[0], sides[0].shape[1] // 2
     shards = n // cap
     chunk = min(n, 2 * CHUNK)
     in_parts = [(group, i, count, flip, place) for i, (group, _, count, flip, place) in enumerate(ins)]
     out_parts = [(i, start, flip, back) for i, (_, parts) in enumerate(outs) for start, flip, back in parts]
     width = sum(count for group, _, count, _, _ in ins if group == 0)
-    side = pl.BlockSpec((chunk, half), lambda i: (i, 0))
+    side = pl.BlockSpec((chunk, 2 * half), lambda i: (i, 0))
     line = pl.BlockSpec((shards, 2 * cap), lambda i: (0, 0))
     whole = lambda a: pl.BlockSpec(a.shape, lambda i: (0, 0))
     units = len(backs) * width
@@ -330,16 +338,16 @@
         ),
         grid=(n // chunk,),
         out_shape=jax.ShapeDtypeStruct((shards, 2 * cap), F32),
-        in_specs=[side] * 4
+        in_specs=[side] * 2
         + ([] if before is None else [line])
         + [whole(a) for a in in_arrays + out_arrays]
         + [ANY] * len(after),
         out_specs=line,
         scratch_shapes=[pltpu.VMEM((len(backs), width, 2 * half), BF16), pltpu.VMEM((len(backs), half, width), BF16)],
-        compiler_params=pltpu.CompilerParams(vmem_limit_bytes=44 * 2**20),
+        compiler_params=pltpu.CompilerParams(vmem_limit_bytes=40 * 2**20),
         cost_estimate=pl.CostEstimate(flops=12 * n * units * half, bytes_accessed=10**7, transcendentals=2 * n * units),
         name="tower",
-    )(*fresh, *inputs, *([] if before is None else [before]), *in_arrays, *out_arrays, *after)
+    )(*sides, *([] if before is None else [before]), *in_arrays, *out_arrays, *after)
 
 
 def pick_kernel(back_ref, slot_ref, out_ref, *, cap):
@@ -363,6 +371,7 @@
         out_shape=jax.ShapeDtypeStruct((1, slots.shape[1]), F32),
         in_specs=[VMEM] * 2,
         out_specs=VMEM,
+        compiler_params=pltpu.CompilerParams(vmem_limit_bytes=8 * 2**20),
         cost_estimate=pl.CostEstimate(flops=10**8, bytes_accessed=10**5, transcendentals=0),
         name="pick",
     )(back, slots)
@@ -382,7 +391,7 @@
     return jnp.concatenate([jnp.where(even, mine, got), jnp.where(even, got, mine)], axis=axis)
 
 
-def tower_gathered(fresh, inputs, tower_in, tower_out, devices, cap):
+def tower_gathered(sides, tower_in, tower_out, devices, cap):
     same_core = [list(range(0, devices, 2)), list(range(1, devices, 2))]
     rows = tower_out.shape[0]
     cols = tower_out.reshape(rows, devices // 2, 2, -1)
@@ -391,7 +400,7 @@
     half = by_core(jnp.where(even, cols[0], cols[1]), jnp.where(even, cols[1], cols[0]), devices, 0)
     win, wout = [lax.all_gather(w, AXES, axis_index_groups=same_core, tiled=True) for w in (tower_in, half)]
     ins = [(0, win, win.shape[0], None, 0)]
-    return step(fresh, inputs, None, ins, [(wout, [])], [0], (0, 0), 1, cap, True)
+    return step(sides, None, ins, [(wout, [])], [0], (0, 0), 1, cap, True)
 
 
 def per_device(
@@ -414,26 +423,48 @@
     requests, slots, *cut = route(
         row_of_user, event_users, event_features, tower_out, shards, cap, states.shape[0], chips
     )
-    sent = send_tower(tower_in, *cut, shards) if by_steps else None
-    due = sent[2] if by_steps else [()] * 4
-    asked = exchange(requests)
-    prior = fetch(asked, states, cap, 0, after=due[0])
-    inputs = fetch(asked, feature_table, cap, 1, after=(*due[1], prior))
-    fresh = cell(prior, inputs, gate_in, gate_state, after=due[2])
-    new_states = update(asked, fresh, states, cap, after=due[3])
-    both = [[x, send(x, shards, lambda d: d ^ 1)] for x in (fresh, inputs)]
+    tables = (states, feature_table, gate_in, gate_state)
     if by_steps:
-        parts = tower_by_steps(*both, sent, tower_in.shape[0], 2 * tower_out.shape[0], cap, new_states)
+        asked, joined, parts = by_waves(requests, cut, tables, tower_in, shards, cap)
     else:
-        parts = tower_gathered(*both, tower_in, tower_out, shards, cap)
+        asked = exchange(requests)
+        prior, inputs = fetch(asked, states, cap, 0), fetch(asked, feature_table, cap, 1)
+        joined = cell(prior, inputs, gate_in, gate_state)
+        sides = [joined, send(joined, shards, lambda d: d ^ 1)]
+        parts = tower_gathered(sides, tower_in, tower_out, shards, cap)
     back = exchange(parts)
+    new_states = update(asked, joined, states, cap)
     scores = pick(back, slots, cap).reshape(events)
     return (new_states, scores)
 
 
-def send_tower(tower_in, mine, theirs, devices):
-    def ahead(x):
-        return send(x, devices, lambda d: (d & ~6) | ((d + 2) & 6))
+def place_kernel(*refs, n, parts):
+    sources, outs = refs[:n], refs[-len(parts) :]
+    for out, pieces in zip(outs, parts, strict=True):
+        to = 0
+        for index, start, rows in pieces:
+            out[to : to + rows, :] = sources[index][start : start + rows, :]
+            to += rows
+
+
+def place(arrays, parts, after=()):
+    cols = arrays[0].shape[1]
+    return pl.pallas_call(
+        functools.partial(place_kernel, n=len(arrays), parts=parts),
+        out_shape=[jax.ShapeDtypeStruct((sum(p[2] for p in ps), cols), arrays[0].dtype) for ps in parts],
+        in_specs=[VMEM] * len(arrays) + [ANY] * len(after),
+        out_specs=[VMEM] * len(parts),
+        compiler_params=pltpu.CompilerParams(vmem_limit_bytes=8 * 2**20),
+        cost_estimate=pl.CostEstimate(flops=0, bytes_accessed=10**6, transcendentals=0),
+        name="place",
+    )(*arrays, *after)
+
+
+def by_waves(requests, parts, tables, tower_in, devices, cap):
+    states, feature_table, gate_in, gate_state = tables
+
+    def ahead(x, places=1):
+        return send(x, devices, lambda d: (d & ~6) | ((d + 2 * places) & 6))
 
     def along_x(x):
         return send(x, devices, lambda d: d ^ 8)
@@ -441,49 +472,55 @@
     def along_y(x):
         return send(x, devices, lambda d: d ^ 16)
 
-    def plane(x):
-        ax, ay = along_x(x), along_y(x)
-        half = x.shape[0] // 2
-        return x, ax, ay, along_x(ay[:half]), along_y(ax[half:])
-
+    def corner(ax, ay, after=()):
+        half = ax.shape[0] // 2
+        top, bottom = place([ay, ax], [[(0, 0, half)], [(1, half, half)]], after)
+        return along_x(top), along_y(bottom)
+
+    mine, theirs = [p.reshape(2, p.shape[0] // 2, p.shape[1]) for p in parts]
+    rows = by_core(mine, theirs, devices, 1).reshape(-1, mine.shape[2])
     line = [tower_in]
     for _ in range(3):
         line.append(ahead(line[-1]))
-    ins = [plane(x) for x in line]
-    parts = (2, mine.shape[0] // 2, mine.shape[1])
-    rows = [by_core(mine.reshape(parts), theirs.reshape(parts), devices, 1).reshape(-1, mine.shape[1])]
-    for _ in range(3):
-        rows.append(ahead(rows[-1]))
-    outs = plane(jnp.concatenate(rows, axis=0))
-    due = [
-        (*ins[0][1:3], line[1], rows[1]),
-        (*ins[0][3:], *ins[1][1:3], line[2], rows[2]),
-        (*ins[1][3:], line[3], rows[3]),
-        outs[1:3],
-    ]
-    return ins, outs, due
-
-
-def tower_by_steps(fresh, inputs, sent, rows_in, rows_out, cap, done):
+    ax, ay = [along_x(x) for x in line[:3]], [along_y(x) for x in line[:3]]
+    asked = exchange(requests)
+    n_rows = rows.shape[0]
+    line_rows = [rows] + [ahead(rows, k) for k in (1, 2, 3)]
+    (all_rows,) = place(line_rows, [[(k, 0, n_rows) for k in range(4)]])
+    d = [corner(ax[0], ay[0])]
+    rx, ry = along_x(all_rows), along_y(all_rows)
+    due = [(), (ax[0], ay[0], line[1]), (rx, ry, ax[1], ay[1], line[2], *d[0])]
+    prior = fetch(asked, states, cap, 0, after=due[0])
+    inputs = fetch(asked, feature_table, cap, 1, after=(*due[1], prior))
+    joined = cell(prior, inputs, gate_in, gate_state, after=due[2])
+    d.append(corner(ax[1], ay[1], (joined,)))
+    outs = (all_rows, rx, ry, *corner(rx, ry))
+    sides = [joined, send(joined, devices, lambda d: d ^ 1)]
+    score = None
+    for k in range(4):
+        plane = (line[k], ax[k], ay[k], *d[k])
+        score = tower_step(sides, score, [plane], outs, k, tower_in.shape[0], n_rows // 2, cap)
+        if k == 0:
+            (late,) = place([line[3]], [[(0, 0, line[3].shape[0])]], (score,))
+            ax.append(along_x(late))
+            ay.append(along_y(late))
+        if k < 2:
+            d.append(corner(ax[k + 2], ay[k + 2], (score,)))
+    return asked, joined, score
+
+
+def tower_step(sides, score, planes, outs, first, rows_in, rows_out, cap, after=()):
     depth = 4
-    planes, outs, _ = sent
-    half = rows_in // 2
-
-    def ins_of(back, group):
-        line, ax, ay, top, bottom = planes[back]
-        whole = [(group, a, rows_in, flip, 0) for flip, a in enumerate((line, ax, ay))]
-        return whole + [(group, top, half, 3, 0), (group, bottom, half, 3, half)]
-
-    block = 2 * rows_out
+    half, block = rows_in // 2, 2 * rows_out
+    ins = []
+    for group, (here, ax, ay, top, bottom) in enumerate(planes):
+        ins += [(group, a, rows_in, flip, 0) for flip, a in enumerate((here, ax, ay))]
+        ins += [(group, top, half, 3, 0), (group, bottom, half, 3, half)]
     out_parts = [(a, [(back * block, flip, back) for back in range(depth)]) for flip, a in enumerate(outs[:3])]
     out_parts += [(a, [(k * block, 3, 2 * i + k) for k in range(2)]) for i, a in enumerate(outs[3:])]
-    score = None
-    for backs in ([0, 1], [2], [3]):
-        ins = [part for group, back in enumerate(backs) for part in ins_of(back, group)]
-        after = (done,) if score is None else ()
-        last = backs[-1] == depth - 1
-        score = step(fresh, inputs, score, ins, out_parts, backs, (rows_in, rows_out), depth, cap, last, after)
-    return score
+    backs = list(range(first, first + len(planes)))
+    last = backs[-1] == depth - 1
+    return step(sides, score, ins, out_parts, backs, (rows_in, rows_out), depth, cap, last, after)
 
 
 def solution(mesh):

time: 129 us -> 108 us (0.84)
  waiting for transfers between devices: 36.4 us -> 12.7 us
  starting transfers between devices: 34.4 us -> 46.5 us
  blocking collectives: 9.34 us -> 0 us
  local copies, waits for them, and re-layouts: 6.13 us -> 2.25 us
  Pallas kernels: 41.9 us -> 44.4 us
    ppermute x29 -> x28, waiting for transfers between devices: 32.7 us -> 12.7 us  [send(): return lax.ppermute(x, AXES, [(d, to(d)) for d in range(devices)])]
    all_to_all x1 -> x0, blocking collectives: 9.34 us -> none  [exchange(): return lax.all_to_all(x, AXES, split_axis=0, concat_axis=0, tiled=True)]
    ppermute x29 -> x28, starting transfers between devices: 30.9 us -> 39.1 us  [send(): return lax.ppermute(x, AXES, [(d, to(d)) for d in range(devices)])]
    all_to_all x1 -> x2, starting transfers between devices: 3.46 us -> 7.47 us  [exchange(): return lax.all_to_all(x, AXES, split_axis=0, concat_axis=0, tiled=True)]
    unnamed x22 -> x16, local copies, waits for them, and re-layouts: 6.01 us -> 2.25 us
    all_to_all x1 -> x2, waiting for transfers between devices: 3.66 us -> 0.01 us  [exchange(): return lax.all_to_all(x, AXES, split_axis=0, concat_axis=0, tiled=True)]
    pallas_call x3 -> x4, Pallas kernels: 19.7 us -> 21.5 us  [step(): pl.pallas_call(functools.partial(step_kernel, n_in=len(in_arrays), n_out=...]
    pallas_call x1 -> x8, Pallas kernels: 3.96 us -> 4.24 us  [the longest x1 4.04 us: cell(): pl.pallas_call(cell_kernel, out_shape=jax.ShapeDtypeStruct((n, 2 * width)...]
  transfers between devices with their start and end apart: 30 -> 30, of which waited for: 6 -> 3; matrix products, arithmetic and copies ran while one was open for 0% -> 1% of each run, Pallas kernels for 26% -> 29%
where the time goes in v2:
time: 108 us
  starting transfers between devices  46.5 us (43%)
  Pallas kernels  44.4 us (41%)
  waiting for transfers between devices  12.7 us (12%)
  local copies, waits for them, and re-layouts  2.25 us (2%)
    ppermute x28, starting transfers between devices, send(): return lax.ppermute(x, AXES, [(d, to(d)) for d in range(devices)])  39.1 us
    pallas_call x4, Pallas kernels, step(): pl.pallas_call(functools.partial(step_kernel, n_in=len(in_arrays), n_out=...  21.5 us
    ppermute x28, waiting for transfers between devices, send(): return lax.ppermute(x, AXES, [(d, to(d)) for d in range(devices)])  12.7 us
    pallas_call x2, Pallas kernels, fetch(): pl.pallas_call(functools.partial(fetch_kernel, cap=cap, column=column), o...  8.22 us
    all_to_all x2, starting transfers between devices, exchange(): return lax.all_to_all(x, AXES, split_axis=0, concat_axis=0, tiled=True)  7.47 us
    pallas_call x1, Pallas kernels, update(): pl.pallas_call(functools.partial(update_kernel, cap=cap), out_shape=jax.S...  6.92 us
    pallas_call x1, Pallas kernels, cell(): pl.pallas_call(cell_kernel, out_shape=jax.ShapeDtypeStruct((n, 2 * width)...  4.04 us
    pallas_call x1, Pallas kernels, route(): pl.pallas_call(functools.partial(route_kernel, shards=shards, cap=cap, ro...  2.69 us
  transfers between devices with their start and end apart: 30, of which 3 were waited for; matrix products, arithmetic and copies ran while one was open for 1% of the time, Pallas kernels for 29%

profile of v2, /device:TPU:0, one launch (start us, length us, event | category | flops | bytes accessed | tf_op | source)
XLA Modules:
  0.0 107.6 jit_solution(16910436408193352388)
XLA Ops:
  0.6 2.7 %route.1 = (s32[32,64]{1,0:T(8,128)}, s32[2,512]{1,0:T(2,128)}, bf16[32,1024]{1,0:T(8,128)(2,1)}, bf16[32,1024]{1,0:T(8,128)(2,1)}) custom-call(s32[512,128]{1,0:T(8,128)} %bitcast.25, s32[1,512]{1,0:T(1,128)} %bitcast.27, s32[1,512]{1,0:T(1,128)} %bitcast.28, bf16[16,4096]{1,0:T(8,128)(2,1)} %refs_3_.1), custom_call_target="tpu_custom_call" | custom-call | flops 1000000000 | bytes 1000000 | tf_op jit(solution)/shard_map/route/pallas_call | solution.py:106
  3.9 2.6 %collective-permute-start = (bf16[128,1024]{1,0:T(8,128)(2,1)S(1)}, bf16[128,1024]{1,0:T(8,128)(2,1)S(1)}, u32[]{:S(2)}, u32[]{:S(2)}) collective-permute-start(bf16[128,1024]{1,0:T(8,128)(2,1)S(1)} %copy-done.6), channel_id=1, source_target_pairs={{0,8},{1,9},{2,10},{3,11},{4,12},{5,13},{6,14},{7,15},{8,0},{9,1},... | collective-permute-start | bytes 786440 | tf_op jit(solution)/shard_map/ppermute | solution.py:385
  6.4 1.5 %collective-permute-start.1 = (bf16[128,1024]{1,0:T(8,128)(2,1)S(1)}, bf16[128,1024]{1,0:T(8,128)(2,1)S(1)}, u32[]{:S(2)}, u32[]{:S(2)}) collective-permute-start(bf16[128,1024]{1,0:T(8,128)(2,1)S(1)} %copy-done.6), channel_id=1, source_target_pairs={{0,16},{1,17},{2,18},{3,19},{4,20},{5,21},{6,22},{7,23},{8,24},{9,... | collective-permute-start | bytes 786440 | tf_op jit(solution)/shard_map/ppermute | solution.py:385
  8.8 1.6 %collective-permute-start.4 = (bf16[64,1024]{1,0:T(8,128)(2,1)S(1)}, bf16[64,1024]{1,0:T(8,128)(2,1)S(1)}, u32[]{:S(2)}, u32[]{:S(2)}) collective-permute-start(bf16[64,1024]{1,0:T(8,128)(2,1)S(1)} %bitcast.15), channel_id=1, source_target_pairs={{0,2},{1,3},{2,4},{3,5},{4,6},{5,7},{6,0},{7,1},{8,10},{9,11},{10,... | collective-permute-start | bytes 393224 | tf_op jit(solution)/shard_map/ppermute | solution.py:385
  10.5 3.2 %all-to-all-start = ((s32[32,1,64]{2,1,0:T(1,128)}), s32[32,1,64]{2,1,0:T(1,128)S(1)}, u32[]{:S(2)}, u32[]{:S(2)}) async-start(s32[32,1,64]{2,1,0:T(1,128)} %bitcast.24), calls=%async_computation | async-start | bytes 32768 | tf_op jit(solution)/shard_map/all_to_all | solution.py:381
  13.7 1.8 %collective-permute-start.2 = (bf16[128,1024]{1,0:T(8,128)(2,1)S(1)}, bf16[128,1024]{1,0:T(8,128)(2,1)S(1)}, u32[]{:S(2)}, u32[]{:S(2)}) collective-permute-start(bf16[128,1024]{1,0:T(8,128)(2,1)S(1)} %copy-done.6), channel_id=1, source_target_pairs={{0,2},{1,3},{2,4},{3,5},{4,6},{5,7},{6,0},{7,1},{8,10},{9,11},{10,... | collective-permute-start | bytes 786440 | tf_op jit(solution)/shard_map/ppermute | solution.py:385
  15.5 2.4 %collective-permute-start.5 = (bf16[64,1024]{1,0:T(8,128)(2,1)S(1)}, bf16[64,1024]{1,0:T(8,128)(2,1)S(1)}, u32[]{:S(2)}, u32[]{:S(2)}) collective-permute-start(bf16[64,1024]{1,0:T(8,128)(2,1)S(1)} %bitcast.16), channel_id=1, source_target_pairs={{0,4},{1,5},{2,6},{3,7},{4,0},{5,1},{6,2},{7,3},{8,12},{9,13},{10,... | collective-permute-start | bytes 393224 | tf_op jit(solution)/shard_map/ppermute | solution.py:385
  17.9 1.4 %collective-permute-start.6 = (bf16[64,1024]{1,0:T(8,128)(2,1)S(1)}, bf16[64,1024]{1,0:T(8,128)(2,1)S(1)}, u32[]{:S(2)}, u32[]{:S(2)}) collective-permute-start(bf16[64,1024]{1,0:T(8,128)(2,1)S(1)} %bitcast.17), channel_id=1, source_target_pairs={{0,6},{1,7},{2,0},{3,1},{4,2},{5,3},{6,4},{7,5},{8,14},{9,15},{10,... | collective-permute-start | bytes 393224 | tf_op jit(solution)/shard_map/ppermute | solution.py:385
  19.4 1.5 %collective-permute-start.12 = (bf16[64,1024]{1,0:T(8,128)(2,1)S(1)}, bf16[64,1024]{1,0:T(8,128)(2,1)S(1)}, u32[]{:S(2)}, u32[]{:S(2)}) collective-permute-start(bf16[64,1024]{1,0:T(8,128)(2,1)S(1)} %get-tuple-element.19), channel_id=1, source_target_pairs={{0,8},{1,9},{2,10},{3,11},{4,12},{5,13},{6,14},{7,15},{8,0},{9,1},... | collective-permute-start | bytes 393224 | tf_op jit(solution)/shard_map/ppermute | solution.py:385
  20.9 1.5 %collective-permute-start.13 = (bf16[64,1024]{1,0:T(8,128)(2,1)S(1)}, bf16[64,1024]{1,0:T(8,128)(2,1)S(1)}, u32[]{:S(2)}, u32[]{:S(2)}) collective-permute-start(bf16[64,1024]{1,0:T(8,128)(2,1)S(1)} %get-tuple-element.20), channel_id=1, source_target_pairs={{0,16},{1,17},{2,18},{3,19},{4,20},{5,21},{6,22},{7,23},{8,24},{9,... | collective-permute-start | bytes 393224 | tf_op jit(solution)/shard_map/ppermute | solution.py:385
  22.4 2.2 %copy-done.3 = f32[2048,512]{1,0:T(8,128)S(1)} copy-done((f32[2048,512]{1,0:T(8,128)S(1)}, f32[2048,512]{1,0:T(8,128)}, u32[]{:S(2)}) %copy-start.3) | copy-done | bytes 4194328
  24.6 3.0 %fetch.2.refs_3_.prior_ref = bf16[1024,512]{1,0:T(8,128)(2,1)S(1)} custom-call(s32[32,64]{1,0:T(8,128)S(1)} %bitcast.19, f32[2048,512]{1,0:T(8,128)S(1)} %copy-done.3), custom_call_target="tpu_custom_call" | custom-call | flops 10737418240 | bytes 5000000 | tf_op jit(solution)/shard_map/fetch/pallas_call | solution.py:161
  27.6 2.4 %collective-permute-done.5.refs_2_ = bf16[64,1024]{1,0:T(8,128)(2,1)S(1)} collective-permute-done((bf16[64,1024]{1,0:T(8,128)(2,1)S(1)}, bf16[64,1024]{1,0:T(8,128)(2,1)S(1)}, u32[]{:S(2)}, u32[]{:S(2)}) %collective-permute-start.5) | collective-permute-done | bytes 131104 | tf_op jit(solution)/shard_map/ppermute | solution.py:385
  30.0 1.6 %collective-permute-start.7 = (bf16[256,1024]{1,0:T(8,128)(2,1)S(1)}, bf16[256,1024]{1,0:T(8,128)(2,1)S(1)}, u32[]{:S(2)}, u32[]{:S(2)}) collective-permute-start(bf16[256,1024]{1,0:T(8,128)(2,1)S(1)} %place.7.refs_7_.refs_8_), channel_id=1, source_target_pairs={{0,8},{1,9},{2,10},{3,11},{4,12},{5,13},{6,14},{7,15},{8,0},{9,1},... | collective-permute-start | bytes 1572872 | tf_op jit(solution)/shard_map/ppermute | solution.py:385
  31.6 1.5 %collective-permute-start.8 = (bf16[256,1024]{1,0:T(8,128)(2,1)S(1)}, bf16[256,1024]{1,0:T(8,128)(2,1)S(1)}, u32[]{:S(2)}, u32[]{:S(2)}) collective-permute-start(bf16[256,1024]{1,0:T(8,128)(2,1)S(1)} %place.7.refs_7_.refs_8_), channel_id=1, source_target_pairs={{0,16},{1,17},{2,18},{3,19},{4,20},{5,21},{6,22},{7,23},{8,24},{9,... | collective-permute-start | bytes 1572872 | tf_op jit(solution)/shard_map/ppermute | solution.py:385
  33.1 3.3 %collective-permute-start.11 = (bf16[128,1024]{1,0:T(8,128)(2,1)S(1)}, bf16[128,1024]{1,0:T(8,128)(2,1)S(1)}, u32[]{:S(2)}, u32[]{:S(2)}) collective-permute-start(bf16[128,1024]{1,0:T(8,128)(2,1)S(1)} %collective-permute-done.2.refs_2_.refs_3_), channel_id=1, source_target_pairs={{0,2},{1,3},{2,4},{3,5},{4,6},{5,7},{6,0},{7,1},{8,10},{9,11},{10,... | collective-permute-start | bytes 786440 | tf_op jit(solution)/shard_map/ppermute | solution.py:385
  37.4 5.2 %fetch.3.inputs_ref = bf16[1024,512]{1,0:T(8,128)(2,1)S(1)} custom-call(s32[32,64]{1,0:T(8,128)S(1)} %bitcast.20, bf16[4096,512]{1,0:T(8,128)(2,1)S(1)} %copy-done.2, bf16[128,1024]{1,0:T(8,128)(2,1)S(1)} %collective-permute-done.refs_0_.refs_1_.refs_3_, bf16[128,1024]{1,0:T(8,128)(2,1)S(1)} %collective-permute-done.1.refs_1_.refs_0_.refs_4_, ...), custom_call_target="tpu_custom_call" | custom-call | flops 21474836480 | bytes 5000000 | tf_op jit(solution)/shard_map/fetch/pallas_call | solution.py:161
  42.7 8.0 %collective-permute-done.10.refs_3_.refs_0_.refs_5_ = bf16[128,1024]{1,0:T(8,128)(2,1)S(1)} collective-permute-done((bf16[128,1024]{1,0:T(8,128)(2,1)S(1)}, bf16[128,1024]{1,0:T(8,128)(2,1)S(1)}, u32[]{:S(2)}, u32[]{:S(2)}) %collective-permute-start.10) | collective-permute-done | bytes 262176 | tf_op jit(solution)/shard_map/ppermute | solution.py:385
  50.7 4.0 %cell.1.joined_ref.refs_0_.refs_2_ = bf16[1024,1024]{1,0:T(8,128)(2,1)S(1)} custom-call(bf16[1024,512]{1,0:T(8,128)(2,1)S(1)} %fetch.2.refs_3_.prior_ref, bf16[1024,512]{1,0:T(8,128)(2,1)S(1)} %fetch.3.inputs_ref, bf16[512,1536]{1,0:T(8,128)(2,1)S(1)} %copy-done.4, bf16[512,1536]{1,0:T(8,128)(2,1)S(1)} %copy-done.5, ...), custom_call_target="tpu_custom_call" | custom-call | flops 4000000000 | bytes 6000000 | tf_op jit(solution)/shard_map/cell/pallas_call | solution.py:196
  55.5 1.5 %collective-permute-start.16 = (bf16[128,1024]{1,0:T(8,128)(2,1)S(1)}, bf16[128,1024]{1,0:T(8,128)(2,1)S(1)}, u32[]{:S(2)}, u32[]{:S(2)}) collective-permute-start(bf16[128,1024]{1,0:T(8,128)(2,1)S(1)} %get-tuple-element.22), channel_id=1, source_target_pairs={{0,16},{1,17},{2,18},{3,19},{4,20},{5,21},{6,22},{7,23},{8,24},{9,... | collective-permute-start | bytes 786440 | tf_op jit(solution)/shard_map/ppermute | solution.py:385
  57.0 3.4 %collective-permute-start.23 = (bf16[128,1024]{1,0:T(8,128)(2,1)S(1)}, bf16[128,1024]{1,0:T(8,128)(2,1)S(1)}, u32[]{:S(2)}, u32[]{:S(2)}) collective-permute-start(bf16[128,1024]{1,0:T(8,128)(2,1)S(1)} %collective-permute-done.11.refs_4_.refs_3_), channel_id=1, source_target_pairs={{0,2},{1,3},{2,4},{3,5},{4,6},{5,7},{6,0},{7,1},{8,10},{9,11},{10,... | collective-permute-start | bytes 786440 | tf_op jit(solution)/shard_map/ppermute | solution.py:385
  60.4 1.5 %collective-permute-start.19 = (bf16[128,1024]{1,0:T(8,128)(2,1)S(1)}, bf16[128,1024]{1,0:T(8,128)(2,1)S(1)}, u32[]{:S(2)}, u32[]{:S(2)}) collective-permute-start(bf16[128,1024]{1,0:T(8,128)(2,1)S(1)} %collective-permute-done.11.refs_4_.refs_3_), channel_id=1, source_target_pairs={{0,8},{1,9},{2,10},{3,11},{4,12},{5,13},{6,14},{7,15},{8,0},{9,1},... | collective-permute-start | bytes 786440 | tf_op jit(solution)/shard_map/ppermute | solution.py:385
  61.9 2.2 %collective-permute-done.15.refs_10_.refs_11_ = bf16[128,1024]{1,0:T(8,128)(2,1)S(1)} collective-permute-done((bf16[128,1024]{1,0:T(8,128)(2,1)S(1)}, bf16[128,1024]{1,0:T(8,128)(2,1)S(1)}, u32[]{:S(2)}, u32[]{:S(2)}) %collective-permute-start.15) | collective-permute-done | bytes 262176 | tf_op jit(solution)/shard_map/ppermute | solution.py:385
  64.1 1.5 %collective-permute-start.20 = (bf16[128,1024]{1,0:T(8,128)(2,1)S(1)}, bf16[128,1024]{1,0:T(8,128)(2,1)S(1)}, u32[]{:S(2)}, u32[]{:S(2)}) collective-permute-start(bf16[128,1024]{1,0:T(8,128)(2,1)S(1)} %collective-permute-done.11.refs_4_.refs_3_), channel_id=1, source_target_pairs={{0,16},{1,17},{2,18},{3,19},{4,20},{5,21},{6,22},{7,23},{8,24},{9,... | collective-permute-start | bytes 786440 | tf_op jit(solution)/shard_map/ppermute | solution.py:385
  66.9 5.2 %tower.4.refs_2_.refs_1_ = f32[32,64]{1,0:T(8,128)S(1)} custom-call(bf16[1024,1024]{1,0:T(8,128)(2,1)S(1)} %cell.1.joined_ref.refs_0_.refs_2_, bf16[1024,1024]{1,0:T(8,128)(2,1)S(1)} %collective-permute-done.14.refs_1_, bf16[128,1024]{1,0:T(8,128)(2,1)S(1)} %copy-done.6, bf16[128,1024]{1,0:T(8,128)(2,1)S(1)} %collective-permute-done.refs_0_.refs_1_.refs_3_, ...), custom_call_target="tpu_custom_call" | custom-call | flops 3221225472 | bytes 10000000 | tf_op jit(solution)/shard_map/tower/pallas_call | solution.py:324
  73.5 1.5 %collective-permute-start.25 = (bf16[128,1024]{1,0:T(8,128)(2,1)S(1)}, bf16[128,1024]{1,0:T(8,128)(2,1)S(1)}, u32[]{:S(2)}, u32[]{:S(2)}) collective-permute-start(bf16[128,1024]{1,0:T(8,128)(2,1)S(1)} %place.12), channel_id=1, source_target_pairs={{0,16},{1,17},{2,18},{3,19},{4,20},{5,21},{6,22},{7,23},{8,24},{9,... | collective-permute-start | bytes 786440 | tf_op jit(solution)/shard_map/ppermute | solution.py:385
  76.4 5.2 %tower.5.refs_2_ = f32[32,64]{1,0:T(8,128)S(1)} custom-call(bf16[1024,1024]{1,0:T(8,128)(2,1)S(1)} %cell.1.joined_ref.refs_0_.refs_2_, bf16[1024,1024]{1,0:T(8,128)(2,1)S(1)} %collective-permute-done.14.refs_1_, f32[32,64]{1,0:T(8,128)S(1)} %tower.4.refs_2_.refs_1_, bf16[128,1024]{1,0:T(8,128)(2,1)S(1)} %collective-permute-done.2.refs_2_.refs_3_, ...), custom_call_target="tpu_custom_call" | custom-call | flops 3221225472 | bytes 10000000 | tf_op jit(solution)/shard_map/tower/pallas_call | solution.py:324
  83.0 1.5 %collective-permute-start.27 = (bf16[64,1024]{1,0:T(8,128)(2,1)S(1)}, bf16[64,1024]{1,0:T(8,128)(2,1)S(1)}, u32[]{:S(2)}, u32[]{:S(2)}) collective-permute-start(bf16[64,1024]{1,0:T(8,128)(2,1)S(1)} %get-tuple-element.28), channel_id=1, source_target_pairs={{0,16},{1,17},{2,18},{3,19},{4,20},{5,21},{6,22},{7,23},{8,24},{9,... | collective-permute-start | bytes 393224 | tf_op jit(solution)/shard_map/ppermute | solution.py:385
  84.4 5.2 %tower.6.refs_2_ = f32[32,64]{1,0:T(8,128)S(1)} custom-call(bf16[1024,1024]{1,0:T(8,128)(2,1)S(1)} %cell.1.joined_ref.refs_0_.refs_2_, bf16[1024,1024]{1,0:T(8,128)(2,1)S(1)} %collective-permute-done.14.refs_1_, f32[32,64]{1,0:T(8,128)S(1)} %tower.5.refs_2_, bf16[128,1024]{1,0:T(8,128)(2,1)S(1)} %collective-permute-done.11.refs_4_.refs_3_, ...), custom_call_target="tpu_custom_call" | custom-call | flops 3221225472 | bytes 10000000 | tf_op jit(solution)/shard_map/tower/pallas_call | solution.py:324
  89.7 5.9 %tower.7 = f32[32,64]{1,0:T(8,128)} custom-call(bf16[1024,1024]{1,0:T(8,128)(2,1)S(1)} %cell.1.joined_ref.refs_0_.refs_2_, bf16[1024,1024]{1,0:T(8,128)(2,1)S(1)} %collective-permute-done.14.refs_1_, f32[32,64]{1,0:T(8,128)S(1)} %tower.6.refs_2_, bf16[128,1024]{1,0:T(8,128)(2,1)S(1)} %collective-permute-done.23.refs_0_.refs_3_, ...), custom_call_target="tpu_custom_call" | custom-call | flops 3221225472 | bytes 10000000 | tf_op jit(solution)/shard_map/tower/pallas_call | solution.py:324
  95.6 4.3 %all-to-all-start.1 = ((f32[32,1,64]{2,1,0:T(1,128)}), f32[32,1,64]{2,1,0:T(1,128)S(1)}, u32[]{:S(2)}, u32[]{:S(2)}) async-start(f32[32,1,64]{2,1,0:T(1,128)} %bitcast.10), calls=%async_computation.1 | async-start | bytes 32768 | tf_op jit(solution)/shard_map/all_to_all | solution.py:381
  99.9 6.9 %update.1 = f32[2048,512]{1,0:T(8,128)} custom-call(s32[32,64]{1,0:T(8,128)} %bitcast.21, bf16[1024,1024]{1,0:T(8,128)(2,1)} %copy-done, f32[2048,512]{1,0:T(8,128)} %states_ref.1), custom_call_target="tpu_custom_call" | custom-call | flops 4000000000 | bytes 10000000 | tf_op jit(solution)/shard_map/update/pallas_call | solution.py:237
  (63 shorter events, 9.6 us)
Async XLA Ops:
  3.3 4.6 %collective-permute-start.3 = (bf16[2,16,1024]{2,1,0:T(8,128)(2,1)}, bf16[2,16,1024]{2,1,0:T(8,128)(2,1)S(1)}, u32[]{:S(2)}, u32[]{:S(2)}) collective-permute-start(bf16[2,16,1024]{2,1,0:T(8,128)(2,1)} %bitcast.26), channel_id=1, source_target_pairs={{0,1},{1,0},{2,3},{3,2},{4,5},{5,4},{6,7},{7,6},{8,9},{9,8},{10,11... | collective-permute-start | bytes 196616 | tf_op jit(solution)/shard_map/ppermute | solution.py:385
  3.9 14.0 %collective-permute-start = (bf16[128,1024]{1,0:T(8,128)(2,1)S(1)}, bf16[128,1024]{1,0:T(8,128)(2,1)S(1)}, u32[]{:S(2)}, u32[]{:S(2)}) collective-permute-start(bf16[128,1024]{1,0:T(8,128)(2,1)S(1)} %copy-done.6), channel_id=1, source_target_pairs={{0,8},{1,9},{2,10},{3,11},{4,12},{5,13},{6,14},{7,15},{8,0},{9,1},... | collective-permute-start | bytes 786440 | tf_op jit(solution)/shard_map/ppermute | solution.py:385
  6.4 12.9 %collective-permute-start.1 = (bf16[128,1024]{1,0:T(8,128)(2,1)S(1)}, bf16[128,1024]{1,0:T(8,128)(2,1)S(1)}, u32[]{:S(2)}, u32[]{:S(2)}) collective-permute-start(bf16[128,1024]{1,0:T(8,128)(2,1)S(1)} %copy-done.6), channel_id=1, source_target_pairs={{0,16},{1,17},{2,18},{3,19},{4,20},{5,21},{6,22},{7,23},{8,24},{9,... | collective-permute-start | bytes 786440 | tf_op jit(solution)/shard_map/ppermute | solution.py:385
  8.8 12.0 %collective-permute-start.4 = (bf16[64,1024]{1,0:T(8,128)(2,1)S(1)}, bf16[64,1024]{1,0:T(8,128)(2,1)S(1)}, u32[]{:S(2)}, u32[]{:S(2)}) collective-permute-start(bf16[64,1024]{1,0:T(8,128)(2,1)S(1)} %bitcast.15), channel_id=1, source_target_pairs={{0,2},{1,3},{2,4},{3,5},{4,6},{5,7},{6,0},{7,1},{8,10},{9,11},{10,... | collective-permute-start | bytes 393224 | tf_op jit(solution)/shard_map/ppermute | solution.py:385
  10.5 11.9 %all-to-all-start = ((s32[32,1,64]{2,1,0:T(1,128)}), s32[32,1,64]{2,1,0:T(1,128)S(1)}, u32[]{:S(2)}, u32[]{:S(2)}) async-start(s32[32,1,64]{2,1,0:T(1,128)} %bitcast.24), calls=%async_computation | async-start | bytes 32768 | tf_op jit(solution)/shard_map/all_to_all | solution.py:381
  13.7 19.4 %collective-permute-start.2 = (bf16[128,1024]{1,0:T(8,128)(2,1)S(1)}, bf16[128,1024]{1,0:T(8,128)(2,1)S(1)}, u32[]{:S(2)}, u32[]{:S(2)}) collective-permute-start(bf16[128,1024]{1,0:T(8,128)(2,1)S(1)} %copy-done.6), channel_id=1, source_target_pairs={{0,2},{1,3},{2,4},{3,5},{4,6},{5,7},{6,0},{7,1},{8,10},{9,11},{10,... | collective-permute-start | bytes 786440 | tf_op jit(solution)/shard_map/ppermute | solution.py:385
  15.5 14.5 %collective-permute-start.5 = (bf16[64,1024]{1,0:T(8,128)(2,1)S(1)}, bf16[64,1024]{1,0:T(8,128)(2,1)S(1)}, u32[]{:S(2)}, u32[]{:S(2)}) collective-permute-start(bf16[64,1024]{1,0:T(8,128)(2,1)S(1)} %bitcast.16), channel_id=1, source_target_pairs={{0,4},{1,5},{2,6},{3,7},{4,0},{5,1},{6,2},{7,3},{8,12},{9,13},{10,... | collective-permute-start | bytes 393224 | tf_op jit(solution)/shard_map/ppermute | solution.py:385
  17.9 12.0 %collective-permute-start.6 = (bf16[64,1024]{1,0:T(8,128)(2,1)S(1)}, bf16[64,1024]{1,0:T(8,128)(2,1)S(1)}, u32[]{:S(2)}, u32[]{:S(2)}) collective-permute-start(bf16[64,1024]{1,0:T(8,128)(2,1)S(1)} %bitcast.17), channel_id=1, source_target_pairs={{0,6},{1,7},{2,0},{3,1},{4,2},{5,3},{6,4},{7,5},{8,14},{9,15},{10,... | collective-permute-start | bytes 393224 | tf_op jit(solution)/shard_map/ppermute | solution.py:385
  19.4 17.0 %collective-permute-start.12 = (bf16[64,1024]{1,0:T(8,128)(2,1)S(1)}, bf16[64,1024]{1,0:T(8,128)(2,1)S(1)}, u32[]{:S(2)}, u32[]{:S(2)}) collective-permute-start(bf16[64,1024]{1,0:T(8,128)(2,1)S(1)} %get-tuple-element.19), channel_id=1, source_target_pairs={{0,8},{1,9},{2,10},{3,11},{4,12},{5,13},{6,14},{7,15},{8,0},{9,1},... | collective-permute-start | bytes 393224 | tf_op jit(solution)/shard_map/ppermute | solution.py:385
  20.9 16.1 %collective-permute-start.13 = (bf16[64,1024]{1,0:T(8,128)(2,1)S(1)}, bf16[64,1024]{1,0:T(8,128)(2,1)S(1)}, u32[]{:S(2)}, u32[]{:S(2)}) collective-permute-start(bf16[64,1024]{1,0:T(8,128)(2,1)S(1)} %get-tuple-element.20), channel_id=1, source_target_pairs={{0,16},{1,17},{2,18},{3,19},{4,20},{5,21},{6,22},{7,23},{8,24},{9,... | collective-permute-start | bytes 393224 | tf_op jit(solution)/shard_map/ppermute | solution.py:385
  30.0 20.7 %copy-start.4 = (bf16[512,1536]{1,0:T(8,128)(2,1)S(1)}, bf16[512,1536]{1,0:T(8,128)(2,1)}, u32[]{:S(2)}) copy-start(bf16[512,1536]{1,0:T(8,128)(2,1)} %gin_hbm.1) | copy-start | bytes 4718596
  30.0 20.7 %collective-permute-start.7 = (bf16[256,1024]{1,0:T(8,128)(2,1)S(1)}, bf16[256,1024]{1,0:T(8,128)(2,1)S(1)}, u32[]{:S(2)}, u32[]{:S(2)}) collective-permute-start(bf16[256,1024]{1,0:T(8,128)(2,1)S(1)} %place.7.refs_7_.refs_8_), channel_id=1, source_target_pairs={{0,8},{1,9},{2,10},{3,11},{4,12},{5,13},{6,14},{7,15},{8,0},{9,1},... | collective-permute-start | bytes 1572872 | tf_op jit(solution)/shard_map/ppermute | solution.py:385
  31.6 19.1 %collective-permute-start.8 = (bf16[256,1024]{1,0:T(8,128)(2,1)S(1)}, bf16[256,1024]{1,0:T(8,128)(2,1)S(1)}, u32[]{:S(2)}, u32[]{:S(2)}) collective-permute-start(bf16[256,1024]{1,0:T(8,128)(2,1)S(1)} %place.7.refs_7_.refs_8_), channel_id=1, source_target_pairs={{0,16},{1,17},{2,18},{3,19},{4,20},{5,21},{6,22},{7,23},{8,24},{9,... | collective-permute-start | bytes 1572872 | tf_op jit(solution)/shard_map/ppermute | solution.py:385
  33.1 9.6 %collective-permute-start.11 = (bf16[128,1024]{1,0:T(8,128)(2,1)S(1)}, bf16[128,1024]{1,0:T(8,128)(2,1)S(1)}, u32[]{:S(2)}, u32[]{:S(2)}) collective-permute-start(bf16[128,1024]{1,0:T(8,128)(2,1)S(1)} %collective-permute-done.2.refs_2_.refs_3_), channel_id=1, source_target_pairs={{0,2},{1,3},{2,4},{3,5},{4,6},{5,7},{6,0},{7,1},{8,10},{9,11},{10,... | collective-permute-start | bytes 786440 | tf_op jit(solution)/shard_map/ppermute | solution.py:385
  36.4 14.3 %collective-permute-start.10 = (bf16[128,1024]{1,0:T(8,128)(2,1)S(1)}, bf16[128,1024]{1,0:T(8,128)(2,1)S(1)}, u32[]{:S(2)}, u32[]{:S(2)}) collective-permute-start(bf16[128,1024]{1,0:T(8,128)(2,1)S(1)} %collective-permute-done.2.refs_2_.refs_3_), channel_id=1, source_target_pairs={{0,16},{1,17},{2,18},{3,19},{4,20},{5,21},{6,22},{7,23},{8,24},{9,... | collective-permute-start | bytes 786440 | tf_op jit(solution)/shard_map/ppermute | solution.py:385
  36.9 13.8 %collective-permute-start.9 = (bf16[128,1024]{1,0:T(8,128)(2,1)S(1)}, bf16[128,1024]{1,0:T(8,128)(2,1)S(1)}, u32[]{:S(2)}, u32[]{:S(2)}) collective-permute-start(bf16[128,1024]{1,0:T(8,128)(2,1)S(1)} %collective-permute-done.2.refs_2_.refs_3_), channel_id=1, source_target_pairs={{0,8},{1,9},{2,10},{3,11},{4,12},{5,13},{6,14},{7,15},{8,0},{9,1},... | collective-permute-start | bytes 786440 | tf_op jit(solution)/shard_map/ppermute | solution.py:385
  54.8 34.9 %copy-start = (bf16[1024,1024]{1,0:T(8,128)(2,1)}, bf16[1024,1024]{1,0:T(8,128)(2,1)S(1)}, u32[]{:S(2)}) copy-start(bf16[1024,1024]{1,0:T(8,128)(2,1)S(1)} %cell.1.joined_ref.refs_0_.refs_2_) | copy-start | bytes 6291460
  54.8 11.3 %collective-permute-start.14 = (bf16[1024,1024]{1,0:T(8,128)(2,1)S(1)}, bf16[1024,1024]{1,0:T(8,128)(2,1)S(1)}, u32[]{:S(2)}, u32[]{:S(2)}) collective-permute-start(bf16[1024,1024]{1,0:T(8,128)(2,1)S(1)} %cell.1.joined_ref.refs_0_.refs_2_), channel_id=1, source_target_pairs={{0,1},{1,0},{2,3},{3,2},{4,5},{5,4},{6,7},{7,6},{8,9},{9,8},{10,11... | collective-permute-start | bytes 6291464 | tf_op jit(solution)/shard_map/ppermute | solution.py:385
  54.9 9.2 %collective-permute-start.15 = (bf16[128,1024]{1,0:T(8,128)(2,1)S(1)}, bf16[128,1024]{1,0:T(8,128)(2,1)S(1)}, u32[]{:S(2)}, u32[]{:S(2)}) collective-permute-start(bf16[128,1024]{1,0:T(8,128)(2,1)S(1)} %get-tuple-element.21), channel_id=1, source_target_pairs={{0,8},{1,9},{2,10},{3,11},{4,12},{5,13},{6,14},{7,15},{8,0},{9,1},... | collective-permute-start | bytes 786440 | tf_op jit(solution)/shard_map/ppermute | solution.py:385
  55.5 10.1 %collective-permute-start.16 = (bf16[128,1024]{1,0:T(8,128)(2,1)S(1)}, bf16[128,1024]{1,0:T(8,128)(2,1)S(1)}, u32[]{:S(2)}, u32[]{:S(2)}) collective-permute-start(bf16[128,1024]{1,0:T(8,128)(2,1)S(1)} %get-tuple-element.22), channel_id=1, source_target_pairs={{0,16},{1,17},{2,18},{3,19},{4,20},{5,21},{6,22},{7,23},{8,24},{9,... | collective-permute-start | bytes 786440 | tf_op jit(solution)/shard_map/ppermute | solution.py:385
  57.0 15.1 %collective-permute-start.23 = (bf16[128,1024]{1,0:T(8,128)(2,1)S(1)}, bf16[128,1024]{1,0:T(8,128)(2,1)S(1)}, u32[]{:S(2)}, u32[]{:S(2)}) collective-permute-start(bf16[128,1024]{1,0:T(8,128)(2,1)S(1)} %collective-permute-done.11.refs_4_.refs_3_), channel_id=1, source_target_pairs={{0,2},{1,3},{2,4},{3,5},{4,6},{5,7},{6,0},{7,1},{8,10},{9,11},{10,... | collective-permute-start | bytes 786440 | tf_op jit(solution)/shard_map/ppermute | solution.py:385
  60.4 13.1 %collective-permute-start.19 = (bf16[128,1024]{1,0:T(8,128)(2,1)S(1)}, bf16[128,1024]{1,0:T(8,128)(2,1)S(1)}, u32[]{:S(2)}, u32[]{:S(2)}) collective-permute-start(bf16[128,1024]{1,0:T(8,128)(2,1)S(1)} %collective-permute-done.11.refs_4_.refs_3_), channel_id=1, source_target_pairs={{0,8},{1,9},{2,10},{3,11},{4,12},{5,13},{6,14},{7,15},{8,0},{9,1},... | collective-permute-start | bytes 786440 | tf_op jit(solution)/shard_map/ppermute | solution.py:385
  64.1 10.9 %collective-permute-start.20 = (bf16[128,1024]{1,0:T(8,128)(2,1)S(1)}, bf16[128,1024]{1,0:T(8,128)(2,1)S(1)}, u32[]{:S(2)}, u32[]{:S(2)}) collective-permute-start(bf16[128,1024]{1,0:T(8,128)(2,1)S(1)} %collective-permute-done.11.refs_4_.refs_3_), channel_id=1, source_target_pairs={{0,16},{1,17},{2,18},{3,19},{4,20},{5,21},{6,22},{7,23},{8,24},{9,... | collective-permute-start | bytes 786440 | tf_op jit(solution)/shard_map/ppermute | solution.py:385
  65.6 10.0 %collective-permute-start.17 = (bf16[64,1024]{1,0:T(8,128)(2,1)S(1)}, bf16[64,1024]{1,0:T(8,128)(2,1)S(1)}, u32[]{:S(2)}, u32[]{:S(2)}) collective-permute-start(bf16[64,1024]{1,0:T(8,128)(2,1)S(1)} %get-tuple-element.23), channel_id=1, source_target_pairs={{0,8},{1,9},{2,10},{3,11},{4,12},{5,13},{6,14},{7,15},{8,0},{9,1},... | collective-permute-start | bytes 393224 | tf_op jit(solution)/shard_map/ppermute | solution.py:385
  66.1 10.3 %collective-permute-start.18 = (bf16[64,1024]{1,0:T(8,128)(2,1)S(1)}, bf16[64,1024]{1,0:T(8,128)(2,1)S(1)}, u32[]{:S(2)}, u32[]{:S(2)}) collective-permute-start(bf16[64,1024]{1,0:T(8,128)(2,1)S(1)} %get-tuple-element.24), channel_id=1, source_target_pairs={{0,16},{1,17},{2,18},{3,19},{4,20},{5,21},{6,22},{7,23},{8,24},{9,... | collective-permute-start | bytes 393224 | tf_op jit(solution)/shard_map/ppermute | solution.py:385
  72.2 9.4 %collective-permute-start.24 = (bf16[128,1024]{1,0:T(8,128)(2,1)S(1)}, bf16[128,1024]{1,0:T(8,128)(2,1)S(1)}, u32[]{:S(2)}, u32[]{:S(2)}) collective-permute-start(bf16[128,1024]{1,0:T(8,128)(2,1)S(1)} %place.12), channel_id=1, source_target_pairs={{0,8},{1,9},{2,10},{3,11},{4,12},{5,13},{6,14},{7,15},{8,0},{9,1},... | collective-permute-start | bytes 786440 | tf_op jit(solution)/shard_map/ppermute | solution.py:385
  73.5 8.1 %collective-permute-start.25 = (bf16[128,1024]{1,0:T(8,128)(2,1)S(1)}, bf16[128,1024]{1,0:T(8,128)(2,1)S(1)}, u32[]{:S(2)}, u32[]{:S(2)}) collective-permute-start(bf16[128,1024]{1,0:T(8,128)(2,1)S(1)} %place.12), channel_id=1, source_target_pairs={{0,16},{1,17},{2,18},{3,19},{4,20},{5,21},{6,22},{7,23},{8,24},{9,... | collective-permute-start | bytes 786440 | tf_op jit(solution)/shard_map/ppermute | solution.py:385
  75.0 9.5 %collective-permute-start.21 = (bf16[64,1024]{1,0:T(8,128)(2,1)S(1)}, bf16[64,1024]{1,0:T(8,128)(2,1)S(1)}, u32[]{:S(2)}, u32[]{:S(2)}) collective-permute-start(bf16[64,1024]{1,0:T(8,128)(2,1)S(1)} %get-tuple-element.25), channel_id=1, source_target_pairs={{0,8},{1,9},{2,10},{3,11},{4,12},{5,13},{6,14},{7,15},{8,0},{9,1},... | collective-permute-start | bytes 393224 | tf_op jit(solution)/shard_map/ppermute | solution.py:385
  75.6 8.8 %collective-permute-start.22 = (bf16[64,1024]{1,0:T(8,128)(2,1)S(1)}, bf16[64,1024]{1,0:T(8,128)(2,1)S(1)}, u32[]{:S(2)}, u32[]{:S(2)}) collective-permute-start(bf16[64,1024]{1,0:T(8,128)(2,1)S(1)} %get-tuple-element.26), channel_id=1, source_target_pairs={{0,16},{1,17},{2,18},{3,19},{4,20},{5,21},{6,22},{7,23},{8,24},{9,... | collective-permute-start | bytes 393224 | tf_op jit(solution)/shard_map/ppermute | solution.py:385
  81.7 8.0 %collective-permute-start.26 = (bf16[64,1024]{1,0:T(8,128)(2,1)S(1)}, bf16[64,1024]{1,0:T(8,128)(2,1)S(1)}, u32[]{:S(2)}, u32[]{:S(2)}) collective-permute-start(bf16[64,1024]{1,0:T(8,128)(2,1)S(1)} %get-tuple-element.27), channel_id=1, source_target_pairs={{0,8},{1,9},{2,10},{3,11},{4,12},{5,13},{6,14},{7,15},{8,0},{9,1},... | collective-permute-start | bytes 393224 | tf_op jit(solution)/shard_map/ppermute | solution.py:385
  83.0 6.7 %collective-permute-start.27 = (bf16[64,1024]{1,0:T(8,128)(2,1)S(1)}, bf16[64,1024]{1,0:T(8,128)(2,1)S(1)}, u32[]{:S(2)}, u32[]{:S(2)}) collective-permute-start(bf16[64,1024]{1,0:T(8,128)(2,1)S(1)} %get-tuple-element.28), channel_id=1, source_target_pairs={{0,16},{1,17},{2,18},{3,19},{4,20},{5,21},{6,22},{7,23},{8,24},{9,... | collective-permute-start | bytes 393224 | tf_op jit(solution)/shard_map/ppermute | solution.py:385
  95.6 11.2 %all-to-all-start.1 = ((f32[32,1,64]{2,1,0:T(1,128)}), f32[32,1,64]{2,1,0:T(1,128)S(1)}, u32[]{:S(2)}, u32[]{:S(2)}) async-start(f32[32,1,64]{2,1,0:T(1,128)} %bitcast.10), calls=%async_computation.1 | async-start | bytes 32768 | tf_op jit(solution)/shard_map/all_to_all | solution.py:381
  (6 other events, 61.0 us)

commit v3 on v2

--- a/solution.py
+++ b/solution.py
@@ -269,56 +269,51 @@
     line_ref, win_ref, wout_ref = take(3)
     groups, width, both = win_ref.shape
     half = both // 2
-    chunk = sides[0].shape[0]
-
-    @pl.when(pl.program_id(0) == 0)
-    def _():
-        for group, index, count, flip, place in ins:
-            owner = 0 if flip is None else owner_at(flip)
-            at = pl.multiple_of(owner * rows[0] + place, 16)
-            win_ref[group, pl.ds(at, count), :] = in_refs[index][...]
-        if depth == 1:
-            wout_ref[0] = out_refs[0][...]
-        else:
-            for index, start, flip, back in outs:
-                chip = owner_at(flip) * depth + depth_at(back, depth)
-                to = pl.ds(pl.multiple_of(chip * rows[1], 16), rows[1])
-                for g, group_back in enumerate(backs):
-                    place = depth_at(group_back, depth)
-                    lanes = pl.ds(pl.multiple_of(lax.rem(place, 2) * width, LANES), width)
-                    line = pl.ds(pl.multiple_of(start + rows[1] * (place // 2), 16), rows[1])
-                    wout_ref[g, to, :] = out_refs[index][line, lanes]
+    chunk = min(sides[0].shape[0], 2 * CHUNK)
+
+    for group, index, count, flip, place in ins:
+        owner = 0 if flip is None else owner_at(flip)
+        at = pl.multiple_of(owner * rows[0] + place, 16)
+        win_ref[group, pl.ds(at, count), :] = in_refs[index][...]
+    if depth == 1:
+        wout_ref[0] = out_refs[0][...]
+    else:
+        for index, start, flip, back in outs:
+            chip = owner_at(flip) * depth + depth_at(back, depth)
+            to = pl.ds(pl.multiple_of(chip * rows[1], 16), rows[1])
+            for g, group_back in enumerate(backs):
+                place = depth_at(group_back, depth)
+                lanes = pl.ds(pl.multiple_of(lax.rem(place, 2) * width, LANES), width)
+                line = pl.ds(pl.multiple_of(start + rows[1] * (place // 2), 16), rows[1])
+                wout_ref[g, to, :] = out_refs[index][line, lanes]
 
     near = chunk // cap
-    at = pl.ds(pl.multiple_of(pl.program_id(0) * near, near), near)
-    for side in range(2):
-        joined = sides[side][...]
-        tower = jnp.zeros((chunk, half), F32)
-        for g in range(groups):
-            h = gelu(dot(joined, win_ref[g], 1, 1)).astype(BF16)
-            tower = tower + dot(h, wout_ref[g], 1, 1)
-        score = jnp.sum(tower * joined[:, half:].astype(F32), axis=1, keepdims=True)
-        place = (iota((chunk, cap), 0) & (cap - 1)) == iota((chunk, cap), 1)
-        source = onehot(iota((near, chunk), 1) // cap == iota((near, chunk), 0))
-        lines = sum(dot(source, p) for p in split3(jnp.where(place, score, 0.0)))
-        lanes = slice(side * cap, (side + 1) * cap)
-        if not first:
-            lines = lines + before[at, lanes]
-        if last:
-            lines = lines / jnp.sqrt(F32(half))
-        line_ref[at, lanes] = lines
+    for k in range(sides[0].shape[0] // chunk):
+        at = slice(k * near, (k + 1) * near)
+        for side in range(2):
+            joined = sides[side][k * chunk : (k + 1) * chunk, :]
+            tower = jnp.zeros((chunk, half), F32)
+            for g in range(groups):
+                h = gelu(dot(joined, win_ref[g], 1, 1)).astype(BF16)
+                tower = tower + dot(h, wout_ref[g], 1, 1)
+            score = jnp.sum(tower * joined[:, half:].astype(F32), axis=1, keepdims=True)
+            place = (iota((chunk, cap), 0) & (cap - 1)) == iota((chunk, cap), 1)
+            source = onehot(iota((near, chunk), 1) // cap == iota((near, chunk), 0))
+            lines = sum(dot(source, p) for p in split3(jnp.where(place, score, 0.0)))
+            lanes = slice(side * cap, (side + 1) * cap)
+            if not first:
+                lines = lines + before[at, lanes]
+            if last:
+                lines = lines / jnp.sqrt(F32(half))
+            line_ref[at, lanes] = lines
 
 
 def step(sides, before, ins, outs, backs, rows, depth, cap, last, after=()):
     n, half = sides[0].shape[0], sides[0].shape[1] // 2
     shards = n // cap
-    chunk = min(n, 2 * CHUNK)
     in_parts = [(group, i, count, flip, place) for i, (group, _, count, flip, place) in enumerate(ins)]
     out_parts = [(i, start, flip, back) for i, (_, parts) in enumerate(outs) for start, flip, back in parts]
     width = sum(count for group, _, count, _, _ in ins if group == 0)
-    side = pl.BlockSpec((chunk, 2 * half), lambda i: (i, 0))
-    line = pl.BlockSpec((shards, 2 * cap), lambda i: (0, 0))
-    whole = lambda a: pl.BlockSpec(a.shape, lambda i: (0, 0))
     units = len(backs) * width
     in_arrays, out_arrays = [a for _, a, _, _, _ in ins], [a for a, _ in outs]
     return pl.pallas_call(
@@ -336,13 +331,9 @@
             first=before is None,
             last=last,
         ),
-        grid=(n // chunk,),
         out_shape=jax.ShapeDtypeStruct((shards, 2 * cap), F32),
-        in_specs=[side] * 2
-        + ([] if before is None else [line])
-        + [whole(a) for a in in_arrays + out_arrays]
-        + [ANY] * len(after),
-        out_specs=line,
+        in_specs=[VMEM] * (2 + (before is not None) + len(in_arrays) + len(out_arrays)) + [ANY] * len(after),
+        out_specs=VMEM,
         scratch_shapes=[pltpu.VMEM((len(backs), width, 2 * half), BF16), pltpu.VMEM((len(backs), half, width), BF16)],
         compiler_params=pltpu.CompilerParams(vmem_limit_bytes=40 * 2**20),
         cost_estimate=pl.CostEstimate(flops=12 * n * units * half, bytes_accessed=10**7, transcendentals=2 * n * units),

time: 108 us -> 107 us (level)
  Pallas kernels: 44.4 us -> 43.3 us
  transfers between devices with their start and end apart: 30 -> 30, of which waited for: 3 -> 5; matrix products, arithmetic and copies ran while one was open for 1% -> 1% of each run, Pallas kernels for 29% -> 28%
where the time goes in v3:
time: 107 us
  starting transfers between devices  46.4 us (43%)
  Pallas kernels  43.3 us (40%)
  waiting for transfers between devices  13.4 us (13%)
  local copies, waits for them, and re-layouts  2.25 us (2%)
    ppermute x28, starting transfers between devices, send(): return lax.ppermute(x, AXES, [(d, to(d)) for d in range(devices)])  38.6 us
    pallas_call x4, Pallas kernels, step(): pl.pallas_call(functools.partial(step_kernel, n_in=len(in_arrays), n_out=...  20.5 us
    ppermute x28, waiting for transfers between devices, send(): return lax.ppermute(x, AXES, [(d, to(d)) for d in range(devices)])  13.2 us
    pallas_call x2, Pallas kernels, fetch(): pl.pallas_call(functools.partial(fetch_kernel, cap=cap, column=column), o...  8.22 us
    all_to_all x2, starting transfers between devices, exchange(): return lax.all_to_all(x, AXES, split_axis=0, concat_axis=0, tiled=True)  7.74 us
    pallas_call x1, Pallas kernels, update(): pl.pallas_call(functools.partial(update_kernel, cap=cap), out_shape=jax.S...  6.93 us
    pallas_call x1, Pallas kernels, cell(): pl.pallas_call(cell_kernel, out_shape=jax.ShapeDtypeStruct((n, 2 * width)...  4.04 us
    pallas_call x1, Pallas kernels, route(): pl.pallas_call(functools.partial(route_kernel, shards=shards, cap=cap, ro...  2.69 us
  transfers between devices with their start and end apart: 30, of which 5 were waited for; matrix products, arithmetic and copies ran while one was open for 1% of the time, Pallas kernels for 28%

profile of v3, /device:TPU:0, one launch (start us, length us, event | category | flops | bytes accessed | tf_op | source)
XLA Modules:
  0.0 107.0 jit_solution(4197403408039026176)
XLA Ops:
  0.6 2.7 %route.1 = (s32[32,64]{1,0:T(8,128)}, s32[2,512]{1,0:T(2,128)}, bf16[32,1024]{1,0:T(8,128)(2,1)}, bf16[32,1024]{1,0:T(8,128)(2,1)}) custom-call(s32[512,128]{1,0:T(8,128)} %bitcast.25, s32[1,512]{1,0:T(1,128)} %bitcast.27, s32[1,512]{1,0:T(1,128)} %bitcast.28, bf16[16,4096]{1,0:T(8,128)(2,1)} %refs_3_.1), custom_call_target="tpu_custom_call" | custom-call | flops 1000000000 | bytes 1000000 | tf_op jit(solution)/shard_map/route/pallas_call | solution.py:106
  3.9 2.6 %collective-permute-start = (bf16[128,1024]{1,0:T(8,128)(2,1)S(1)}, bf16[128,1024]{1,0:T(8,128)(2,1)S(1)}, u32[]{:S(2)}, u32[]{:S(2)}) collective-permute-start(bf16[128,1024]{1,0:T(8,128)(2,1)S(1)} %copy-done.6), channel_id=1, source_target_pairs={{0,8},{1,9},{2,10},{3,11},{4,12},{5,13},{6,14},{7,15},{8,0},{9,1},... | collective-permute-start | bytes 786440 | tf_op jit(solution)/shard_map/ppermute | solution.py:376
  6.4 1.5 %collective-permute-start.1 = (bf16[128,1024]{1,0:T(8,128)(2,1)S(1)}, bf16[128,1024]{1,0:T(8,128)(2,1)S(1)}, u32[]{:S(2)}, u32[]{:S(2)}) collective-permute-start(bf16[128,1024]{1,0:T(8,128)(2,1)S(1)} %copy-done.6), channel_id=1, source_target_pairs={{0,16},{1,17},{2,18},{3,19},{4,20},{5,21},{6,22},{7,23},{8,24},{9,... | collective-permute-start | bytes 786440 | tf_op jit(solution)/shard_map/ppermute | solution.py:376
  8.8 1.6 %collective-permute-start.4 = (bf16[64,1024]{1,0:T(8,128)(2,1)S(1)}, bf16[64,1024]{1,0:T(8,128)(2,1)S(1)}, u32[]{:S(2)}, u32[]{:S(2)}) collective-permute-start(bf16[64,1024]{1,0:T(8,128)(2,1)S(1)} %bitcast.15), channel_id=1, source_target_pairs={{0,2},{1,3},{2,4},{3,5},{4,6},{5,7},{6,0},{7,1},{8,10},{9,11},{10,... | collective-permute-start | bytes 393224 | tf_op jit(solution)/shard_map/ppermute | solution.py:376
  10.5 3.2 %all-to-all-start = ((s32[32,1,64]{2,1,0:T(1,128)}), s32[32,1,64]{2,1,0:T(1,128)S(1)}, u32[]{:S(2)}, u32[]{:S(2)}) async-start(s32[32,1,64]{2,1,0:T(1,128)} %bitcast.24), calls=%async_computation | async-start | bytes 32768 | tf_op jit(solution)/shard_map/all_to_all | solution.py:372
  13.7 1.8 %collective-permute-start.2 = (bf16[128,1024]{1,0:T(8,128)(2,1)S(1)}, bf16[128,1024]{1,0:T(8,128)(2,1)S(1)}, u32[]{:S(2)}, u32[]{:S(2)}) collective-permute-start(bf16[128,1024]{1,0:T(8,128)(2,1)S(1)} %copy-done.6), channel_id=1, source_target_pairs={{0,2},{1,3},{2,4},{3,5},{4,6},{5,7},{6,0},{7,1},{8,10},{9,11},{10,... | collective-permute-start | bytes 786440 | tf_op jit(solution)/shard_map/ppermute | solution.py:376
  15.5 2.4 %collective-permute-start.5 = (bf16[64,1024]{1,0:T(8,128)(2,1)S(1)}, bf16[64,1024]{1,0:T(8,128)(2,1)S(1)}, u32[]{:S(2)}, u32[]{:S(2)}) collective-permute-start(bf16[64,1024]{1,0:T(8,128)(2,1)S(1)} %bitcast.16), channel_id=1, source_target_pairs={{0,4},{1,5},{2,6},{3,7},{4,0},{5,1},{6,2},{7,3},{8,12},{9,13},{10,... | collective-permute-start | bytes 393224 | tf_op jit(solution)/shard_map/ppermute | solution.py:376
  17.9 1.4 %collective-permute-start.6 = (bf16[64,1024]{1,0:T(8,128)(2,1)S(1)}, bf16[64,1024]{1,0:T(8,128)(2,1)S(1)}, u32[]{:S(2)}, u32[]{:S(2)}) collective-permute-start(bf16[64,1024]{1,0:T(8,128)(2,1)S(1)} %bitcast.17), channel_id=1, source_target_pairs={{0,6},{1,7},{2,0},{3,1},{4,2},{5,3},{6,4},{7,5},{8,14},{9,15},{10,... | collective-permute-start | bytes 393224 | tf_op jit(solution)/shard_map/ppermute | solution.py:376
  19.4 1.5 %collective-permute-start.12 = (bf16[64,1024]{1,0:T(8,128)(2,1)S(1)}, bf16[64,1024]{1,0:T(8,128)(2,1)S(1)}, u32[]{:S(2)}, u32[]{:S(2)}) collective-permute-start(bf16[64,1024]{1,0:T(8,128)(2,1)S(1)} %get-tuple-element.19), channel_id=1, source_target_pairs={{0,8},{1,9},{2,10},{3,11},{4,12},{5,13},{6,14},{7,15},{8,0},{9,1},... | collective-permute-start | bytes 393224 | tf_op jit(solution)/shard_map/ppermute | solution.py:376
  20.9 1.5 %collective-permute-start.13 = (bf16[64,1024]{1,0:T(8,128)(2,1)S(1)}, bf16[64,1024]{1,0:T(8,128)(2,1)S(1)}, u32[]{:S(2)}, u32[]{:S(2)}) collective-permute-start(bf16[64,1024]{1,0:T(8,128)(2,1)S(1)} %get-tuple-element.20), channel_id=1, source_target_pairs={{0,16},{1,17},{2,18},{3,19},{4,20},{5,21},{6,22},{7,23},{8,24},{9,... | collective-permute-start | bytes 393224 | tf_op jit(solution)/shard_map/ppermute | solution.py:376
  22.4 2.2 %copy-done.3 = f32[2048,512]{1,0:T(8,128)S(1)} copy-done((f32[2048,512]{1,0:T(8,128)S(1)}, f32[2048,512]{1,0:T(8,128)}, u32[]{:S(2)}) %copy-start.3) | copy-done | bytes 4194328
  24.6 3.0 %fetch.2.refs_3_.prior_ref = bf16[1024,512]{1,0:T(8,128)(2,1)S(1)} custom-call(s32[32,64]{1,0:T(8,128)S(1)} %bitcast.19, f32[2048,512]{1,0:T(8,128)S(1)} %copy-done.3), custom_call_target="tpu_custom_call" | custom-call | flops 10737418240 | bytes 5000000 | tf_op jit(solution)/shard_map/fetch/pallas_call | solution.py:161
  27.6 2.4 %collective-permute-done.5.refs_2_ = bf16[64,1024]{1,0:T(8,128)(2,1)S(1)} collective-permute-done((bf16[64,1024]{1,0:T(8,128)(2,1)S(1)}, bf16[64,1024]{1,0:T(8,128)(2,1)S(1)}, u32[]{:S(2)}, u32[]{:S(2)}) %collective-permute-start.5) | collective-permute-done | bytes 131104 | tf_op jit(solution)/shard_map/ppermute | solution.py:376
  30.0 1.6 %collective-permute-start.7 = (bf16[256,1024]{1,0:T(8,128)(2,1)S(1)}, bf16[256,1024]{1,0:T(8,128)(2,1)S(1)}, u32[]{:S(2)}, u32[]{:S(2)}) collective-permute-start(bf16[256,1024]{1,0:T(8,128)(2,1)S(1)} %place.7.refs_7_.refs_8_), channel_id=1, source_target_pairs={{0,8},{1,9},{2,10},{3,11},{4,12},{5,13},{6,14},{7,15},{8,0},{9,1},... | collective-permute-start | bytes 1572872 | tf_op jit(solution)/shard_map/ppermute | solution.py:376
  31.6 1.5 %collective-permute-start.8 = (bf16[256,1024]{1,0:T(8,128)(2,1)S(1)}, bf16[256,1024]{1,0:T(8,128)(2,1)S(1)}, u32[]{:S(2)}, u32[]{:S(2)}) collective-permute-start(bf16[256,1024]{1,0:T(8,128)(2,1)S(1)} %place.7.refs_7_.refs_8_), channel_id=1, source_target_pairs={{0,16},{1,17},{2,18},{3,19},{4,20},{5,21},{6,22},{7,23},{8,24},{9,... | collective-permute-start | bytes 1572872 | tf_op jit(solution)/shard_map/ppermute | solution.py:376
  33.1 3.3 %collective-permute-start.11 = (bf16[128,1024]{1,0:T(8,128)(2,1)S(1)}, bf16[128,1024]{1,0:T(8,128)(2,1)S(1)}, u32[]{:S(2)}, u32[]{:S(2)}) collective-permute-start(bf16[128,1024]{1,0:T(8,128)(2,1)S(1)} %collective-permute-done.2.refs_2_.refs_3_), channel_id=1, source_target_pairs={{0,2},{1,3},{2,4},{3,5},{4,6},{5,7},{6,0},{7,1},{8,10},{9,11},{10,... | collective-permute-start | bytes 786440 | tf_op jit(solution)/shard_map/ppermute | solution.py:376
  37.4 5.2 %fetch.3.inputs_ref = bf16[1024,512]{1,0:T(8,128)(2,1)S(1)} custom-call(s32[32,64]{1,0:T(8,128)S(1)} %bitcast.20, bf16[4096,512]{1,0:T(8,128)(2,1)S(1)} %copy-done.2, bf16[128,1024]{1,0:T(8,128)(2,1)S(1)} %collective-permute-done.refs_0_.refs_1_.refs_3_, bf16[128,1024]{1,0:T(8,128)(2,1)S(1)} %collective-permute-done.1.refs_1_.refs_0_.refs_4_, ...), custom_call_target="tpu_custom_call" | custom-call | flops 21474836480 | bytes 5000000 | tf_op jit(solution)/shard_map/fetch/pallas_call | solution.py:161
  42.7 8.0 %collective-permute-done.10.refs_3_.refs_0_.refs_5_ = bf16[128,1024]{1,0:T(8,128)(2,1)S(1)} collective-permute-done((bf16[128,1024]{1,0:T(8,128)(2,1)S(1)}, bf16[128,1024]{1,0:T(8,128)(2,1)S(1)}, u32[]{:S(2)}, u32[]{:S(2)}) %collective-permute-start.10) | collective-permute-done | bytes 262176 | tf_op jit(solution)/shard_map/ppermute | solution.py:376
  50.7 4.0 %cell.1.joined_ref.refs_0_.refs_2_ = bf16[1024,1024]{1,0:T(8,128)(2,1)S(1)} custom-call(bf16[1024,512]{1,0:T(8,128)(2,1)S(1)} %fetch.2.refs_3_.prior_ref, bf16[1024,512]{1,0:T(8,128)(2,1)S(1)} %fetch.3.inputs_ref, bf16[512,1536]{1,0:T(8,128)(2,1)S(1)} %copy-done.4, bf16[512,1536]{1,0:T(8,128)(2,1)S(1)} %copy-done.5, ...), custom_call_target="tpu_custom_call" | custom-call | flops 4000000000 | bytes 6000000 | tf_op jit(solution)/shard_map/cell/pallas_call | solution.py:196
  55.5 1.5 %collective-permute-start.16 = (bf16[128,1024]{1,0:T(8,128)(2,1)S(1)}, bf16[128,1024]{1,0:T(8,128)(2,1)S(1)}, u32[]{:S(2)}, u32[]{:S(2)}) collective-permute-start(bf16[128,1024]{1,0:T(8,128)(2,1)S(1)} %get-tuple-element.22), channel_id=1, source_target_pairs={{0,16},{1,17},{2,18},{3,19},{4,20},{5,21},{6,22},{7,23},{8,24},{9,... | collective-permute-start | bytes 786440 | tf_op jit(solution)/shard_map/ppermute | solution.py:376
  57.0 3.4 %collective-permute-start.23 = (bf16[128,1024]{1,0:T(8,128)(2,1)S(1)}, bf16[128,1024]{1,0:T(8,128)(2,1)S(1)}, u32[]{:S(2)}, u32[]{:S(2)}) collective-permute-start(bf16[128,1024]{1,0:T(8,128)(2,1)S(1)} %collective-permute-done.11.refs_4_.refs_3_), channel_id=1, source_target_pairs={{0,2},{1,3},{2,4},{3,5},{4,6},{5,7},{6,0},{7,1},{8,10},{9,11},{10,... | collective-permute-start | bytes 786440 | tf_op jit(solution)/shard_map/ppermute | solution.py:376
  60.4 1.5 %collective-permute-start.19 = (bf16[128,1024]{1,0:T(8,128)(2,1)S(1)}, bf16[128,1024]{1,0:T(8,128)(2,1)S(1)}, u32[]{:S(2)}, u32[]{:S(2)}) collective-permute-start(bf16[128,1024]{1,0:T(8,128)(2,1)S(1)} %collective-permute-done.11.refs_4_.refs_3_), channel_id=1, source_target_pairs={{0,8},{1,9},{2,10},{3,11},{4,12},{5,13},{6,14},{7,15},{8,0},{9,1},... | collective-permute-start | bytes 786440 | tf_op jit(solution)/shard_map/ppermute | solution.py:376
  61.9 2.2 %collective-permute-done.15.refs_10_.refs_11_ = bf16[128,1024]{1,0:T(8,128)(2,1)S(1)} collective-permute-done((bf16[128,1024]{1,0:T(8,128)(2,1)S(1)}, bf16[128,1024]{1,0:T(8,128)(2,1)S(1)}, u32[]{:S(2)}, u32[]{:S(2)}) %collective-permute-start.15) | collective-permute-done | bytes 262176 | tf_op jit(solution)/shard_map/ppermute | solution.py:376
  64.1 1.5 %collective-permute-start.20 = (bf16[128,1024]{1,0:T(8,128)(2,1)S(1)}, bf16[128,1024]{1,0:T(8,128)(2,1)S(1)}, u32[]{:S(2)}, u32[]{:S(2)}) collective-permute-start(bf16[128,1024]{1,0:T(8,128)(2,1)S(1)} %collective-permute-done.11.refs_4_.refs_3_), channel_id=1, source_target_pairs={{0,16},{1,17},{2,18},{3,19},{4,20},{5,21},{6,22},{7,23},{8,24},{9,... | collective-permute-start | bytes 786440 | tf_op jit(solution)/shard_map/ppermute | solution.py:376
  66.9 4.9 %tower.4.refs_2_.refs_1_ = f32[32,64]{1,0:T(8,128)S(1)} custom-call(bf16[1024,1024]{1,0:T(8,128)(2,1)S(1)} %cell.1.joined_ref.refs_0_.refs_2_, bf16[1024,1024]{1,0:T(8,128)(2,1)S(1)} %collective-permute-done.14.refs_1_, bf16[128,1024]{1,0:T(8,128)(2,1)S(1)} %copy-done.6, bf16[128,1024]{1,0:T(8,128)(2,1)S(1)} %collective-permute-done.refs_0_.refs_1_.refs_3_, ...), custom_call_target="tpu_custom_call" | custom-call | flops 3221225472 | bytes 10000000 | tf_op jit(solution)/shard_map/tower/pallas_call | solution.py:319
  73.2 1.5 %collective-permute-start.25 = (bf16[128,1024]{1,0:T(8,128)(2,1)S(1)}, bf16[128,1024]{1,0:T(8,128)(2,1)S(1)}, u32[]{:S(2)}, u32[]{:S(2)}) collective-permute-start(bf16[128,1024]{1,0:T(8,128)(2,1)S(1)} %place.12), channel_id=1, source_target_pairs={{0,16},{1,17},{2,18},{3,19},{4,20},{5,21},{6,22},{7,23},{8,24},{9,... | collective-permute-start | bytes 786440 | tf_op jit(solution)/shard_map/ppermute | solution.py:376
  76.1 4.9 %tower.5.refs_2_ = f32[32,64]{1,0:T(8,128)S(1)} custom-call(bf16[1024,1024]{1,0:T(8,128)(2,1)S(1)} %cell.1.joined_ref.refs_0_.refs_2_, bf16[1024,1024]{1,0:T(8,128)(2,1)S(1)} %collective-permute-done.14.refs_1_, f32[32,64]{1,0:T(8,128)S(1)} %tower.4.refs_2_.refs_1_, bf16[128,1024]{1,0:T(8,128)(2,1)S(1)} %collective-permute-done.2.refs_2_.refs_3_, ...), custom_call_target="tpu_custom_call" | custom-call | flops 3221225472 | bytes 10000000 | tf_op jit(solution)/shard_map/tower/pallas_call | solution.py:319
  82.3 1.5 %collective-permute-start.27 = (bf16[64,1024]{1,0:T(8,128)(2,1)S(1)}, bf16[64,1024]{1,0:T(8,128)(2,1)S(1)}, u32[]{:S(2)}, u32[]{:S(2)}) collective-permute-start(bf16[64,1024]{1,0:T(8,128)(2,1)S(1)} %get-tuple-element.28), channel_id=1, source_target_pairs={{0,16},{1,17},{2,18},{3,19},{4,20},{5,21},{6,22},{7,23},{8,24},{9,... | collective-permute-start | bytes 393224 | tf_op jit(solution)/shard_map/ppermute | solution.py:376
  83.8 5.1 %tower.6.refs_2_ = f32[32,64]{1,0:T(8,128)S(1)} custom-call(bf16[1024,1024]{1,0:T(8,128)(2,1)S(1)} %cell.1.joined_ref.refs_0_.refs_2_, bf16[1024,1024]{1,0:T(8,128)(2,1)S(1)} %collective-permute-done.14.refs_1_, f32[32,64]{1,0:T(8,128)S(1)} %tower.5.refs_2_, bf16[128,1024]{1,0:T(8,128)(2,1)S(1)} %collective-permute-done.11.refs_4_.refs_3_, ...), custom_call_target="tpu_custom_call" | custom-call | flops 3221225472 | bytes 10000000 | tf_op jit(solution)/shard_map/tower/pallas_call | solution.py:319
  89.0 5.5 %tower.7 = f32[32,64]{1,0:T(8,128)} custom-call(bf16[1024,1024]{1,0:T(8,128)(2,1)S(1)} %cell.1.joined_ref.refs_0_.refs_2_, bf16[1024,1024]{1,0:T(8,128)(2,1)S(1)} %collective-permute-done.14.refs_1_, f32[32,64]{1,0:T(8,128)S(1)} %tower.6.refs_2_, bf16[128,1024]{1,0:T(8,128)(2,1)S(1)} %collective-permute-done.23.refs_0_.refs_3_, ...), custom_call_target="tpu_custom_call" | custom-call | flops 3221225472 | bytes 10000000 | tf_op jit(solution)/shard_map/tower/pallas_call | solution.py:319
  94.5 4.5 %all-to-all-start.1 = ((f32[32,1,64]{2,1,0:T(1,128)}), f32[32,1,64]{2,1,0:T(1,128)S(1)}, u32[]{:S(2)}, u32[]{:S(2)}) async-start(f32[32,1,64]{2,1,0:T(1,128)} %bitcast.10), calls=%async_computation.1 | async-start | bytes 32768 | tf_op jit(solution)/shard_map/all_to_all | solution.py:372
  99.1 6.9 %update.1 = f32[2048,512]{1,0:T(8,128)} custom-call(s32[32,64]{1,0:T(8,128)} %bitcast.21, bf16[1024,1024]{1,0:T(8,128)(2,1)} %copy-done, f32[2048,512]{1,0:T(8,128)} %states_ref.1), custom_call_target="tpu_custom_call" | custom-call | flops 4000000000 | bytes 10000000 | tf_op jit(solution)/shard_map/update/pallas_call | solution.py:237
  (63 shorter events, 9.8 us)
Async XLA Ops:
  3.3 4.6 %collective-permute-start.3 = (bf16[2,16,1024]{2,1,0:T(8,128)(2,1)}, bf16[2,16,1024]{2,1,0:T(8,128)(2,1)S(1)}, u32[]{:S(2)}, u32[]{:S(2)}) collective-permute-start(bf16[2,16,1024]{2,1,0:T(8,128)(2,1)} %bitcast.26), channel_id=1, source_target_pairs={{0,1},{1,0},{2,3},{3,2},{4,5},{5,4},{6,7},{7,6},{8,9},{9,8},{10,11... | collective-permute-start | bytes 196616 | tf_op jit(solution)/shard_map/ppermute | solution.py:376
  3.9 14.0 %collective-permute-start = (bf16[128,1024]{1,0:T(8,128)(2,1)S(1)}, bf16[128,1024]{1,0:T(8,128)(2,1)S(1)}, u32[]{:S(2)}, u32[]{:S(2)}) collective-permute-start(bf16[128,1024]{1,0:T(8,128)(2,1)S(1)} %copy-done.6), channel_id=1, source_target_pairs={{0,8},{1,9},{2,10},{3,11},{4,12},{5,13},{6,14},{7,15},{8,0},{9,1},... | collective-permute-start | bytes 786440 | tf_op jit(solution)/shard_map/ppermute | solution.py:376
  6.4 12.9 %collective-permute-start.1 = (bf16[128,1024]{1,0:T(8,128)(2,1)S(1)}, bf16[128,1024]{1,0:T(8,128)(2,1)S(1)}, u32[]{:S(2)}, u32[]{:S(2)}) collective-permute-start(bf16[128,1024]{1,0:T(8,128)(2,1)S(1)} %copy-done.6), channel_id=1, source_target_pairs={{0,16},{1,17},{2,18},{3,19},{4,20},{5,21},{6,22},{7,23},{8,24},{9,... | collective-permute-start | bytes 786440 | tf_op jit(solution)/shard_map/ppermute | solution.py:376
  8.8 12.0 %collective-permute-start.4 = (bf16[64,1024]{1,0:T(8,128)(2,1)S(1)}, bf16[64,1024]{1,0:T(8,128)(2,1)S(1)}, u32[]{:S(2)}, u32[]{:S(2)}) collective-permute-start(bf16[64,1024]{1,0:T(8,128)(2,1)S(1)} %bitcast.15), channel_id=1, source_target_pairs={{0,2},{1,3},{2,4},{3,5},{4,6},{5,7},{6,0},{7,1},{8,10},{9,11},{10,... | collective-permute-start | bytes 393224 | tf_op jit(solution)/shard_map/ppermute | solution.py:376
  10.5 11.9 %all-to-all-start = ((s32[32,1,64]{2,1,0:T(1,128)}), s32[32,1,64]{2,1,0:T(1,128)S(1)}, u32[]{:S(2)}, u32[]{:S(2)}) async-start(s32[32,1,64]{2,1,0:T(1,128)} %bitcast.24), calls=%async_computation | async-start | bytes 32768 | tf_op jit(solution)/shard_map/all_to_all | solution.py:372
  13.7 19.4 %collective-permute-start.2 = (bf16[128,1024]{1,0:T(8,128)(2,1)S(1)}, bf16[128,1024]{1,0:T(8,128)(2,1)S(1)}, u32[]{:S(2)}, u32[]{:S(2)}) collective-permute-start(bf16[128,1024]{1,0:T(8,128)(2,1)S(1)} %copy-done.6), channel_id=1, source_target_pairs={{0,2},{1,3},{2,4},{3,5},{4,6},{5,7},{6,0},{7,1},{8,10},{9,11},{10,... | collective-permute-start | bytes 786440 | tf_op jit(solution)/shard_map/ppermute | solution.py:376
  15.5 14.5 %collective-permute-start.5 = (bf16[64,1024]{1,0:T(8,128)(2,1)S(1)}, bf16[64,1024]{1,0:T(8,128)(2,1)S(1)}, u32[]{:S(2)}, u32[]{:S(2)}) collective-permute-start(bf16[64,1024]{1,0:T(8,128)(2,1)S(1)} %bitcast.16), channel_id=1, source_target_pairs={{0,4},{1,5},{2,6},{3,7},{4,0},{5,1},{6,2},{7,3},{8,12},{9,13},{10,... | collective-permute-start | bytes 393224 | tf_op jit(solution)/shard_map/ppermute | solution.py:376
  17.9 12.0 %collective-permute-start.6 = (bf16[64,1024]{1,0:T(8,128)(2,1)S(1)}, bf16[64,1024]{1,0:T(8,128)(2,1)S(1)}, u32[]{:S(2)}, u32[]{:S(2)}) collective-permute-start(bf16[64,1024]{1,0:T(8,128)(2,1)S(1)} %bitcast.17), channel_id=1, source_target_pairs={{0,6},{1,7},{2,0},{3,1},{4,2},{5,3},{6,4},{7,5},{8,14},{9,15},{10,... | collective-permute-start | bytes 393224 | tf_op jit(solution)/shard_map/ppermute | solution.py:376
  19.4 17.0 %collective-permute-start.12 = (bf16[64,1024]{1,0:T(8,128)(2,1)S(1)}, bf16[64,1024]{1,0:T(8,128)(2,1)S(1)}, u32[]{:S(2)}, u32[]{:S(2)}) collective-permute-start(bf16[64,1024]{1,0:T(8,128)(2,1)S(1)} %get-tuple-element.19), channel_id=1, source_target_pairs={{0,8},{1,9},{2,10},{3,11},{4,12},{5,13},{6,14},{7,15},{8,0},{9,1},... | collective-permute-start | bytes 393224 | tf_op jit(solution)/shard_map/ppermute | solution.py:376
  20.9 16.1 %collective-permute-start.13 = (bf16[64,1024]{1,0:T(8,128)(2,1)S(1)}, bf16[64,1024]{1,0:T(8,128)(2,1)S(1)}, u32[]{:S(2)}, u32[]{:S(2)}) collective-permute-start(bf16[64,1024]{1,0:T(8,128)(2,1)S(1)} %get-tuple-element.20), channel_id=1, source_target_pairs={{0,16},{1,17},{2,18},{3,19},{4,20},{5,21},{6,22},{7,23},{8,24},{9,... | collective-permute-start | bytes 393224 | tf_op jit(solution)/shard_map/ppermute | solution.py:376
  30.0 20.7 %copy-start.4 = (bf16[512,1536]{1,0:T(8,128)(2,1)S(1)}, bf16[512,1536]{1,0:T(8,128)(2,1)}, u32[]{:S(2)}) copy-start(bf16[512,1536]{1,0:T(8,128)(2,1)} %gin_hbm.1) | copy-start | bytes 4718596
  30.0 20.7 %collective-permute-start.7 = (bf16[256,1024]{1,0:T(8,128)(2,1)S(1)}, bf16[256,1024]{1,0:T(8,128)(2,1)S(1)}, u32[]{:S(2)}, u32[]{:S(2)}) collective-permute-start(bf16[256,1024]{1,0:T(8,128)(2,1)S(1)} %place.7.refs_7_.refs_8_), channel_id=1, source_target_pairs={{0,8},{1,9},{2,10},{3,11},{4,12},{5,13},{6,14},{7,15},{8,0},{9,1},... | collective-permute-start | bytes 1572872 | tf_op jit(solution)/shard_map/ppermute | solution.py:376
  31.6 19.1 %collective-permute-start.8 = (bf16[256,1024]{1,0:T(8,128)(2,1)S(1)}, bf16[256,1024]{1,0:T(8,128)(2,1)S(1)}, u32[]{:S(2)}, u32[]{:S(2)}) collective-permute-start(bf16[256,1024]{1,0:T(8,128)(2,1)S(1)} %place.7.refs_7_.refs_8_), channel_id=1, source_target_pairs={{0,16},{1,17},{2,18},{3,19},{4,20},{5,21},{6,22},{7,23},{8,24},{9,... | collective-permute-start | bytes 1572872 | tf_op jit(solution)/shard_map/ppermute | solution.py:376
  33.1 9.6 %collective-permute-start.11 = (bf16[128,1024]{1,0:T(8,128)(2,1)S(1)}, bf16[128,1024]{1,0:T(8,128)(2,1)S(1)}, u32[]{:S(2)}, u32[]{:S(2)}) collective-permute-start(bf16[128,1024]{1,0:T(8,128)(2,1)S(1)} %collective-permute-done.2.refs_2_.refs_3_), channel_id=1, source_target_pairs={{0,2},{1,3},{2,4},{3,5},{4,6},{5,7},{6,0},{7,1},{8,10},{9,11},{10,... | collective-permute-start | bytes 786440 | tf_op jit(solution)/shard_map/ppermute | solution.py:376
  36.4 14.3 %collective-permute-start.10 = (bf16[128,1024]{1,0:T(8,128)(2,1)S(1)}, bf16[128,1024]{1,0:T(8,128)(2,1)S(1)}, u32[]{:S(2)}, u32[]{:S(2)}) collective-permute-start(bf16[128,1024]{1,0:T(8,128)(2,1)S(1)} %collective-permute-done.2.refs_2_.refs_3_), channel_id=1, source_target_pairs={{0,16},{1,17},{2,18},{3,19},{4,20},{5,21},{6,22},{7,23},{8,24},{9,... | collective-permute-start | bytes 786440 | tf_op jit(solution)/shard_map/ppermute | solution.py:376
  36.9 13.8 %collective-permute-start.9 = (bf16[128,1024]{1,0:T(8,128)(2,1)S(1)}, bf16[128,1024]{1,0:T(8,128)(2,1)S(1)}, u32[]{:S(2)}, u32[]{:S(2)}) collective-permute-start(bf16[128,1024]{1,0:T(8,128)(2,1)S(1)} %collective-permute-done.2.refs_2_.refs_3_), channel_id=1, source_target_pairs={{0,8},{1,9},{2,10},{3,11},{4,12},{5,13},{6,14},{7,15},{8,0},{9,1},... | collective-permute-start | bytes 786440 | tf_op jit(solution)/shard_map/ppermute | solution.py:376
  54.8 34.2 %copy-start = (bf16[1024,1024]{1,0:T(8,128)(2,1)}, bf16[1024,1024]{1,0:T(8,128)(2,1)S(1)}, u32[]{:S(2)}) copy-start(bf16[1024,1024]{1,0:T(8,128)(2,1)S(1)} %cell.1.joined_ref.refs_0_.refs_2_) | copy-start | bytes 6291460
  54.8 11.3 %collective-permute-start.14 = (bf16[1024,1024]{1,0:T(8,128)(2,1)S(1)}, bf16[1024,1024]{1,0:T(8,128)(2,1)S(1)}, u32[]{:S(2)}, u32[]{:S(2)}) collective-permute-start(bf16[1024,1024]{1,0:T(8,128)(2,1)S(1)} %cell.1.joined_ref.refs_0_.refs_2_), channel_id=1, source_target_pairs={{0,1},{1,0},{2,3},{3,2},{4,5},{5,4},{6,7},{7,6},{8,9},{9,8},{10,11... | collective-permute-start | bytes 6291464 | tf_op jit(solution)/shard_map/ppermute | solution.py:376
  54.9 9.2 %collective-permute-start.15 = (bf16[128,1024]{1,0:T(8,128)(2,1)S(1)}, bf16[128,1024]{1,0:T(8,128)(2,1)S(1)}, u32[]{:S(2)}, u32[]{:S(2)}) collective-permute-start(bf16[128,1024]{1,0:T(8,128)(2,1)S(1)} %get-tuple-element.21), channel_id=1, source_target_pairs={{0,8},{1,9},{2,10},{3,11},{4,12},{5,13},{6,14},{7,15},{8,0},{9,1},... | collective-permute-start | bytes 786440 | tf_op jit(solution)/shard_map/ppermute | solution.py:376
  55.5 10.1 %collective-permute-start.16 = (bf16[128,1024]{1,0:T(8,128)(2,1)S(1)}, bf16[128,1024]{1,0:T(8,128)(2,1)S(1)}, u32[]{:S(2)}, u32[]{:S(2)}) collective-permute-start(bf16[128,1024]{1,0:T(8,128)(2,1)S(1)} %get-tuple-element.22), channel_id=1, source_target_pairs={{0,16},{1,17},{2,18},{3,19},{4,20},{5,21},{6,22},{7,23},{8,24},{9,... | collective-permute-start | bytes 786440 | tf_op jit(solution)/shard_map/ppermute | solution.py:376
  57.0 14.8 %collective-permute-start.23 = (bf16[128,1024]{1,0:T(8,128)(2,1)S(1)}, bf16[128,1024]{1,0:T(8,128)(2,1)S(1)}, u32[]{:S(2)}, u32[]{:S(2)}) collective-permute-start(bf16[128,1024]{1,0:T(8,128)(2,1)S(1)} %collective-permute-done.11.refs_4_.refs_3_), channel_id=1, source_target_pairs={{0,2},{1,3},{2,4},{3,5},{4,6},{5,7},{6,0},{7,1},{8,10},{9,11},{10,... | collective-permute-start | bytes 786440 | tf_op jit(solution)/shard_map/ppermute | solution.py:376
  60.4 12.8 %collective-permute-start.19 = (bf16[128,1024]{1,0:T(8,128)(2,1)S(1)}, bf16[128,1024]{1,0:T(8,128)(2,1)S(1)}, u32[]{:S(2)}, u32[]{:S(2)}) collective-permute-start(bf16[128,1024]{1,0:T(8,128)(2,1)S(1)} %collective-permute-done.11.refs_4_.refs_3_), channel_id=1, source_target_pairs={{0,8},{1,9},{2,10},{3,11},{4,12},{5,13},{6,14},{7,15},{8,0},{9,1},... | collective-permute-start | bytes 786440 | tf_op jit(solution)/shard_map/ppermute | solution.py:376
  64.1 10.5 %collective-permute-start.20 = (bf16[128,1024]{1,0:T(8,128)(2,1)S(1)}, bf16[128,1024]{1,0:T(8,128)(2,1)S(1)}, u32[]{:S(2)}, u32[]{:S(2)}) collective-permute-start(bf16[128,1024]{1,0:T(8,128)(2,1)S(1)} %collective-permute-done.11.refs_4_.refs_3_), channel_id=1, source_target_pairs={{0,16},{1,17},{2,18},{3,19},{4,20},{5,21},{6,22},{7,23},{8,24},{9,... | collective-permute-start | bytes 786440 | tf_op jit(solution)/shard_map/ppermute | solution.py:376
  65.6 9.7 %collective-permute-start.17 = (bf16[64,1024]{1,0:T(8,128)(2,1)S(1)}, bf16[64,1024]{1,0:T(8,128)(2,1)S(1)}, u32[]{:S(2)}, u32[]{:S(2)}) collective-permute-start(bf16[64,1024]{1,0:T(8,128)(2,1)S(1)} %get-tuple-element.23), channel_id=1, source_target_pairs={{0,8},{1,9},{2,10},{3,11},{4,12},{5,13},{6,14},{7,15},{8,0},{9,1},... | collective-permute-start | bytes 393224 | tf_op jit(solution)/shard_map/ppermute | solution.py:376
  66.1 10.0 %collective-permute-start.18 = (bf16[64,1024]{1,0:T(8,128)(2,1)S(1)}, bf16[64,1024]{1,0:T(8,128)(2,1)S(1)}, u32[]{:S(2)}, u32[]{:S(2)}) collective-permute-start(bf16[64,1024]{1,0:T(8,128)(2,1)S(1)} %get-tuple-element.24), channel_id=1, source_target_pairs={{0,16},{1,17},{2,18},{3,19},{4,20},{5,21},{6,22},{7,23},{8,24},{9,... | collective-permute-start | bytes 393224 | tf_op jit(solution)/shard_map/ppermute | solution.py:376
  71.9 9.1 %collective-permute-start.24 = (bf16[128,1024]{1,0:T(8,128)(2,1)S(1)}, bf16[128,1024]{1,0:T(8,128)(2,1)S(1)}, u32[]{:S(2)}, u32[]{:S(2)}) collective-permute-start(bf16[128,1024]{1,0:T(8,128)(2,1)S(1)} %place.12), channel_id=1, source_target_pairs={{0,8},{1,9},{2,10},{3,11},{4,12},{5,13},{6,14},{7,15},{8,0},{9,1},... | collective-permute-start | bytes 786440 | tf_op jit(solution)/shard_map/ppermute | solution.py:376
  73.2 8.3 %collective-permute-start.25 = (bf16[128,1024]{1,0:T(8,128)(2,1)S(1)}, bf16[128,1024]{1,0:T(8,128)(2,1)S(1)}, u32[]{:S(2)}, u32[]{:S(2)}) collective-permute-start(bf16[128,1024]{1,0:T(8,128)(2,1)S(1)} %place.12), channel_id=1, source_target_pairs={{0,16},{1,17},{2,18},{3,19},{4,20},{5,21},{6,22},{7,23},{8,24},{9,... | collective-permute-start | bytes 786440 | tf_op jit(solution)/shard_map/ppermute | solution.py:376
  74.7 9.2 %collective-permute-start.21 = (bf16[64,1024]{1,0:T(8,128)(2,1)S(1)}, bf16[64,1024]{1,0:T(8,128)(2,1)S(1)}, u32[]{:S(2)}, u32[]{:S(2)}) collective-permute-start(bf16[64,1024]{1,0:T(8,128)(2,1)S(1)} %get-tuple-element.25), channel_id=1, source_target_pairs={{0,8},{1,9},{2,10},{3,11},{4,12},{5,13},{6,14},{7,15},{8,0},{9,1},... | collective-permute-start | bytes 393224 | tf_op jit(solution)/shard_map/ppermute | solution.py:376
  75.3 8.5 %collective-permute-start.22 = (bf16[64,1024]{1,0:T(8,128)(2,1)S(1)}, bf16[64,1024]{1,0:T(8,128)(2,1)S(1)}, u32[]{:S(2)}, u32[]{:S(2)}) collective-permute-start(bf16[64,1024]{1,0:T(8,128)(2,1)S(1)} %get-tuple-element.26), channel_id=1, source_target_pairs={{0,16},{1,17},{2,18},{3,19},{4,20},{5,21},{6,22},{7,23},{8,24},{9,... | collective-permute-start | bytes 393224 | tf_op jit(solution)/shard_map/ppermute | solution.py:376
  81.5 7.5 %collective-permute-start.26 = (bf16[64,1024]{1,0:T(8,128)(2,1)S(1)}, bf16[64,1024]{1,0:T(8,128)(2,1)S(1)}, u32[]{:S(2)}, u32[]{:S(2)}) collective-permute-start(bf16[64,1024]{1,0:T(8,128)(2,1)S(1)} %get-tuple-element.27), channel_id=1, source_target_pairs={{0,8},{1,9},{2,10},{3,11},{4,12},{5,13},{6,14},{7,15},{8,0},{9,1},... | collective-permute-start | bytes 393224 | tf_op jit(solution)/shard_map/ppermute | solution.py:376
  82.3 6.6 %collective-permute-start.27 = (bf16[64,1024]{1,0:T(8,128)(2,1)S(1)}, bf16[64,1024]{1,0:T(8,128)(2,1)S(1)}, u32[]{:S(2)}, u32[]{:S(2)}) collective-permute-start(bf16[64,1024]{1,0:T(8,128)(2,1)S(1)} %get-tuple-element.28), channel_id=1, source_target_pairs={{0,16},{1,17},{2,18},{3,19},{4,20},{5,21},{6,22},{7,23},{8,24},{9,... | collective-permute-start | bytes 393224 | tf_op jit(solution)/shard_map/ppermute | solution.py:376
  94.5 11.7 %all-to-all-start.1 = ((f32[32,1,64]{2,1,0:T(1,128)}), f32[32,1,64]{2,1,0:T(1,128)S(1)}, u32[]{:S(2)}, u32[]{:S(2)}) async-start(f32[32,1,64]{2,1,0:T(1,128)} %bitcast.10), calls=%async_computation.1 | async-start | bytes 32768 | tf_op jit(solution)/shard_map/all_to_all | solution.py:372
  (6 other events, 61.2 us)

commit v4 on v3

--- a/solution.py
+++ b/solution.py
@@ -10,6 +10,7 @@
 AXES = ("owner", "worker")
 LANES = 128
 CHUNK = 256
+WIDE = 512
 F32 = jnp.float32
 BF16 = jnp.bfloat16
 I32 = jnp.int32
@@ -178,8 +179,8 @@
     for copy in copies:
         copy.wait()
     n, width = prior_ref.shape
-    for k in range(n // CHUNK):
-        at = slice(k * CHUNK, (k + 1) * CHUNK)
+    for k in range(n // WIDE):
+        at = slice(k * WIDE, (k + 1) * WIDE)
         prior = prior_ref[at, :]
         joined_ref[at, width:] = inputs_ref[at, :]
         gh = dot(prior, gst_ref[...])

time: 107 us -> 108 us (level)
  no operation moved by 1% of the time
where the time goes in v4:
time: 108 us; the launch traced here: 107 us
  starting transfers between devices  46.4 us (43%)
  Pallas kernels  43.5 us (40%)
  waiting for transfers between devices  13.3 us (12%)
  local copies, waits for them, and re-layouts  2.25 us (2%)
    ppermute x28, starting transfers between devices, send(): return lax.ppermute(x, AXES, [(d, to(d)) for d in range(devices)])  38.7 us
    pallas_call x4, Pallas kernels, step(): pl.pallas_call(functools.partial(step_kernel, n_in=len(in_arrays), n_out=...  20.5 us
    ppermute x28, waiting for transfers between devices, send(): return lax.ppermute(x, AXES, [(d, to(d)) for d in range(devices)])  13.1 us
    pallas_call x2, Pallas kernels, fetch(): pl.pallas_call(functools.partial(fetch_kernel, cap=cap, column=column), o...  8.22 us
    all_to_all x2, starting transfers between devices, exchange(): return lax.all_to_all(x, AXES, split_axis=0, concat_axis=0, tiled=True)  7.75 us
    pallas_call x1, Pallas kernels, update(): pl.pallas_call(functools.partial(update_kernel, cap=cap), out_shape=jax.S...  6.92 us
    pallas_call x1, Pallas kernels, cell(): pl.pallas_call(cell_kernel, out_shape=jax.ShapeDtypeStruct((n, 2 * width)...  4.21 us
    pallas_call x1, Pallas kernels, route(): pl.pallas_call(functools.partial(route_kernel, shards=shards, cap=cap, ro...  2.69 us
  transfers between devices with their start and end apart: 30, of which 5 were waited for; matrix products, arithmetic and copies ran while one was open for 1% of the time, Pallas kernels for 28%

profile of v4, /device:TPU:0, one launch (start us, length us, event | category | flops | bytes accessed | tf_op | source)
XLA Modules:
  0.0 107.2 jit_solution(13718770336051251695)
XLA Ops:
  0.6 2.7 %route.1 = (s32[32,64]{1,0:T(8,128)}, s32[2,512]{1,0:T(2,128)}, bf16[32,1024]{1,0:T(8,128)(2,1)}, bf16[32,1024]{1,0:T(8,128)(2,1)}) custom-call(s32[512,128]{1,0:T(8,128)} %bitcast.25, s32[1,512]{1,0:T(1,128)} %bitcast.27, s32[1,512]{1,0:T(1,128)} %bitcast.28, bf16[16,4096]{1,0:T(8,128)(2,1)} %refs_3_.1), custom_call_target="tpu_custom_call" | custom-call | flops 1000000000 | bytes 1000000 | tf_op jit(solution)/shard_map/route/pallas_call | solution.py:107
  3.9 2.6 %collective-permute-start = (bf16[128,1024]{1,0:T(8,128)(2,1)S(1)}, bf16[128,1024]{1,0:T(8,128)(2,1)S(1)}, u32[]{:S(2)}, u32[]{:S(2)}) collective-permute-start(bf16[128,1024]{1,0:T(8,128)(2,1)S(1)} %copy-done.6), channel_id=1, source_target_pairs={{0,8},{1,9},{2,10},{3,11},{4,12},{5,13},{6,14},{7,15},{8,0},{9,1},... | collective-permute-start | bytes 786440 | tf_op jit(solution)/shard_map/ppermute | solution.py:377
  6.4 1.5 %collective-permute-start.1 = (bf16[128,1024]{1,0:T(8,128)(2,1)S(1)}, bf16[128,1024]{1,0:T(8,128)(2,1)S(1)}, u32[]{:S(2)}, u32[]{:S(2)}) collective-permute-start(bf16[128,1024]{1,0:T(8,128)(2,1)S(1)} %copy-done.6), channel_id=1, source_target_pairs={{0,16},{1,17},{2,18},{3,19},{4,20},{5,21},{6,22},{7,23},{8,24},{9,... | collective-permute-start | bytes 786440 | tf_op jit(solution)/shard_map/ppermute | solution.py:377
  8.8 1.6 %collective-permute-start.4 = (bf16[64,1024]{1,0:T(8,128)(2,1)S(1)}, bf16[64,1024]{1,0:T(8,128)(2,1)S(1)}, u32[]{:S(2)}, u32[]{:S(2)}) collective-permute-start(bf16[64,1024]{1,0:T(8,128)(2,1)S(1)} %bitcast.15), channel_id=1, source_target_pairs={{0,2},{1,3},{2,4},{3,5},{4,6},{5,7},{6,0},{7,1},{8,10},{9,11},{10,... | collective-permute-start | bytes 393224 | tf_op jit(solution)/shard_map/ppermute | solution.py:377
  10.5 3.2 %all-to-all-start = ((s32[32,1,64]{2,1,0:T(1,128)}), s32[32,1,64]{2,1,0:T(1,128)S(1)}, u32[]{:S(2)}, u32[]{:S(2)}) async-start(s32[32,1,64]{2,1,0:T(1,128)} %bitcast.24), calls=%async_computation | async-start | bytes 32768 | tf_op jit(solution)/shard_map/all_to_all | solution.py:373
  13.7 1.8 %collective-permute-start.2 = (bf16[128,1024]{1,0:T(8,128)(2,1)S(1)}, bf16[128,1024]{1,0:T(8,128)(2,1)S(1)}, u32[]{:S(2)}, u32[]{:S(2)}) collective-permute-start(bf16[128,1024]{1,0:T(8,128)(2,1)S(1)} %copy-done.6), channel_id=1, source_target_pairs={{0,2},{1,3},{2,4},{3,5},{4,6},{5,7},{6,0},{7,1},{8,10},{9,11},{10,... | collective-permute-start | bytes 786440 | tf_op jit(solution)/shard_map/ppermute | solution.py:377
  15.5 2.4 %collective-permute-start.5 = (bf16[64,1024]{1,0:T(8,128)(2,1)S(1)}, bf16[64,1024]{1,0:T(8,128)(2,1)S(1)}, u32[]{:S(2)}, u32[]{:S(2)}) collective-permute-start(bf16[64,1024]{1,0:T(8,128)(2,1)S(1)} %bitcast.16), channel_id=1, source_target_pairs={{0,4},{1,5},{2,6},{3,7},{4,0},{5,1},{6,2},{7,3},{8,12},{9,13},{10,... | collective-permute-start | bytes 393224 | tf_op jit(solution)/shard_map/ppermute | solution.py:377
  17.9 1.4 %collective-permute-start.6 = (bf16[64,1024]{1,0:T(8,128)(2,1)S(1)}, bf16[64,1024]{1,0:T(8,128)(2,1)S(1)}, u32[]{:S(2)}, u32[]{:S(2)}) collective-permute-start(bf16[64,1024]{1,0:T(8,128)(2,1)S(1)} %bitcast.17), channel_id=1, source_target_pairs={{0,6},{1,7},{2,0},{3,1},{4,2},{5,3},{6,4},{7,5},{8,14},{9,15},{10,... | collective-permute-start | bytes 393224 | tf_op jit(solution)/shard_map/ppermute | solution.py:377
  19.4 1.5 %collective-permute-start.12 = (bf16[64,1024]{1,0:T(8,128)(2,1)S(1)}, bf16[64,1024]{1,0:T(8,128)(2,1)S(1)}, u32[]{:S(2)}, u32[]{:S(2)}) collective-permute-start(bf16[64,1024]{1,0:T(8,128)(2,1)S(1)} %get-tuple-element.19), channel_id=1, source_target_pairs={{0,8},{1,9},{2,10},{3,11},{4,12},{5,13},{6,14},{7,15},{8,0},{9,1},... | collective-permute-start | bytes 393224 | tf_op jit(solution)/shard_map/ppermute | solution.py:377
  20.9 1.5 %collective-permute-start.13 = (bf16[64,1024]{1,0:T(8,128)(2,1)S(1)}, bf16[64,1024]{1,0:T(8,128)(2,1)S(1)}, u32[]{:S(2)}, u32[]{:S(2)}) collective-permute-start(bf16[64,1024]{1,0:T(8,128)(2,1)S(1)} %get-tuple-element.20), channel_id=1, source_target_pairs={{0,16},{1,17},{2,18},{3,19},{4,20},{5,21},{6,22},{7,23},{8,24},{9,... | collective-permute-start | bytes 393224 | tf_op jit(solution)/shard_map/ppermute | solution.py:377
  22.4 2.2 %copy-done.3 = f32[2048,512]{1,0:T(8,128)S(1)} copy-done((f32[2048,512]{1,0:T(8,128)S(1)}, f32[2048,512]{1,0:T(8,128)}, u32[]{:S(2)}) %copy-start.3) | copy-done | bytes 4194328
  24.6 3.0 %fetch.2.refs_3_.prior_ref = bf16[1024,512]{1,0:T(8,128)(2,1)S(1)} custom-call(s32[32,64]{1,0:T(8,128)S(1)} %bitcast.19, f32[2048,512]{1,0:T(8,128)S(1)} %copy-done.3), custom_call_target="tpu_custom_call" | custom-call | flops 10737418240 | bytes 5000000 | tf_op jit(solution)/shard_map/fetch/pallas_call | solution.py:162
  27.6 2.4 %collective-permute-done.5.refs_2_ = bf16[64,1024]{1,0:T(8,128)(2,1)S(1)} collective-permute-done((bf16[64,1024]{1,0:T(8,128)(2,1)S(1)}, bf16[64,1024]{1,0:T(8,128)(2,1)S(1)}, u32[]{:S(2)}, u32[]{:S(2)}) %collective-permute-start.5) | collective-permute-done | bytes 131104 | tf_op jit(solution)/shard_map/ppermute | solution.py:377
  30.0 1.6 %collective-permute-start.7 = (bf16[256,1024]{1,0:T(8,128)(2,1)S(1)}, bf16[256,1024]{1,0:T(8,128)(2,1)S(1)}, u32[]{:S(2)}, u32[]{:S(2)}) collective-permute-start(bf16[256,1024]{1,0:T(8,128)(2,1)S(1)} %place.7.refs_7_.refs_8_), channel_id=1, source_target_pairs={{0,8},{1,9},{2,10},{3,11},{4,12},{5,13},{6,14},{7,15},{8,0},{9,1},... | collective-permute-start | bytes 1572872 | tf_op jit(solution)/shard_map/ppermute | solution.py:377
  31.6 1.5 %collective-permute-start.8 = (bf16[256,1024]{1,0:T(8,128)(2,1)S(1)}, bf16[256,1024]{1,0:T(8,128)(2,1)S(1)}, u32[]{:S(2)}, u32[]{:S(2)}) collective-permute-start(bf16[256,1024]{1,0:T(8,128)(2,1)S(1)} %place.7.refs_7_.refs_8_), channel_id=1, source_target_pairs={{0,16},{1,17},{2,18},{3,19},{4,20},{5,21},{6,22},{7,23},{8,24},{9,... | collective-permute-start | bytes 1572872 | tf_op jit(solution)/shard_map/ppermute | solution.py:377
  33.1 3.3 %collective-permute-start.11 = (bf16[128,1024]{1,0:T(8,128)(2,1)S(1)}, bf16[128,1024]{1,0:T(8,128)(2,1)S(1)}, u32[]{:S(2)}, u32[]{:S(2)}) collective-permute-start(bf16[128,1024]{1,0:T(8,128)(2,1)S(1)} %collective-permute-done.2.refs_2_.refs_3_), channel_id=1, source_target_pairs={{0,2},{1,3},{2,4},{3,5},{4,6},{5,7},{6,0},{7,1},{8,10},{9,11},{10,... | collective-permute-start | bytes 786440 | tf_op jit(solution)/shard_map/ppermute | solution.py:377
  37.4 5.2 %fetch.3.inputs_ref = bf16[1024,512]{1,0:T(8,128)(2,1)S(1)} custom-call(s32[32,64]{1,0:T(8,128)S(1)} %bitcast.20, bf16[4096,512]{1,0:T(8,128)(2,1)S(1)} %copy-done.2, bf16[128,1024]{1,0:T(8,128)(2,1)S(1)} %collective-permute-done.refs_0_.refs_1_.refs_3_, bf16[128,1024]{1,0:T(8,128)(2,1)S(1)} %collective-permute-done.1.refs_1_.refs_0_.refs_4_, ...), custom_call_target="tpu_custom_call" | custom-call | flops 21474836480 | bytes 5000000 | tf_op jit(solution)/shard_map/fetch/pallas_call | solution.py:162
  42.7 8.0 %collective-permute-done.10.refs_3_.refs_0_.refs_5_ = bf16[128,1024]{1,0:T(8,128)(2,1)S(1)} collective-permute-done((bf16[128,1024]{1,0:T(8,128)(2,1)S(1)}, bf16[128,1024]{1,0:T(8,128)(2,1)S(1)}, u32[]{:S(2)}, u32[]{:S(2)}) %collective-permute-start.10) | collective-permute-done | bytes 262176 | tf_op jit(solution)/shard_map/ppermute | solution.py:377
  50.7 4.2 %cell.1.joined_ref.refs_0_.refs_2_ = bf16[1024,1024]{1,0:T(8,128)(2,1)S(1)} custom-call(bf16[1024,512]{1,0:T(8,128)(2,1)S(1)} %fetch.2.refs_3_.prior_ref, bf16[1024,512]{1,0:T(8,128)(2,1)S(1)} %fetch.3.inputs_ref, bf16[512,1536]{1,0:T(8,128)(2,1)S(1)} %copy-done.4, bf16[512,1536]{1,0:T(8,128)(2,1)S(1)} %copy-done.5, ...), custom_call_target="tpu_custom_call" | custom-call | flops 4000000000 | bytes 6000000 | tf_op jit(solution)/shard_map/cell/pallas_call | solution.py:197
  55.7 1.5 %collective-permute-start.16 = (bf16[128,1024]{1,0:T(8,128)(2,1)S(1)}, bf16[128,1024]{1,0:T(8,128)(2,1)S(1)}, u32[]{:S(2)}, u32[]{:S(2)}) collective-permute-start(bf16[128,1024]{1,0:T(8,128)(2,1)S(1)} %get-tuple-element.22), channel_id=1, source_target_pairs={{0,16},{1,17},{2,18},{3,19},{4,20},{5,21},{6,22},{7,23},{8,24},{9,... | collective-permute-start | bytes 786440 | tf_op jit(solution)/shard_map/ppermute | solution.py:377
  57.2 3.4 %collective-permute-start.23 = (bf16[128,1024]{1,0:T(8,128)(2,1)S(1)}, bf16[128,1024]{1,0:T(8,128)(2,1)S(1)}, u32[]{:S(2)}, u32[]{:S(2)}) collective-permute-start(bf16[128,1024]{1,0:T(8,128)(2,1)S(1)} %collective-permute-done.11.refs_4_.refs_3_), channel_id=1, source_target_pairs={{0,2},{1,3},{2,4},{3,5},{4,6},{5,7},{6,0},{7,1},{8,10},{9,11},{10,... | collective-permute-start | bytes 786440 | tf_op jit(solution)/shard_map/ppermute | solution.py:377
  60.6 1.5 %collective-permute-start.19 = (bf16[128,1024]{1,0:T(8,128)(2,1)S(1)}, bf16[128,1024]{1,0:T(8,128)(2,1)S(1)}, u32[]{:S(2)}, u32[]{:S(2)}) collective-permute-start(bf16[128,1024]{1,0:T(8,128)(2,1)S(1)} %collective-permute-done.11.refs_4_.refs_3_), channel_id=1, source_target_pairs={{0,8},{1,9},{2,10},{3,11},{4,12},{5,13},{6,14},{7,15},{8,0},{9,1},... | collective-permute-start | bytes 786440 | tf_op jit(solution)/shard_map/ppermute | solution.py:377
  62.1 2.2 %collective-permute-done.15.refs_10_.refs_11_ = bf16[128,1024]{1,0:T(8,128)(2,1)S(1)} collective-permute-done((bf16[128,1024]{1,0:T(8,128)(2,1)S(1)}, bf16[128,1024]{1,0:T(8,128)(2,1)S(1)}, u32[]{:S(2)}, u32[]{:S(2)}) %collective-permute-start.15) | collective-permute-done | bytes 262176 | tf_op jit(solution)/shard_map/ppermute | solution.py:377
  64.3 1.5 %collective-permute-start.20 = (bf16[128,1024]{1,0:T(8,128)(2,1)S(1)}, bf16[128,1024]{1,0:T(8,128)(2,1)S(1)}, u32[]{:S(2)}, u32[]{:S(2)}) collective-permute-start(bf16[128,1024]{1,0:T(8,128)(2,1)S(1)} %collective-permute-done.11.refs_4_.refs_3_), channel_id=1, source_target_pairs={{0,16},{1,17},{2,18},{3,19},{4,20},{5,21},{6,22},{7,23},{8,24},{9,... | collective-permute-start | bytes 786440 | tf_op jit(solution)/shard_map/ppermute | solution.py:377
  67.1 4.9 %tower.4.refs_2_.refs_1_ = f32[32,64]{1,0:T(8,128)S(1)} custom-call(bf16[1024,1024]{1,0:T(8,128)(2,1)S(1)} %cell.1.joined_ref.refs_0_.refs_2_, bf16[1024,1024]{1,0:T(8,128)(2,1)S(1)} %collective-permute-done.14.refs_1_, bf16[128,1024]{1,0:T(8,128)(2,1)S(1)} %copy-done.6, bf16[128,1024]{1,0:T(8,128)(2,1)S(1)} %collective-permute-done.refs_0_.refs_1_.refs_3_, ...), custom_call_target="tpu_custom_call" | custom-call | flops 3221225472 | bytes 10000000 | tf_op jit(solution)/shard_map/tower/pallas_call | solution.py:320
  73.3 1.5 %collective-permute-start.25 = (bf16[128,1024]{1,0:T(8,128)(2,1)S(1)}, bf16[128,1024]{1,0:T(8,128)(2,1)S(1)}, u32[]{:S(2)}, u32[]{:S(2)}) collective-permute-start(bf16[128,1024]{1,0:T(8,128)(2,1)S(1)} %place.12), channel_id=1, source_target_pairs={{0,16},{1,17},{2,18},{3,19},{4,20},{5,21},{6,22},{7,23},{8,24},{9,... | collective-permute-start | bytes 786440 | tf_op jit(solution)/shard_map/ppermute | solution.py:377
  76.2 4.9 %tower.5.refs_2_ = f32[32,64]{1,0:T(8,128)S(1)} custom-call(bf16[1024,1024]{1,0:T(8,128)(2,1)S(1)} %cell.1.joined_ref.refs_0_.refs_2_, bf16[1024,1024]{1,0:T(8,128)(2,1)S(1)} %collective-permute-done.14.refs_1_, f32[32,64]{1,0:T(8,128)S(1)} %tower.4.refs_2_.refs_1_, bf16[128,1024]{1,0:T(8,128)(2,1)S(1)} %collective-permute-done.2.refs_2_.refs_3_, ...), custom_call_target="tpu_custom_call" | custom-call | flops 3221225472 | bytes 10000000 | tf_op jit(solution)/shard_map/tower/pallas_call | solution.py:320
  82.5 1.5 %collective-permute-start.27 = (bf16[64,1024]{1,0:T(8,128)(2,1)S(1)}, bf16[64,1024]{1,0:T(8,128)(2,1)S(1)}, u32[]{:S(2)}, u32[]{:S(2)}) collective-permute-start(bf16[64,1024]{1,0:T(8,128)(2,1)S(1)} %get-tuple-element.28), channel_id=1, source_target_pairs={{0,16},{1,17},{2,18},{3,19},{4,20},{5,21},{6,22},{7,23},{8,24},{9,... | collective-permute-start | bytes 393224 | tf_op jit(solution)/shard_map/ppermute | solution.py:377
  84.0 5.1 %tower.6.refs_2_ = f32[32,64]{1,0:T(8,128)S(1)} custom-call(bf16[1024,1024]{1,0:T(8,128)(2,1)S(1)} %cell.1.joined_ref.refs_0_.refs_2_, bf16[1024,1024]{1,0:T(8,128)(2,1)S(1)} %collective-permute-done.14.refs_1_, f32[32,64]{1,0:T(8,128)S(1)} %tower.5.refs_2_, bf16[128,1024]{1,0:T(8,128)(2,1)S(1)} %collective-permute-done.11.refs_4_.refs_3_, ...), custom_call_target="tpu_custom_call" | custom-call | flops 3221225472 | bytes 10000000 | tf_op jit(solution)/shard_map/tower/pallas_call | solution.py:320
  89.2 5.5 %tower.7 = f32[32,64]{1,0:T(8,128)} custom-call(bf16[1024,1024]{1,0:T(8,128)(2,1)S(1)} %cell.1.joined_ref.refs_0_.refs_2_, bf16[1024,1024]{1,0:T(8,128)(2,1)S(1)} %collective-permute-done.14.refs_1_, f32[32,64]{1,0:T(8,128)S(1)} %tower.6.refs_2_, bf16[128,1024]{1,0:T(8,128)(2,1)S(1)} %collective-permute-done.23.refs_0_.refs_3_, ...), custom_call_target="tpu_custom_call" | custom-call | flops 3221225472 | bytes 10000000 | tf_op jit(solution)/shard_map/tower/pallas_call | solution.py:320
  94.7 4.6 %all-to-all-start.1 = ((f32[32,1,64]{2,1,0:T(1,128)}), f32[32,1,64]{2,1,0:T(1,128)S(1)}, u32[]{:S(2)}, u32[]{:S(2)}) async-start(f32[32,1,64]{2,1,0:T(1,128)} %bitcast.10), calls=%async_computation.1 | async-start | bytes 32768 | tf_op jit(solution)/shard_map/all_to_all | solution.py:373
  99.3 6.9 %update.1 = f32[2048,512]{1,0:T(8,128)} custom-call(s32[32,64]{1,0:T(8,128)} %bitcast.21, bf16[1024,1024]{1,0:T(8,128)(2,1)} %copy-done, f32[2048,512]{1,0:T(8,128)} %states_ref.1), custom_call_target="tpu_custom_call" | custom-call | flops 4000000000 | bytes 10000000 | tf_op jit(solution)/shard_map/update/pallas_call | solution.py:238
  (63 shorter events, 9.8 us)
Async XLA Ops:
  3.3 4.6 %collective-permute-start.3 = (bf16[2,16,1024]{2,1,0:T(8,128)(2,1)}, bf16[2,16,1024]{2,1,0:T(8,128)(2,1)S(1)}, u32[]{:S(2)}, u32[]{:S(2)}) collective-permute-start(bf16[2,16,1024]{2,1,0:T(8,128)(2,1)} %bitcast.26), channel_id=1, source_target_pairs={{0,1},{1,0},{2,3},{3,2},{4,5},{5,4},{6,7},{7,6},{8,9},{9,8},{10,11... | collective-permute-start | bytes 196616 | tf_op jit(solution)/shard_map/ppermute | solution.py:377
  3.9 14.0 %collective-permute-start = (bf16[128,1024]{1,0:T(8,128)(2,1)S(1)}, bf16[128,1024]{1,0:T(8,128)(2,1)S(1)}, u32[]{:S(2)}, u32[]{:S(2)}) collective-permute-start(bf16[128,1024]{1,0:T(8,128)(2,1)S(1)} %copy-done.6), channel_id=1, source_target_pairs={{0,8},{1,9},{2,10},{3,11},{4,12},{5,13},{6,14},{7,15},{8,0},{9,1},... | collective-permute-start | bytes 786440 | tf_op jit(solution)/shard_map/ppermute | solution.py:377
  6.4 12.9 %collective-permute-start.1 = (bf16[128,1024]{1,0:T(8,128)(2,1)S(1)}, bf16[128,1024]{1,0:T(8,128)(2,1)S(1)}, u32[]{:S(2)}, u32[]{:S(2)}) collective-permute-start(bf16[128,1024]{1,0:T(8,128)(2,1)S(1)} %copy-done.6), channel_id=1, source_target_pairs={{0,16},{1,17},{2,18},{3,19},{4,20},{5,21},{6,22},{7,23},{8,24},{9,... | collective-permute-start | bytes 786440 | tf_op jit(solution)/shard_map/ppermute | solution.py:377
  8.8 12.0 %collective-permute-start.4 = (bf16[64,1024]{1,0:T(8,128)(2,1)S(1)}, bf16[64,1024]{1,0:T(8,128)(2,1)S(1)}, u32[]{:S(2)}, u32[]{:S(2)}) collective-permute-start(bf16[64,1024]{1,0:T(8,128)(2,1)S(1)} %bitcast.15), channel_id=1, source_target_pairs={{0,2},{1,3},{2,4},{3,5},{4,6},{5,7},{6,0},{7,1},{8,10},{9,11},{10,... | collective-permute-start | bytes 393224 | tf_op jit(solution)/shard_map/ppermute | solution.py:377
  10.5 11.9 %all-to-all-start = ((s32[32,1,64]{2,1,0:T(1,128)}), s32[32,1,64]{2,1,0:T(1,128)S(1)}, u32[]{:S(2)}, u32[]{:S(2)}) async-start(s32[32,1,64]{2,1,0:T(1,128)} %bitcast.24), calls=%async_computation | async-start | bytes 32768 | tf_op jit(solution)/shard_map/all_to_all | solution.py:373
  13.7 19.4 %collective-permute-start.2 = (bf16[128,1024]{1,0:T(8,128)(2,1)S(1)}, bf16[128,1024]{1,0:T(8,128)(2,1)S(1)}, u32[]{:S(2)}, u32[]{:S(2)}) collective-permute-start(bf16[128,1024]{1,0:T(8,128)(2,1)S(1)} %copy-done.6), channel_id=1, source_target_pairs={{0,2},{1,3},{2,4},{3,5},{4,6},{5,7},{6,0},{7,1},{8,10},{9,11},{10,... | collective-permute-start | bytes 786440 | tf_op jit(solution)/shard_map/ppermute | solution.py:377
  15.5 14.5 %collective-permute-start.5 = (bf16[64,1024]{1,0:T(8,128)(2,1)S(1)}, bf16[64,1024]{1,0:T(8,128)(2,1)S(1)}, u32[]{:S(2)}, u32[]{:S(2)}) collective-permute-start(bf16[64,1024]{1,0:T(8,128)(2,1)S(1)} %bitcast.16), channel_id=1, source_target_pairs={{0,4},{1,5},{2,6},{3,7},{4,0},{5,1},{6,2},{7,3},{8,12},{9,13},{10,... | collective-permute-start | bytes 393224 | tf_op jit(solution)/shard_map/ppermute | solution.py:377
  17.9 12.0 %collective-permute-start.6 = (bf16[64,1024]{1,0:T(8,128)(2,1)S(1)}, bf16[64,1024]{1,0:T(8,128)(2,1)S(1)}, u32[]{:S(2)}, u32[]{:S(2)}) collective-permute-start(bf16[64,1024]{1,0:T(8,128)(2,1)S(1)} %bitcast.17), channel_id=1, source_target_pairs={{0,6},{1,7},{2,0},{3,1},{4,2},{5,3},{6,4},{7,5},{8,14},{9,15},{10,... | collective-permute-start | bytes 393224 | tf_op jit(solution)/shard_map/ppermute | solution.py:377
  19.4 17.0 %collective-permute-start.12 = (bf16[64,1024]{1,0:T(8,128)(2,1)S(1)}, bf16[64,1024]{1,0:T(8,128)(2,1)S(1)}, u32[]{:S(2)}, u32[]{:S(2)}) collective-permute-start(bf16[64,1024]{1,0:T(8,128)(2,1)S(1)} %get-tuple-element.19), channel_id=1, source_target_pairs={{0,8},{1,9},{2,10},{3,11},{4,12},{5,13},{6,14},{7,15},{8,0},{9,1},... | collective-permute-start | bytes 393224 | tf_op jit(solution)/shard_map/ppermute | solution.py:377
  20.9 16.1 %collective-permute-start.13 = (bf16[64,1024]{1,0:T(8,128)(2,1)S(1)}, bf16[64,1024]{1,0:T(8,128)(2,1)S(1)}, u32[]{:S(2)}, u32[]{:S(2)}) collective-permute-start(bf16[64,1024]{1,0:T(8,128)(2,1)S(1)} %get-tuple-element.20), channel_id=1, source_target_pairs={{0,16},{1,17},{2,18},{3,19},{4,20},{5,21},{6,22},{7,23},{8,24},{9,... | collective-permute-start | bytes 393224 | tf_op jit(solution)/shard_map/ppermute | solution.py:377
  30.0 20.7 %copy-start.4 = (bf16[512,1536]{1,0:T(8,128)(2,1)S(1)}, bf16[512,1536]{1,0:T(8,128)(2,1)}, u32[]{:S(2)}) copy-start(bf16[512,1536]{1,0:T(8,128)(2,1)} %gin_hbm.1) | copy-start | bytes 4718596
  30.0 20.7 %collective-permute-start.7 = (bf16[256,1024]{1,0:T(8,128)(2,1)S(1)}, bf16[256,1024]{1,0:T(8,128)(2,1)S(1)}, u32[]{:S(2)}, u32[]{:S(2)}) collective-permute-start(bf16[256,1024]{1,0:T(8,128)(2,1)S(1)} %place.7.refs_7_.refs_8_), channel_id=1, source_target_pairs={{0,8},{1,9},{2,10},{3,11},{4,12},{5,13},{6,14},{7,15},{8,0},{9,1},... | collective-permute-start | bytes 1572872 | tf_op jit(solution)/shard_map/ppermute | solution.py:377
  31.6 19.1 %collective-permute-start.8 = (bf16[256,1024]{1,0:T(8,128)(2,1)S(1)}, bf16[256,1024]{1,0:T(8,128)(2,1)S(1)}, u32[]{:S(2)}, u32[]{:S(2)}) collective-permute-start(bf16[256,1024]{1,0:T(8,128)(2,1)S(1)} %place.7.refs_7_.refs_8_), channel_id=1, source_target_pairs={{0,16},{1,17},{2,18},{3,19},{4,20},{5,21},{6,22},{7,23},{8,24},{9,... | collective-permute-start | bytes 1572872 | tf_op jit(solution)/shard_map/ppermute | solution.py:377
  33.1 9.6 %collective-permute-start.11 = (bf16[128,1024]{1,0:T(8,128)(2,1)S(1)}, bf16[128,1024]{1,0:T(8,128)(2,1)S(1)}, u32[]{:S(2)}, u32[]{:S(2)}) collective-permute-start(bf16[128,1024]{1,0:T(8,128)(2,1)S(1)} %collective-permute-done.2.refs_2_.refs_3_), channel_id=1, source_target_pairs={{0,2},{1,3},{2,4},{3,5},{4,6},{5,7},{6,0},{7,1},{8,10},{9,11},{10,... | collective-permute-start | bytes 786440 | tf_op jit(solution)/shard_map/ppermute | solution.py:377
  36.4 14.3 %collective-permute-start.10 = (bf16[128,1024]{1,0:T(8,128)(2,1)S(1)}, bf16[128,1024]{1,0:T(8,128)(2,1)S(1)}, u32[]{:S(2)}, u32[]{:S(2)}) collective-permute-start(bf16[128,1024]{1,0:T(8,128)(2,1)S(1)} %collective-permute-done.2.refs_2_.refs_3_), channel_id=1, source_target_pairs={{0,16},{1,17},{2,18},{3,19},{4,20},{5,21},{6,22},{7,23},{8,24},{9,... | collective-permute-start | bytes 786440 | tf_op jit(solution)/shard_map/ppermute | solution.py:377
  36.9 13.8 %collective-permute-start.9 = (bf16[128,1024]{1,0:T(8,128)(2,1)S(1)}, bf16[128,1024]{1,0:T(8,128)(2,1)S(1)}, u32[]{:S(2)}, u32[]{:S(2)}) collective-permute-start(bf16[128,1024]{1,0:T(8,128)(2,1)S(1)} %collective-permute-done.2.refs_2_.refs_3_), channel_id=1, source_target_pairs={{0,8},{1,9},{2,10},{3,11},{4,12},{5,13},{6,14},{7,15},{8,0},{9,1},... | collective-permute-start | bytes 786440 | tf_op jit(solution)/shard_map/ppermute | solution.py:377
  55.0 34.2 %copy-start = (bf16[1024,1024]{1,0:T(8,128)(2,1)}, bf16[1024,1024]{1,0:T(8,128)(2,1)S(1)}, u32[]{:S(2)}) copy-start(bf16[1024,1024]{1,0:T(8,128)(2,1)S(1)} %cell.1.joined_ref.refs_0_.refs_2_) | copy-start | bytes 6291460
  55.0 11.3 %collective-permute-start.14 = (bf16[1024,1024]{1,0:T(8,128)(2,1)S(1)}, bf16[1024,1024]{1,0:T(8,128)(2,1)S(1)}, u32[]{:S(2)}, u32[]{:S(2)}) collective-permute-start(bf16[1024,1024]{1,0:T(8,128)(2,1)S(1)} %cell.1.joined_ref.refs_0_.refs_2_), channel_id=1, source_target_pairs={{0,1},{1,0},{2,3},{3,2},{4,5},{5,4},{6,7},{7,6},{8,9},{9,8},{10,11... | collective-permute-start | bytes 6291464 | tf_op jit(solution)/shard_map/ppermute | solution.py:377
  55.1 9.2 %collective-permute-start.15 = (bf16[128,1024]{1,0:T(8,128)(2,1)S(1)}, bf16[128,1024]{1,0:T(8,128)(2,1)S(1)}, u32[]{:S(2)}, u32[]{:S(2)}) collective-permute-start(bf16[128,1024]{1,0:T(8,128)(2,1)S(1)} %get-tuple-element.21), channel_id=1, source_target_pairs={{0,8},{1,9},{2,10},{3,11},{4,12},{5,13},{6,14},{7,15},{8,0},{9,1},... | collective-permute-start | bytes 786440 | tf_op jit(solution)/shard_map/ppermute | solution.py:377
  55.7 10.1 %collective-permute-start.16 = (bf16[128,1024]{1,0:T(8,128)(2,1)S(1)}, bf16[128,1024]{1,0:T(8,128)(2,1)S(1)}, u32[]{:S(2)}, u32[]{:S(2)}) collective-permute-start(bf16[128,1024]{1,0:T(8,128)(2,1)S(1)} %get-tuple-element.22), channel_id=1, source_target_pairs={{0,16},{1,17},{2,18},{3,19},{4,20},{5,21},{6,22},{7,23},{8,24},{9,... | collective-permute-start | bytes 786440 | tf_op jit(solution)/shard_map/ppermute | solution.py:377
  57.2 14.8 %collective-permute-start.23 = (bf16[128,1024]{1,0:T(8,128)(2,1)S(1)}, bf16[128,1024]{1,0:T(8,128)(2,1)S(1)}, u32[]{:S(2)}, u32[]{:S(2)}) collective-permute-start(bf16[128,1024]{1,0:T(8,128)(2,1)S(1)} %collective-permute-done.11.refs_4_.refs_3_), channel_id=1, source_target_pairs={{0,2},{1,3},{2,4},{3,5},{4,6},{5,7},{6,0},{7,1},{8,10},{9,11},{10,... | collective-permute-start | bytes 786440 | tf_op jit(solution)/shard_map/ppermute | solution.py:377
  60.6 12.8 %collective-permute-start.19 = (bf16[128,1024]{1,0:T(8,128)(2,1)S(1)}, bf16[128,1024]{1,0:T(8,128)(2,1)S(1)}, u32[]{:S(2)}, u32[]{:S(2)}) collective-permute-start(bf16[128,1024]{1,0:T(8,128)(2,1)S(1)} %collective-permute-done.11.refs_4_.refs_3_), channel_id=1, source_target_pairs={{0,8},{1,9},{2,10},{3,11},{4,12},{5,13},{6,14},{7,15},{8,0},{9,1},... | collective-permute-start | bytes 786440 | tf_op jit(solution)/shard_map/ppermute | solution.py:377
  64.3 10.5 %collective-permute-start.20 = (bf16[128,1024]{1,0:T(8,128)(2,1)S(1)}, bf16[128,1024]{1,0:T(8,128)(2,1)S(1)}, u32[]{:S(2)}, u32[]{:S(2)}) collective-permute-start(bf16[128,1024]{1,0:T(8,128)(2,1)S(1)} %collective-permute-done.11.refs_4_.refs_3_), channel_id=1, source_target_pairs={{0,16},{1,17},{2,18},{3,19},{4,20},{5,21},{6,22},{7,23},{8,24},{9,... | collective-permute-start | bytes 786440 | tf_op jit(solution)/shard_map/ppermute | solution.py:377
  65.7 9.8 %collective-permute-start.17 = (bf16[64,1024]{1,0:T(8,128)(2,1)S(1)}, bf16[64,1024]{1,0:T(8,128)(2,1)S(1)}, u32[]{:S(2)}, u32[]{:S(2)}) collective-permute-start(bf16[64,1024]{1,0:T(8,128)(2,1)S(1)} %get-tuple-element.23), channel_id=1, source_target_pairs={{0,8},{1,9},{2,10},{3,11},{4,12},{5,13},{6,14},{7,15},{8,0},{9,1},... | collective-permute-start | bytes 393224 | tf_op jit(solution)/shard_map/ppermute | solution.py:377
  66.3 9.9 %collective-permute-start.18 = (bf16[64,1024]{1,0:T(8,128)(2,1)S(1)}, bf16[64,1024]{1,0:T(8,128)(2,1)S(1)}, u32[]{:S(2)}, u32[]{:S(2)}) collective-permute-start(bf16[64,1024]{1,0:T(8,128)(2,1)S(1)} %get-tuple-element.24), channel_id=1, source_target_pairs={{0,16},{1,17},{2,18},{3,19},{4,20},{5,21},{6,22},{7,23},{8,24},{9,... | collective-permute-start | bytes 393224 | tf_op jit(solution)/shard_map/ppermute | solution.py:377
  72.0 9.1 %collective-permute-start.24 = (bf16[128,1024]{1,0:T(8,128)(2,1)S(1)}, bf16[128,1024]{1,0:T(8,128)(2,1)S(1)}, u32[]{:S(2)}, u32[]{:S(2)}) collective-permute-start(bf16[128,1024]{1,0:T(8,128)(2,1)S(1)} %place.12), channel_id=1, source_target_pairs={{0,8},{1,9},{2,10},{3,11},{4,12},{5,13},{6,14},{7,15},{8,0},{9,1},... | collective-permute-start | bytes 786440 | tf_op jit(solution)/shard_map/ppermute | solution.py:377
  73.3 8.3 %collective-permute-start.25 = (bf16[128,1024]{1,0:T(8,128)(2,1)S(1)}, bf16[128,1024]{1,0:T(8,128)(2,1)S(1)}, u32[]{:S(2)}, u32[]{:S(2)}) collective-permute-start(bf16[128,1024]{1,0:T(8,128)(2,1)S(1)} %place.12), channel_id=1, source_target_pairs={{0,16},{1,17},{2,18},{3,19},{4,20},{5,21},{6,22},{7,23},{8,24},{9,... | collective-permute-start | bytes 786440 | tf_op jit(solution)/shard_map/ppermute | solution.py:377
  74.8 9.1 %collective-permute-start.21 = (bf16[64,1024]{1,0:T(8,128)(2,1)S(1)}, bf16[64,1024]{1,0:T(8,128)(2,1)S(1)}, u32[]{:S(2)}, u32[]{:S(2)}) collective-permute-start(bf16[64,1024]{1,0:T(8,128)(2,1)S(1)} %get-tuple-element.25), channel_id=1, source_target_pairs={{0,8},{1,9},{2,10},{3,11},{4,12},{5,13},{6,14},{7,15},{8,0},{9,1},... | collective-permute-start | bytes 393224 | tf_op jit(solution)/shard_map/ppermute | solution.py:377
  75.5 8.5 %collective-permute-start.22 = (bf16[64,1024]{1,0:T(8,128)(2,1)S(1)}, bf16[64,1024]{1,0:T(8,128)(2,1)S(1)}, u32[]{:S(2)}, u32[]{:S(2)}) collective-permute-start(bf16[64,1024]{1,0:T(8,128)(2,1)S(1)} %get-tuple-element.26), channel_id=1, source_target_pairs={{0,16},{1,17},{2,18},{3,19},{4,20},{5,21},{6,22},{7,23},{8,24},{9,... | collective-permute-start | bytes 393224 | tf_op jit(solution)/shard_map/ppermute | solution.py:377
  81.6 7.5 %collective-permute-start.26 = (bf16[64,1024]{1,0:T(8,128)(2,1)S(1)}, bf16[64,1024]{1,0:T(8,128)(2,1)S(1)}, u32[]{:S(2)}, u32[]{:S(2)}) collective-permute-start(bf16[64,1024]{1,0:T(8,128)(2,1)S(1)} %get-tuple-element.27), channel_id=1, source_target_pairs={{0,8},{1,9},{2,10},{3,11},{4,12},{5,13},{6,14},{7,15},{8,0},{9,1},... | collective-permute-start | bytes 393224 | tf_op jit(solution)/shard_map/ppermute | solution.py:377
  82.5 6.6 %collective-permute-start.27 = (bf16[64,1024]{1,0:T(8,128)(2,1)S(1)}, bf16[64,1024]{1,0:T(8,128)(2,1)S(1)}, u32[]{:S(2)}, u32[]{:S(2)}) collective-permute-start(bf16[64,1024]{1,0:T(8,128)(2,1)S(1)} %get-tuple-element.28), channel_id=1, source_target_pairs={{0,16},{1,17},{2,18},{3,19},{4,20},{5,21},{6,22},{7,23},{8,24},{9,... | collective-permute-start | bytes 393224 | tf_op jit(solution)/shard_map/ppermute | solution.py:377
  94.7 11.7 %all-to-all-start.1 = ((f32[32,1,64]{2,1,0:T(1,128)}), f32[32,1,64]{2,1,0:T(1,128)S(1)}, u32[]{:S(2)}, u32[]{:S(2)}) async-start(f32[32,1,64]{2,1,0:T(1,128)} %bitcast.10), calls=%async_computation.1 | async-start | bytes 32768 | tf_op jit(solution)/shard_map/all_to_all | solution.py:373
  (6 other events, 61.2 us)
